TPU v7x, 32 devices: a whole 2x2x4 slice. The times are simulated.
32 devices in a mesh: wide: 16 (over z, x, core), narrow: 2 (over y).
Axes of the slice: x: 2, y: 2, z: 4, core: 2. Of those that a mesh axis runs over, the one named last changes fastest.
Arguments:
- first_in: float32 [2, 4096, 1024], P(None, 'wide', 'narrow'), may hold values from -6 to 6
- second_in: float32 [2, 4096, 1024], P(None, 'wide', 'narrow'), may hold values from -6 to 6
- attn_norm_gain: float32 [2, 1024], replicated, may hold values from 0.5 to 1.5
- attn_norm_bias: float32 [2, 1024], replicated, may hold values from -1 to 1
- qk_weight: bfloat16 [2, 1024, 1024], P(None, 'wide', 'narrow'), may hold values from -0.1875 to 0.1875
- value_weight: bfloat16 [2, 1024, 1024], P(None, 'wide', 'narrow'), may hold values from -0.1875 to 0.1875
- out_weight: bfloat16 [2, 1024, 1024], P(None, 'wide', 'narrow'), may hold values from -0.75 to 0.75
- out_bias: float32 [2, 1024], P(None, 'narrow'), may hold values from -1 to 1
- ffn_norm_gain: float32 [2, 1024], replicated, may hold values from 0.5 to 1.5
- ffn_norm_bias: float32 [2, 1024], replicated, may hold values from -1 to 1
- up_weight: bfloat16 [2, 1024, 4096], P(None, None, 'narrow'), may hold values from -0.1875 to 0.1875
- up_bias: float32 [2, 4096], P(None, 'narrow'), may hold values from -2.5 to 2.5
- down_weight: bfloat16 [2, 1024, 4096], P(None, None, 'narrow'), may hold values from -0.125 to 0.125
- down_bias: float32 [2, 1024], P(None, 'narrow'), may hold values from -1 to 1
- bucket_perm: int32 [4, 2, 4096], P(None, None, 'wide'), may hold values from 0 to 4095, as said below
- first_cot: float32 [2, 4096, 1024], P(None, 'wide', 'narrow'), may hold values from -6 to 6
- second_cot: float32 [2, 4096, 1024], P(None, 'wide', 'narrow'), may hold values from -6 to 6
Outputs:
- first_out: float32 [2, 4096, 1024], P(None, 'wide', 'narrow')
- second_out: float32 [2, 4096, 1024], P(None, 'wide', 'narrow')
- first_grad: float32 [2, 4096, 1024], P(None, 'wide', 'narrow')
- second_grad: float32 [2, 4096, 1024], P(None, 'wide', 'narrow')
- grad_attn_norm_gain: float32 [2, 1024], replicated
- grad_attn_norm_bias: float32 [2, 1024], replicated
- grad_qk_weight: float32 [2, 1024, 1024], P(None, 'wide', 'narrow')
- grad_value_weight: float32 [2, 1024, 1024], P(None, 'wide', 'narrow')
- grad_out_weight: float32 [2, 1024, 1024], P(None, 'wide', 'narrow')
- grad_out_bias: float32 [2, 1024], P(None, 'narrow')
- grad_ffn_norm_gain: float32 [2, 1024], replicated
- grad_ffn_norm_bias: float32 [2, 1024], replicated
- grad_up_weight: float32 [2, 1024, 4096], P(None, 'wide', 'narrow')
- grad_up_bias: float32 [2, 4096], P(None, 'narrow')
- grad_down_weight: float32 [2, 1024, 4096], P(None, 'wide', 'narrow')
- grad_down_bias: float32 [2, 1024], P(None, 'narrow')
Inputs may be any that keep to these rules, and one draw needn't show every extreme that they name: `bucket_perm`: for each round and sequence the row is a permutation of the positions 0 to 4095; the sorted positions k*256 to (k+1)*256 - 1 take exactly 16 tokens from each run of 256 positions j*256 to (j+1)*256 - 1.
All inputs are finite; a program needn't handle non-finite values.
Results may differ from a plain program's by a relative error of at most 0.02.
Values may be sent and summed in bfloat16 or wider, within the bound.
No kernel may reach another device: no remote copies, remote signals or barrier semaphores. Data moves between devices by JAX's collectives and lax.ppermute only.
A program may use at most 256 MiB of HBM per device.

v0:
```python
import jax
import jax.numpy as jnp
from jax import lax
from jax.sharding import PartitionSpec as P

HD = 128
GROUP = 64
ROUNDS = 4
LAYERS = 2


def from_behind(value, axis, steps):
    count = lax.axis_size(axis)
    pairs = [(source, (source + steps) % count) for source in range(count)]
    return lax.ppermute(value, axis, pairs)


def layer_norm(stream, gain, shift):
    centre = stream - jnp.mean(stream, axis=-1, keepdims=True)
    spread = jnp.mean(centre * centre, axis=-1, keepdims=True)
    return centre * lax.rsqrt(spread + 1e-05) * gain + shift


def unit_keys(raw_rows):
    return raw_rows * lax.rsqrt(jnp.mean(raw_rows * raw_rows, axis=-1, keepdims=True) + 1e-06)


def smooth_act(pre_act):
    return jax.nn.gelu(pre_act, approximate=True)


def self_mask():
    return jnp.arange(GROUP)[:, None] + GROUP == jnp.arange(2 * GROUP)[None, :]


def widen(stream):
    return lax.all_gather(stream, "narrow", axis=1, tiled=True)


def narrow_sum(partial_sum):
    return lax.psum_scatter(partial_sum, "narrow", scatter_dimension=1, tiled=True)


def widen_grad(gradient):
    return lax.all_gather(gradient, "narrow", axis=1, tiled=True)


def full_grad(partial_sum):
    return lax.psum(partial_sum, "narrow")


def sum_weights(qk_part, value_part, out_part, up_part, down_part):
    return (
        lax.psum_scatter(qk_part, "wide", scatter_dimension=1, tiled=True),
        lax.psum_scatter(value_part, "wide", scatter_dimension=1, tiled=True),
        lax.psum_scatter(out_part, "wide", scatter_dimension=1, tiled=True),
        lax.psum_scatter(up_part, "wide", scatter_dimension=1, tiled=True),
        lax.psum_scatter(down_part, "wide", scatter_dimension=1, tiled=True),
    )


def pick_rows(array, index):
    round_idx = jnp.arange(array.shape[0])[:, None, None]
    seq_idx = jnp.arange(array.shape[1])[None, :, None]
    return array[round_idx, seq_idx, index]


def pick_shared(tokens, index):
    seq_idx = jnp.arange(tokens.shape[0])[None, :, None]
    return tokens[seq_idx, index]


def to_send(picked):
    wide_size = lax.axis_size("wide")
    return picked.reshape(
        picked.shape[:2] + (wide_size, picked.shape[2] // wide_size) + picked.shape[3:]
    )


def from_recv(received):
    return received.reshape(
        received.shape[:2] + (received.shape[2] * received.shape[3],) + received.shape[4:]
    )


def sorted_from_tokens(picked, slot_part):
    received = lax.all_to_all(to_send(picked), "wide", split_axis=2, concat_axis=2, tiled=True)
    return (pick_rows(from_recv(received), slot_part),)


def tokens_from_sorted(bucket_rows, inv_part, row_part):
    received = lax.all_to_all(
        to_send(pick_rows(bucket_rows, inv_part)), "wide", split_axis=2, concat_axis=2, tiled=True
    )
    return (pick_rows(from_recv(received), row_part),)


def stats_to_tokens(bucket_rows, inv_part, row_part):
    received = lax.all_to_all(
        to_send(pick_rows(bucket_rows, inv_part)), "wide", split_axis=2, concat_axis=2, tiled=True
    )
    return (pick_rows(from_recv(received), row_part),)


def stats_to_sorted(picked, slot_part):
    received = lax.all_to_all(to_send(picked), "wide", split_axis=2, concat_axis=2, tiled=True)
    return (pick_rows(from_recv(received), slot_part),)


def round_wise(action, members):
    pieces = [
        action(*(member[round_index : round_index + 1] for member in members))
        for round_index in range(ROUNDS)
    ]
    result = tuple(
        (
            jnp.concatenate([piece[slot] for piece in pieces], axis=0)
            for slot in range(len(pieces[0]))
        )
    )
    return result


def build_tables(bucket_perm):
    round_count, seq_count, rows_seq = bucket_perm.shape
    wide_size = lax.axis_size("wide")
    pair_rows = rows_seq // wide_size
    sources = bucket_perm // rows_seq
    src_rows = bucket_perm % rows_seq
    onehot = (sources[..., None] == jnp.arange(wide_size, dtype=jnp.int32)).astype(jnp.int32)
    rank_of = jnp.sum(onehot * (jnp.cumsum(onehot, axis=2) - 1), axis=-1)
    slot_from = sources * pair_rows + rank_of
    round_idx = jnp.arange(round_count)[:, None, None]
    seq_idx = jnp.arange(seq_count)[None, :, None]
    positions = jnp.broadcast_to(jnp.arange(rows_seq, dtype=jnp.int32), bucket_perm.shape)
    inv_slot = jnp.zeros_like(bucket_perm).at[round_idx, seq_idx, slot_from].set(positions)
    wants = jnp.zeros_like(bucket_perm).at[round_idx, seq_idx, slot_from].set(src_rows)
    wanted = lax.all_to_all(
        wants.reshape(round_count, seq_count, wide_size, pair_rows),
        "wide",
        split_axis=2,
        concat_axis=2,
        tiled=True,
    )
    wanted = wanted.reshape(bucket_perm.shape)
    row_from = jnp.zeros_like(bucket_perm).at[round_idx, seq_idx, wanted].set(positions)
    return (slot_from, inv_slot, wanted, row_from)


def grouped(rows):
    return rows.reshape(rows.shape[:2] + (rows.shape[2] // GROUP, GROUP) + rows.shape[3:])


def key_window(current, previous):
    blocks = grouped(current)
    earlier = jnp.concatenate([previous[:, :, None], blocks[:, :, :-1]], axis=2)
    return jnp.concatenate([earlier, blocks], axis=3)


def scores_of(query_blocks, key_block):
    raw_scores = jnp.einsum(
        "rscqhd,rsckhd->rschqk", query_blocks, key_block, preferred_element_type=jnp.float32
    )
    return jnp.where(self_mask(), -1000000000.0, raw_scores * HD ** (-0.5))


def by_groups(stat_rows):
    return jnp.transpose(grouped(stat_rows), (0, 1, 2, 4, 3))


def attention_forward(bucket_queries, bucket_values):
    key_rows = unit_keys(bucket_queries.astype(jnp.float32)).astype(jnp.bfloat16)
    last_keys, last_values = from_behind(
        (key_rows[:, :, -GROUP:], bucket_values[:, :, -GROUP:]), "wide", 1
    )
    key_block = key_window(key_rows, last_keys)
    value_block = key_window(bucket_values, last_values)
    scores = scores_of(grouped(bucket_queries), key_block)
    row_top = jnp.max(scores, axis=-1, keepdims=True)
    log_total = row_top[..., 0] + jnp.log(jnp.sum(jnp.exp(scores - row_top), axis=-1))
    probs = jnp.exp(scores - log_total[..., None]).astype(jnp.bfloat16)
    round_out = jnp.einsum(
        "rschqk,rsckhd->rscqhd", probs, value_block, preferred_element_type=jnp.float32
    )
    full_shape = bucket_queries.shape
    out_rows = round_out.astype(jnp.bfloat16).reshape(
        full_shape[:3] + (1, full_shape[3] * full_shape[4])
    )
    log_rows = jnp.transpose(log_total, (0, 1, 2, 4, 3)).reshape(full_shape[:4])
    return (out_rows, log_rows, key_rows, last_keys, last_values)


def attention_backward(
    bucket_queries, bucket_values, key_rows, last_keys, last_values, log_rows, out_grad, log_grad
):
    full_shape = bucket_queries.shape
    score_scale = HD ** (-0.5)
    key_block = key_window(key_rows, last_keys)
    value_block = key_window(bucket_values, last_values)
    query_blocks = grouped(bucket_queries)
    scores = scores_of(query_blocks, key_block)
    probs = jnp.exp(scores - by_groups(log_rows)[..., None])
    grad_blocks = grouped(out_grad.reshape(full_shape))
    prob_grad = jnp.einsum(
        "rscqhd,rsckhd->rschqk", grad_blocks, value_block, preferred_element_type=jnp.float32
    )
    centre = jnp.sum(probs * prob_grad, axis=-1) - by_groups(log_grad)
    score_grad = (probs * (prob_grad - centre[..., None])).astype(jnp.bfloat16)
    query_use = (
        jnp.einsum(
            "rschqk,rsckhd->rscqhd", score_grad, key_block, preferred_element_type=jnp.float32
        )
        * score_scale
    )
    key_grad = (
        jnp.einsum(
            "rschqk,rscqhd->rsckhd", score_grad, query_blocks, preferred_element_type=jnp.float32
        )
        * score_scale
    )
    value_grad = jnp.einsum(
        "rschqk,rscqhd->rsckhd",
        probs.astype(jnp.bfloat16),
        grad_blocks,
        preferred_element_type=jnp.float32,
    )
    back_keys, back_values = from_behind(
        (key_grad[:, :, 0, :GROUP], value_grad[:, :, 0, :GROUP]), "wide", -1
    )
    own_keys = key_grad[:, :, :, GROUP:] + jnp.concatenate(
        [key_grad[:, :, 1:, :GROUP], back_keys[:, :, None]], axis=2
    )
    own_values = value_grad[:, :, :, GROUP:] + jnp.concatenate(
        [value_grad[:, :, 1:, :GROUP], back_values[:, :, None]], axis=2
    )
    key_pull = jax.vjp(unit_keys, bucket_queries.astype(jnp.float32))[1]
    query_total = query_use.reshape(full_shape) + key_pull(own_keys.reshape(full_shape))[0]
    both = jnp.stack([query_total, own_values.reshape(full_shape)], axis=3).astype(jnp.bfloat16)
    return both.reshape(full_shape[:3] + (2, full_shape[3] * full_shape[4]))


def combine(out_tokens, log_tokens, local_heads):
    round_values = out_tokens.reshape(out_tokens.shape[:3] + (local_heads, HD)).astype(jnp.float32)
    round_top = jnp.max(log_tokens, axis=0, keepdims=True)
    round_weights = jnp.exp(log_tokens - round_top)
    round_weights = round_weights / jnp.sum(round_weights, axis=0, keepdims=True)
    mixed = jnp.sum(round_weights[..., None] * round_values, axis=0)
    return (mixed.reshape(-1, local_heads * HD).astype(jnp.bfloat16), round_weights)


def combine_back(out_tokens, round_weights, attn_grad, local_heads):
    round_values = out_tokens.reshape(out_tokens.shape[:3] + (local_heads, HD)).astype(jnp.float32)
    grad_heads = attn_grad.reshape(out_tokens.shape[1:3] + (local_heads, HD))
    out_grad = (
        (round_weights[..., None] * grad_heads[None]).astype(jnp.bfloat16).reshape(out_tokens.shape)
    )
    weight_dot = jnp.sum(round_values * grad_heads[None], axis=-1)
    log_grad = round_weights * (
        weight_dot - jnp.sum(round_weights * weight_dot, axis=0, keepdims=True)
    )
    return (out_grad, log_grad)


def contract_rows(left, right):
    return lax.dot_general(
        left, right, (((0,), (0,)), ((), ())), preferred_element_type=jnp.float32
    )


def contract_cols(left, right):
    return lax.dot_general(
        left, right, (((1,), (1,)), ((), ())), preferred_element_type=jnp.float32
    )


def shards(
    first_in,
    second_in,
    attn_norm_gain,
    attn_norm_bias,
    qk_weight,
    value_weight,
    out_weight,
    out_bias,
    ffn_norm_gain,
    ffn_norm_bias,
    up_weight,
    up_bias,
    down_weight,
    down_bias,
    bucket_perm,
    first_cot,
    second_cot,
):
    seq_count, rows_seq, half_width = first_in.shape
    tok_rows = seq_count * rows_seq
    narrow_index = lax.axis_index("narrow")
    slot_from, inv_slot, wanted, row_from = build_tables(bucket_perm)
    first_stream = first_in.reshape(tok_rows, half_width)
    second_stream = second_in.reshape(tok_rows, half_width)
    kept_state = []
    for layer_index in range(LAYERS):
        full_second = widen(second_stream)
        normed = layer_norm(
            full_second, attn_norm_gain[layer_index], attn_norm_bias[layer_index]
        ).astype(jnp.bfloat16)
        qk_full, value_full, out_full = (
            lax.all_gather(qk_weight[layer_index], "wide", axis=0, tiled=True),
            lax.all_gather(value_weight[layer_index], "wide", axis=0, tiled=True),
            lax.all_gather(out_weight[layer_index], "wide", axis=0, tiled=True),
        )
        queries = jnp.dot(normed, qk_full, preferred_element_type=jnp.float32).astype(jnp.bfloat16)
        values_tok = jnp.dot(normed, value_full, preferred_element_type=jnp.float32).astype(
            jnp.bfloat16
        )
        head_width = queries.shape[1]
        local_heads = head_width // HD
        stacked_rows = jnp.stack([queries, values_tok], axis=1).reshape(
            seq_count, rows_seq, 2, head_width
        )
        bucket_both = round_wise(
            lambda wanted_part, slot_part: sorted_from_tokens(
                pick_shared(stacked_rows, wanted_part), slot_part
            ),
            (wanted, slot_from),
        )[0]
        split_shape = (ROUNDS, seq_count, rows_seq, local_heads, HD)
        bucket_queries = bucket_both[:, :, :, 0].reshape(split_shape)
        bucket_values = bucket_both[:, :, :, 1].reshape(split_shape)
        out_rows, log_rows, key_rows, last_keys, last_values = attention_forward(
            bucket_queries, bucket_values
        )
        out_tokens = round_wise(tokens_from_sorted, (out_rows, inv_slot, row_from))[0]
        log_tokens = round_wise(stats_to_tokens, (log_rows, inv_slot, row_from))[0]
        attn, round_weights = combine(out_tokens, log_tokens, local_heads)
        first_stream = (
            first_stream + narrow_sum(contract_cols(attn, out_full)) + out_bias[layer_index]
        )
        full_first = widen(first_stream)
        ffn_in = layer_norm(
            full_first, ffn_norm_gain[layer_index], ffn_norm_bias[layer_index]
        ).astype(jnp.bfloat16)
        pre_act = (
            jnp.dot(ffn_in, up_weight[layer_index], preferred_element_type=jnp.float32)
            + up_bias[layer_index]
        )
        hidden = smooth_act(pre_act).astype(jnp.bfloat16)
        second_stream = (
            second_stream
            + narrow_sum(contract_cols(hidden, down_weight[layer_index]))
            + down_bias[layer_index]
        )
        kept_state.append(
            (
                full_second,
                normed,
                qk_full,
                value_full,
                out_full,
                bucket_queries,
                bucket_values,
                key_rows,
                last_keys,
                last_values,
                log_rows,
                out_tokens,
                round_weights,
                attn,
                full_first,
                ffn_in,
                pre_act,
                hidden,
            )
        )
    grad_first = first_cot.reshape(tok_rows, half_width)
    grad_second = second_cot.reshape(tok_rows, half_width)
    weight_parts = [None] * LAYERS
    small_parts = [None] * LAYERS
    for layer_index in reversed(range(LAYERS)):
        (
            full_second,
            normed,
            qk_full,
            value_full,
            out_full,
            bucket_queries,
            bucket_values,
            key_rows,
            last_keys,
            last_values,
            log_rows,
            out_tokens,
            round_weights,
            attn,
            full_first,
            ffn_in,
            pre_act,
            hidden,
        ) = kept_state[layer_index]
        head_width = attn.shape[1]
        local_heads = head_width // HD
        down_grad = widen_grad(grad_second.astype(jnp.bfloat16))
        down_bias_grad = jnp.sum(grad_second, axis=0)
        hidden_grad = jnp.dot(
            down_grad, down_weight[layer_index], preferred_element_type=jnp.float32
        )
        down_weight_grad = contract_rows(down_grad, hidden)
        pre_grad = jax.vjp(smooth_act, pre_act)[1](hidden_grad)[0]
        up_bias_grad = jnp.sum(pre_grad, axis=0)
        pre_low = pre_grad.astype(jnp.bfloat16)
        up_weight_grad = contract_rows(ffn_in, pre_low)
        ffn_in_grad = full_grad(contract_cols(pre_low, up_weight[layer_index]))
        norm_pull = jax.vjp(
            layer_norm, full_first, ffn_norm_gain[layer_index], ffn_norm_bias[layer_index]
        )[1]
        stream_part, ffn_gain_grad, ffn_bias_grad = norm_pull(ffn_in_grad)
        grad_first = grad_first + lax.dynamic_slice_in_dim(
            stream_part, narrow_index * half_width, half_width, 1
        )
        branch_grad = widen_grad(grad_first.astype(jnp.bfloat16))
        out_bias_grad = jnp.sum(grad_first, axis=0)
        attn_grad = jnp.dot(branch_grad, out_full, preferred_element_type=jnp.float32)
        out_weight_grad = contract_rows(branch_grad, attn)
        out_grad, log_grad = combine_back(out_tokens, round_weights, attn_grad, local_heads)
        bucket_out_grad = round_wise(
            lambda grad_part, wanted_part, slot_part: sorted_from_tokens(
                pick_rows(grad_part, wanted_part), slot_part
            ),
            (out_grad, wanted, slot_from),
        )[0]
        bucket_log_grad = round_wise(
            lambda grad_part, wanted_part, slot_part: stats_to_sorted(
                pick_rows(grad_part, wanted_part), slot_part
            ),
            (log_grad, wanted, slot_from),
        )[0]
        bucket_grads = attention_backward(
            bucket_queries,
            bucket_values,
            key_rows,
            last_keys,
            last_values,
            log_rows,
            bucket_out_grad,
            bucket_log_grad,
        )
        token_grads = round_wise(tokens_from_sorted, (bucket_grads, inv_slot, row_from))[0]
        summed = jnp.sum(token_grads.astype(jnp.float32), axis=0).astype(jnp.bfloat16)
        query_grad = summed[:, :, 0].reshape(tok_rows, head_width)
        value_grad = summed[:, :, 1].reshape(tok_rows, head_width)
        qk_weight_grad = contract_rows(normed, query_grad)
        value_weight_grad = contract_rows(normed, value_grad)
        normed_grad = full_grad(
            contract_cols(query_grad, qk_full) + contract_cols(value_grad, value_full)
        )
        norm_pull = jax.vjp(
            layer_norm, full_second, attn_norm_gain[layer_index], attn_norm_bias[layer_index]
        )[1]
        stream_part, attn_gain_grad, attn_bias_grad = norm_pull(normed_grad)
        grad_second = grad_second + lax.dynamic_slice_in_dim(
            stream_part, narrow_index * half_width, half_width, 1
        )
        local_weights = (
            qk_weight_grad,
            value_weight_grad,
            out_weight_grad,
            up_weight_grad,
            down_weight_grad,
        )
        weight_parts[layer_index] = sum_weights(*(member[None] for member in local_weights))
        small_parts[layer_index] = (
            attn_gain_grad,
            attn_bias_grad,
            out_bias_grad,
            ffn_gain_grad,
            ffn_bias_grad,
            up_bias_grad,
            down_bias_grad,
        )
    weight_sums = tuple(
        (
            jnp.concatenate(
                [weight_parts[layer_index][slot] for layer_index in range(LAYERS)], axis=0
            )
            for slot in range(5)
        )
    )
    stacked_small = tuple(
        (
            jnp.stack([small_parts[layer_index][slot] for layer_index in range(LAYERS)], axis=0)
            for slot in range(7)
        )
    )
    small_sums = lax.psum(
        (
            stacked_small[0],
            stacked_small[1],
            stacked_small[2],
            stacked_small[3],
            stacked_small[4],
            stacked_small[5],
            stacked_small[6],
        ),
        "wide",
    )
    out_shape = (seq_count, rows_seq, half_width)
    return (
        first_stream.reshape(out_shape),
        second_stream.reshape(out_shape),
        grad_first.reshape(out_shape),
        grad_second.reshape(out_shape),
        small_sums[0],
        small_sums[1],
        weight_sums[0],
        weight_sums[1],
        weight_sums[2],
        small_sums[2],
        small_sums[3],
        small_sums[4],
        weight_sums[3],
        small_sums[5],
        weight_sums[4],
        small_sums[6],
    )


def solution(mesh):
    placed = (
        P(None, "wide", "narrow"),
        P(None, "wide", "narrow"),
        P(),
        P(),
        P(None, "wide", "narrow"),
        P(None, "wide", "narrow"),
        P(None, "wide", "narrow"),
        P(None, "narrow"),
        P(),
        P(),
        P(None, None, "narrow"),
        P(None, "narrow"),
        P(None, None, "narrow"),
        P(None, "narrow"),
        P(None, None, "wide"),
        P(None, "wide", "narrow"),
        P(None, "wide", "narrow"),
    )
    return jax.shard_map(
        shards,
        mesh=mesh,
        in_specs=placed,
        out_specs=(
            P(None, "wide", "narrow"),
            P(None, "wide", "narrow"),
            P(None, "wide", "narrow"),
            P(None, "wide", "narrow"),
            P(),
            P(),
            P(None, "wide", "narrow"),
            P(None, "wide", "narrow"),
            P(None, "wide", "narrow"),
            P(None, "narrow"),
            P(),
            P(),
            P(None, "wide", "narrow"),
            P(None, "narrow"),
            P(None, "wide", "narrow"),
            P(None, "narrow"),
        ),
        check_vma=False,
    )
```

profile of v0, /device:TPU:0, one launch (start us, length us, event | category | flops | bytes accessed | tf_op | source)
XLA Modules:
  0.0 3062.6 jit_solution(11015575017817929747)
XLA Ops:
  49.7 36.4 %all-gather.39.cloned.1.call-done = bf16[1,1024,512]{2,1,0:T(8,128)(2,1)} async-done(((bf16[1,64,512]{2,1,0:T(8,128)(2,1)}), bf16[1,1024,512]{2,1,0:T(8,128)(2,1)}) %all-gather.39.cloned.1.call-update) | async-done | bytes 1048592 | tf_op jit(solution)/shard_map/all_gather | solution.py:309
  89.9 35.9 %all-gather.37.cloned.1.call-done = bf16[1,1024,512]{2,1,0:T(8,128)(2,1)} async-done(((bf16[1,64,512]{2,1,0:T(8,128)(2,1)}), bf16[1,1024,512]{2,1,0:T(8,128)(2,1)}) %all-gather.37.cloned.1.call-update) | async-done | bytes 1048592 | tf_op jit(solution)/shard_map/all_gather | solution.py:308
  146.8 16.9 all-to-all-done.4
  475.9 32.5 %reduce-scatter.15.cloned.1.call-done = f32[512,512]{1,0:T(8,128)} async-done(((f32[512,1024]{1,0:T(8,128)}), f32[512,512]{1,0:T(8,128)}) %reduce-scatter.15.cloned.1.call-update) | async-done | bytes 1048592 | tf_op jit(solution)/shard_map/reduce_scatter | solution.py:41
  512.1 32.0 %all-gather.23.cloned.1.call-done = f32[512,1024]{1,0:T(8,128)} async-done(((f32[512,512]{1,0:T(8,128)}), f32[512,1024]{1,0:T(8,128)}) %all-gather.23.cloned.1.call-update) | async-done | bytes 2097168 | tf_op jit(solution)/shard_map/all_gather | solution.py:37
  561.9 31.3 %reduce-scatter.17.cloned.1.call-done = f32[512,512]{1,0:T(8,128)} async-done(((f32[512,1024]{1,0:T(8,128)}), f32[512,512]{1,0:T(8,128)}) %reduce-scatter.17.cloned.1.call-update) | async-done | bytes 1048592 | tf_op jit(solution)/shard_map/reduce_scatter | solution.py:41
  596.9 32.0 %all-gather.25.cloned.1.call-done = f32[512,1024]{1,0:T(8,128)} async-done(((f32[512,512]{1,0:T(8,128)}), f32[512,1024]{1,0:T(8,128)}) %all-gather.25.cloned.1.call-update) | async-done | bytes 2097168 | tf_op jit(solution)/shard_map/all_gather | solution.py:37
  633.2 36.4 %all-gather.45.cloned.1.call-done = bf16[1,1024,512]{2,1,0:T(8,128)(2,1)} async-done(((bf16[1,64,512]{2,1,0:T(8,128)(2,1)}), bf16[1,1024,512]{2,1,0:T(8,128)(2,1)}) %all-gather.45.cloned.1.call-update) | async-done | bytes 1048592 | tf_op jit(solution)/shard_map/all_gather | solution.py:309
  672.4 36.7 %all-gather.43.cloned.1.call-done = bf16[1,1024,512]{2,1,0:T(8,128)(2,1)} async-done(((bf16[1,64,512]{2,1,0:T(8,128)(2,1)}), bf16[1,1024,512]{2,1,0:T(8,128)(2,1)}) %all-gather.43.cloned.1.call-update) | async-done | bytes 1048592 | tf_op jit(solution)/shard_map/all_gather | solution.py:308
  730.0 16.9 all-to-all-done.16
  763.5 13.2 all-to-all-done.15
  793.4 13.2 all-to-all-done.14
  1074.2 33.1 %reduce-scatter.19.cloned.1.call-done = f32[512,512]{1,0:T(8,128)} async-done(((f32[512,1024]{1,0:T(8,128)}), f32[512,512]{1,0:T(8,128)}) %reduce-scatter.19.cloned.1.call-update) | async-done | bytes 1048592 | tf_op jit(solution)/shard_map/reduce_scatter | solution.py:41
  1112.6 30.5 all-gather.27.cloned.1.call-done
  1183.1 62.9 %all-reduce.6.cloned.1.call-done = f32[512,1024]{1,0:T(8,128)} async-done(((f32[512,1024]{1,0:T(8,128)}), f32[512,1024]{1,0:T(8,128)}) %all-reduce.6.cloned.1.call-update) | async-done | bytes 2097168 | tf_op jit(solution)/shard_map/psum | solution.py:49
  1280.8 13.5 multiply_reduce_fusion.2
  1536.1 15.5 all-to-all-done.34
  1568.7 12.6 all-to-all-done.33
  1657.6 64.3 %all-reduce.8.cloned.1.call-done = f32[512,1024]{1,0:T(8,128)} async-done(((f32[512,1024]{1,0:T(8,128)}), f32[512,1024]{1,0:T(8,128)}) %all-reduce.8.cloned.1.call-update) | async-done | bytes 2097168 | tf_op jit(solution)/shard_map/psum | solution.py:49
  1728.9 21.4 all-gather.33.cloned.1.call-done
  1767.1 62.9 %all-reduce.10.cloned.1.call-done = f32[512,1024]{1,0:T(8,128)} async-done(((f32[512,1024]{1,0:T(8,128)}), f32[512,1024]{1,0:T(8,128)}) %all-reduce.10.cloned.1.call-update) | async-done | bytes 2097168 | tf_op jit(solution)/shard_map/psum | solution.py:49
  1864.1 13.6 multiply_reduce_fusion
  2195.2 16.8 all-to-all-done.48
  2320.9 40.7 %all-reduce.12.cloned.1.call-done = f32[512,1024]{1,0:T(8,128)} async-done(((f32[512,1024]{1,0:T(8,128)}), f32[512,1024]{1,0:T(8,128)}) %all-reduce.12.cloned.1.call-update) | async-done | bytes 2097168 | tf_op jit(solution)/shard_map/psum | solution.py:49
  2364.0 62.6 %all-reduce = (f32[2,1024]{1,0:T(2,128)}, f32[2,1024]{1,0:T(2,128)}, f32[2,512]{1,0:T(2,128)}, f32[2,1024]{1,0:T(2,128)}, f32[2,1024]{1,0:T(2,128)}, /*index=5*/f32[2,2048]{1,0:T(2,128)}, f32[2,512]{1,0:T(2,128)}) all-reduce(f32[2,1024]{1,0:T(2,128)S(1)} %pad_maximum_fusion.26, ...), channel_id=1, replica_groups=mesh['wide'=16,'narrow'=2] {'wide'}, use_global_device_ids=true, to_apply=%region_50.51 | all-reduce | flops 14336 | bytes 114688 | tf_op jit(solution)/shard_map/psum | solution.py:494
  2430.1 61.6 %reduce-scatter.27.cloned.1.call-done = f32[1,64,512]{2,1,0:T(8,128)} async-done(((f32[1,1024,512]{2,1,0:T(8,128)}), f32[1,64,512]{2,1,0:T(8,128)}) %reduce-scatter.27.cloned.1.call-update) | async-done | bytes 131088 | tf_op jit(solution)/shard_map/reduce_scatter | solution.py:55
  2493.4 62.5 %reduce-scatter.25.cloned.1.call-done = f32[1,64,512]{2,1,0:T(8,128)} async-done(((f32[1,1024,512]{2,1,0:T(8,128)}), f32[1,64,512]{2,1,0:T(8,128)}) %reduce-scatter.25.cloned.1.call-update) | async-done | bytes 131088 | tf_op jit(solution)/shard_map/reduce_scatter | solution.py:54
  2555.9 64.8 %reduce-scatter.23.cloned.1.call-done = f32[1,64,512]{2,1,0:T(8,128)} async-done(((f32[1,1024,512]{2,1,0:T(8,128)}), f32[1,64,512]{2,1,0:T(8,128)}) %reduce-scatter.23.cloned.1.call-update) | async-done | bytes 131088 | tf_op jit(solution)/shard_map/reduce_scatter | solution.py:54
  2622.4 106.0 %reduce-scatter.41.cloned.1.call-done = f32[1,64,2048]{2,1,0:T(8,128)} async-done(((f32[1,1024,2048]{2,1,0:T(8,128)}), f32[1,64,2048]{2,1,0:T(8,128)}) %reduce-scatter.41.cloned.1.call-update) | async-done | bytes 524304 | tf_op jit(solution)/shard_map/reduce_scatter | solution.py:58
  2728.4 108.3 %reduce-scatter.39.cloned.1.call-done = f32[1,64,2048]{2,1,0:T(8,128)} async-done(((f32[1,1024,2048]{2,1,0:T(8,128)}), f32[1,64,2048]{2,1,0:T(8,128)}) %reduce-scatter.39.cloned.1.call-update) | async-done | bytes 524304 | tf_op jit(solution)/shard_map/reduce_scatter | solution.py:58
  2839.0 106.2 %reduce-scatter.37.cloned.1.call-done = f32[1,64,2048]{2,1,0:T(8,128)} async-done(((f32[1,1024,2048]{2,1,0:T(8,128)}), f32[1,64,2048]{2,1,0:T(8,128)}) %reduce-scatter.37.cloned.1.call-update) | async-done | bytes 524304 | tf_op jit(solution)/shard_map/reduce_scatter | solution.py:57
  2945.2 108.5 %reduce-scatter.35.cloned.1.call-done = f32[1,64,2048]{2,1,0:T(8,128)} async-done(((f32[1,1024,2048]{2,1,0:T(8,128)}), f32[1,64,2048]{2,1,0:T(8,128)}) %reduce-scatter.35.cloned.1.call-update) | async-done | bytes 524304 | tf_op jit(solution)/shard_map/reduce_scatter | solution.py:57
  (1206 shorter events, 1642.0 us)
Async XLA Ops:
  7.9 78.2 %all-gather.39.cloned.1.call-start = ((), (), s32[]{:S(2)}) async-start(), calls=%async_computation.90 | async-start | bytes 1114112 | tf_op jit(solution)/shard_map/all_gather | solution.py:309
  33.2 92.6 %all-gather.37.cloned.1.call-start = ((), (), s32[]{:S(2)}) async-start(), calls=%async_computation.89 | async-start | bytes 1114112 | tf_op jit(solution)/shard_map/all_gather | solution.py:308
  402.5 69.1 %all-gather.41.cloned.1.call-start = ((), (), s32[]{:S(2)}) async-start(), calls=%async_computation.91 | async-start | bytes 1114112 | tf_op jit(solution)/shard_map/all_gather | solution.py:310
  421.2 87.2 %reduce-scatter.15.cloned.1.call-start = ((), (), s32[]{:S(2)}) async-start(), calls=%async_computation.64 | async-start | bytes 3145728 | tf_op jit(solution)/shard_map/reduce_scatter | solution.py:41
  475.3 68.8 %all-gather.23.cloned.1.call-start = ((), (), s32[]{:S(2)}) async-start(), calls=%async_computation.65 | async-start | bytes 3145728 | tf_op jit(solution)/shard_map/all_gather | solution.py:37
  510.8 82.4 %reduce-scatter.17.cloned.1.call-start = ((), (), s32[]{:S(2)}) async-start(), calls=%async_computation.66 | async-start | bytes 3145728 | tf_op jit(solution)/shard_map/reduce_scatter | solution.py:41
  561.3 67.6 %all-gather.25.cloned.1.call-start = ((), (), s32[]{:S(2)}) async-start(), calls=%async_computation.67 | async-start | bytes 3145728 | tf_op jit(solution)/shard_map/all_gather | solution.py:37
  595.6 74.0 %all-gather.45.cloned.1.call-start = ((), (), s32[]{:S(2)}) async-start(), calls=%async_computation.93 | async-start | bytes 1114112 | tf_op jit(solution)/shard_map/all_gather | solution.py:309
  596.3 112.7 %all-gather.43.cloned.1.call-start = ((), (), s32[]{:S(2)}) async-start(), calls=%async_computation.92 | async-start | bytes 1114112 | tf_op jit(solution)/shard_map/all_gather | solution.py:308
  862.6 60.2 %collective-permute-start.3 = (bf16[4,2,64,4,128]{4,2,3,1,0:T(8,128)(2,1)}, bf16[4,2,64,4,128]{4,2,3,1,0:T(8,128)(2,1)}, u32[]{:S(2)}, u32[]{:S(2)}) collective-permute-start(bf16[4,2,64,4,128]{4,2,3,1,0:T(8,128)(2,1)} %copy.920), channel_id=1, source_target_pairs={{0,2},{2,4},{4,6},{6,8},{8,10},{10,12},{12,14},{14,16},{16,18},{18... | collective-permute-start | bytes 1572872 | tf_op jit(solution)/shard_map/ppermute | solution.py:15
  990.7 80.0 %all-gather.47.cloned.1.call-start = ((), (), s32[]{:S(2)}) async-start(), calls=%async_computation.94 | async-start | bytes 1114112 | tf_op jit(solution)/shard_map/all_gather | solution.py:310
  1009.4 98.0 %reduce-scatter.19.cloned.1.call-start = ((), (), s32[]{:S(2)}) async-start(), calls=%async_computation.68 | async-start | bytes 3145728 | tf_op jit(solution)/shard_map/reduce_scatter | solution.py:41
  1074.2 68.9 %all-gather.27.cloned.1.call-start = ((), (), s32[]{:S(2)}) async-start(), calls=%async_computation.69 | async-start | bytes 3145728 | tf_op jit(solution)/shard_map/all_gather | solution.py:37
  1109.8 56.7 %all-gather.29.cloned.1.call-start = ((), (), s32[]{:S(2)}) async-start(), calls=%async_computation.71 | async-start | bytes 1572864 | tf_op jit(solution)/shard_map/all_gather | solution.py:45
  1112.6 133.4 %all-reduce.6.cloned.1.call-start = ((), (), s32[]{:S(2)}) async-start(), calls=%async_computation.72 | async-start | bytes 4194304 | tf_op jit(solution)/shard_map/psum | solution.py:49
  1182.9 92.1 %all-gather.31.cloned.1.call-start = ((), (), s32[]{:S(2)}) async-start(), calls=%async_computation.73 | async-start | bytes 1572864 | tf_op jit(solution)/shard_map/all_gather | solution.py:45
  1618.1 103.8 %all-reduce.8.cloned.1.call-start = ((), (), s32[]{:S(2)}) async-start(), calls=%async_computation.74 | async-start | bytes 4194304 | tf_op jit(solution)/shard_map/psum | solution.py:49
  1657.6 92.7 %all-gather.33.cloned.1.call-start = ((), (), s32[]{:S(2)}) async-start(), calls=%async_computation.75 | async-start | bytes 1572864 | tf_op jit(solution)/shard_map/all_gather | solution.py:45
  1728.8 101.1 %all-reduce.10.cloned.1.call-start = ((), (), s32[]{:S(2)}) async-start(), calls=%async_computation.76 | async-start | bytes 4194304 | tf_op jit(solution)/shard_map/psum | solution.py:49
  1766.8 91.5 %all-gather.35.cloned.1.call-start = ((), (), s32[]{:S(2)}) async-start(), calls=%async_computation.77 | async-start | bytes 1572864 | tf_op jit(solution)/shard_map/all_gather | solution.py:45
  1991.0 324.6 %reduce-scatter.21.cloned.1.call-start = ((), (), s32[]{:S(2)}) async-start(), calls=%async_computation.70 | async-start | bytes 3145728 | tf_op jit(solution)/shard_map/reduce_scatter | solution.py:41
  2150.3 168.9 %reduce-scatter.33.cloned.1.call-start = ((), (), s32[]{:S(2)}) async-start(), calls=%async_computation.84 | async-start | bytes 2228224 | tf_op jit(solution)/shard_map/reduce_scatter | solution.py:56
  2219.0 100.2 %reduce-scatter.31.cloned.1.call-start = ((), (), s32[]{:S(2)}) async-start(), calls=%async_computation.83 | async-start | bytes 2228224 | tf_op jit(solution)/shard_map/reduce_scatter | solution.py:56
  2222.4 139.2 %all-reduce.12.cloned.1.call-start = ((), (), s32[]{:S(2)}) async-start(), calls=%async_computation.78 | async-start | bytes 4194304 | tf_op jit(solution)/shard_map/psum | solution.py:49
  2267.0 163.1 %reduce-scatter.29.cloned.1.call-start = ((), (), s32[]{:S(2)}) async-start(), calls=%async_computation.82 | async-start | bytes 2228224 | tf_op jit(solution)/shard_map/reduce_scatter | solution.py:55
  2270.4 221.3 %reduce-scatter.27.cloned.1.call-start = ((), (), s32[]{:S(2)}) async-start(), calls=%async_computation.81 | async-start | bytes 2228224 | tf_op jit(solution)/shard_map/reduce_scatter | solution.py:55
  2274.0 281.9 %reduce-scatter.25.cloned.1.call-start = ((), (), s32[]{:S(2)}) async-start(), calls=%async_computation.80 | async-start | bytes 2228224 | tf_op jit(solution)/shard_map/reduce_scatter | solution.py:54
  2277.4 343.3 %reduce-scatter.23.cloned.1.call-start = ((), (), s32[]{:S(2)}) async-start(), calls=%async_computation.79 | async-start | bytes 2228224 | tf_op jit(solution)/shard_map/reduce_scatter | solution.py:54
  2280.8 447.5 %reduce-scatter.41.cloned.1.call-start = ((), (), s32[]{:S(2)}) async-start(), calls=%async_computation.88 | async-start | bytes 8912896 | tf_op jit(solution)/shard_map/reduce_scatter | solution.py:58
  2289.3 547.4 %reduce-scatter.39.cloned.1.call-start = ((), (), s32[]{:S(2)}) async-start(), calls=%async_computation.87 | async-start | bytes 8912896 | tf_op jit(solution)/shard_map/reduce_scatter | solution.py:58
  2298.4 646.7 %reduce-scatter.37.cloned.1.call-start = ((), (), s32[]{:S(2)}) async-start(), calls=%async_computation.86 | async-start | bytes 8912896 | tf_op jit(solution)/shard_map/reduce_scatter | solution.py:57
  2307.3 746.4 %reduce-scatter.35.cloned.1.call-start = ((), (), s32[]{:S(2)}) async-start(), calls=%async_computation.85 | async-start | bytes 8912896 | tf_op jit(solution)/shard_map/reduce_scatter | solution.py:57
  (235 other events, 6045.7 us)
Sparse Core Ops, SparseCore 0:
  9.6 35.8 all-gather.20
  48.1 37.9 all-gather.38
  88.9 36.8 all-gather.36
  405.8 42.0 all-gather.40
  475.4 33.0 reduce-scatter.14
  510.9 33.1 all-gather.22
  561.4 31.8 reduce-scatter.16
  595.7 33.1 all-gather.24
  631.6 37.9 all-gather.44
  672.2 36.8 all-gather.42
  994.3 41.9 all-gather.46
  1074.3 33.0 reduce-scatter.18
  1109.9 33.1 all-gather.26
  1145.2 21.2 all-gather.28
  1183.0 62.9 all-reduce.5
  1253.7 21.2 all-gather.30
  1657.7 64.1 all-reduce.7
  1728.9 21.2 all-gather.32
  1766.9 62.9 all-reduce.9
  1837.0 21.2 all-gather.34
  1998.8 32.3 reduce-scatter.20
  2155.4 77.3 reduce-scatter.32
  2236.5 60.9 reduce-scatter.30
  2299.7 61.8 all-reduce.11
  2365.4 61.6 reduce-scatter.28
  2431.1 60.5 reduce-scatter.26
  2495.3 60.5 reduce-scatter.24
  2560.1 60.5 reduce-scatter.22
  2624.8 103.5 reduce-scatter.40
  2732.3 104.3 reduce-scatter.38
  2840.8 104.3 reduce-scatter.36
  2949.2 104.3 reduce-scatter.34
where the time goes:
time: 3080 us; the launch traced here: 3060 us
  waiting for transfers between devices  1510 us (49%)
  local copies, waits for them, and re-layouts  813 us (26%)
  starting transfers between devices  283 us (9%)
  other arithmetic  193 us (6%)
  matrix products  183 us (6%)
  blocking collectives  62.6 us (2%)
    gather x112, local copies, waits for them, and re-layouts, pick_rows(): return array[round_idx, seq_idx, index]  389 us
    psum x4, waiting for transfers between devices, full_grad(): return lax.psum(partial_sum, 'narrow')  231 us
    reduce_scatter x2, waiting for transfers between devices, sum_weights(): lax.psum_scatter(up_part, 'wide', scatter_dimension=1, tiled=True)  215 us
    reduce_scatter x2, waiting for transfers between devices, sum_weights(): lax.psum_scatter(down_part, 'wide', scatter_dimension=1, tiled=True)  214 us
    reduce_scatter x2, waiting for transfers between devices, sum_weights(): lax.psum_scatter(qk_part, 'wide', scatter_dimension=1, tiled=True)  127 us
    all_to_all x16, waiting for transfers between devices, tokens_from_sorted(): lax.all_to_all(to_send(pick_rows(bucket_rows, inv_part)), 'wide', split_a...  119 us
    all_to_all x16, waiting for transfers between devices, sorted_from_tokens(): lax.all_to_all(to_send(picked), 'wide', split_axis=2, concat_axis=2, tile...  117 us
    all_gather x4, waiting for transfers between devices, widen(): return lax.all_gather(stream, 'narrow', axis=1, tiled=True)  98.6 us
  transfers between devices with their start and end apart: 89, of which 61 were waited for; matrix products, arithmetic and copies ran while one was open for 30% of the time, Pallas kernels for 0%

commit v1 on v0

v1 whole, which is shorter than its diff:
```python
import functools

import jax
import jax.numpy as jnp
from jax import lax
from jax.experimental import pallas as pl
from jax.experimental.pallas import tpu as pltpu
from jax.sharding import PartitionSpec as P

HD = 128
GROUP = 64
ROUNDS = 4
LAYERS = 2
BLOCK = 256
F32 = jnp.float32
BF16 = jnp.bfloat16
SCALE = HD ** (-0.5)
VMEM_LIMIT = 56 * 1024 * 1024


def swap(value, axis, mask):
    count = lax.axis_size(axis)
    return lax.ppermute(value, axis, [(source, source ^ mask) for source in range(count)])


def dot(left, right, dims):
    return lax.dot_general(left, right, (dims, ((), ())), preferred_element_type=F32)


def mm(left, right):
    return dot(left, right, ((1,), (0,)))


def mm_t(left, right):
    return dot(left, right, ((1,), (1,)))


def t_mm(left, right):
    return dot(left, right, ((0,), (0,)))


def chip_exchange(slots):
    return [slots[0]] + [swap(slots[k], "wide", 2 * k) for k in range(1, len(slots))]


def split3(value):
    high = value.astype(BF16)
    rest = value - high.astype(F32)
    mid = rest.astype(BF16)
    low = (rest - mid.astype(F32)).astype(BF16)
    return high.astype(F32), mid.astype(F32), low.astype(F32)


def exact_split3(value):
    high = lax.reduce_precision(value, 8, 7)
    mid = lax.reduce_precision(value - high, 8, 7)
    low = lax.reduce_precision(value - high - mid, 8, 7)
    return high, mid, low


def layer_norm(stream, gain, shift):
    centre = stream - jnp.mean(stream, axis=-1, keepdims=True)
    spread = jnp.mean(centre * centre, axis=-1, keepdims=True)
    return centre * lax.rsqrt(spread + 1e-05) * gain + shift


def layer_norm_back(stream, gain, grad):
    centre = stream - jnp.mean(stream, axis=-1, keepdims=True)
    inv = lax.rsqrt(jnp.mean(centre * centre, axis=-1, keepdims=True) + 1e-05)
    unit = centre * inv
    scaled = grad * gain
    back = inv * (
        scaled
        - jnp.mean(scaled, axis=-1, keepdims=True)
        - unit * jnp.mean(scaled * unit, axis=-1, keepdims=True)
    )
    return back, unit


def build_tables(tokens):
    rounds, seq = tokens.shape
    blocks = seq // BLOCK
    rank_rows = BLOCK // blocks
    tokens = tokens.reshape(rounds, blocks, BLOCK)
    run = tokens // BLOCK
    row = tokens % BLOCK
    onehot = (run[..., None] == jnp.arange(blocks, dtype=jnp.int32)).astype(BF16)
    before = (jnp.arange(BLOCK)[:, None] > jnp.arange(BLOCK)[None, :]).astype(BF16)
    counts = jnp.einsum("jl,rkla->rkja", before, onehot, preferred_element_type=F32)
    rank = jnp.sum(onehot.astype(F32) * counts, axis=-1).astype(jnp.int32)
    slot = run * rank_rows + rank
    iota = jnp.arange(BLOCK, dtype=jnp.int32)
    into = (slot[..., None] == iota).astype(BF16)
    into_t = (slot[..., None, :] == iota[:, None]).astype(BF16)
    wants = jnp.einsum("rknj,rkj->rkn", into_t, row.astype(BF16), preferred_element_type=F32)
    wants = wants.reshape(rounds, blocks, blocks, rank_rows)
    wants = jnp.transpose(wants, (0, 2, 1, 3)).reshape(rounds, blocks, BLOCK).astype(jnp.int32)
    out_of = (wants[..., None] == iota).astype(BF16)
    out_of_t = (wants[..., None, :] == iota[:, None]).astype(BF16)
    return out_of, into, out_of_t, into_t


def load_tokens(pos_ref, own_ref, sib_ref, tok, sems, slots, rows):
    chip, core = pos_ref[0], pos_ref[1]
    copies = []
    for k in range(slots):
        other = chip ^ k
        for half, source in ((0, own_ref), (1, sib_ref)):
            start = pl.multiple_of((2 * other + (core ^ half)) * rows, rows)
            copies.append(
                pltpu.make_async_copy(
                    source.at[k], tok.at[pl.ds(start, rows)], sems.at[2 * k + half]
                )
            )
    for copy in copies:
        copy.start()
    for copy in copies:
        copy.wait()


def store_run(pos_ref, out_ref, run, value, rows):
    chip, core = pos_ref[0], pos_ref[1]
    for part in range(BLOCK // rows):
        device = run * (BLOCK // rows) + part
        out_ref[(device & 1) ^ core, (device >> 1) ^ chip] = value[part * rows : (part + 1) * rows]


def permute_in(tok, out_of, mixed, blocks):
    def body(a, carry):
        source = tok[pl.ds(pl.multiple_of(a * BLOCK, BLOCK), BLOCK), :]
        moved = mm(out_of[0, a], source).astype(BF16)
        mixed[:, a] = moved.reshape(blocks, BLOCK // blocks, 2 * HD)
        return carry

    lax.fori_loop(0, blocks, body, 0)


def self_mask():
    row = lax.broadcasted_iota(jnp.int32, (GROUP, 2 * GROUP), 0)
    col = lax.broadcasted_iota(jnp.int32, (GROUP, 2 * GROUP), 1)
    return col == row + GROUP


def forward_kernel(
    slots, rows, pos_ref, own_ref, sib_ref, out_of, into, out_of_t, into_t,
    sorted_ref, mix_ref, tok, mixed, keys, vals, first_out, first_lse, sems,
):
    seq = tok.shape[0]
    blocks = seq // BLOCK
    step = pl.program_id(0)

    @pl.when(step == 0)
    def _():
        load_tokens(pos_ref, own_ref, sib_ref, tok, sems, slots, rows)

    permute_in(tok, out_of, mixed, blocks)

    def place(k, carry):
        base = pl.multiple_of(k * BLOCK, BLOCK)
        rows_sorted = mm(into[0, k], mixed[k].reshape(BLOCK, 2 * HD))
        sorted_ref[0, pl.ds(base, BLOCK), :] = rows_sorted.astype(BF16)
        query = rows_sorted[:, :HD]
        unit = query * lax.rsqrt(jnp.mean(query * query, axis=-1, keepdims=True) + 1e-06)
        where = pl.ds(pl.multiple_of(base + GROUP, GROUP), BLOCK)
        keys[where, :] = unit.astype(BF16)
        vals[where, :] = rows_sorted[:, HD:].astype(BF16)
        return carry

    lax.fori_loop(0, blocks, place, 0)
    keys[0:GROUP, :] = keys[seq : seq + GROUP, :]
    vals[0:GROUP, :] = vals[seq : seq + GROUP, :]

    def attend(k, carry):
        lane = lax.broadcasted_iota(jnp.int32, (GROUP, HD), 1)
        own = self_mask()
        pieces = []
        for b in range(BLOCK // GROUP):
            base = pl.multiple_of(k * BLOCK + b * GROUP, GROUP)
            query = sorted_ref[0, pl.ds(base, GROUP), 0:HD]
            window = pl.ds(base, 2 * GROUP)
            scores = jnp.where(own, -1000000000.0, mm_t(query, keys[window, :]) * SCALE)
            top = jnp.max(scores, axis=-1, keepdims=True)
            weight = jnp.exp(scores - top)
            total = jnp.sum(weight, axis=-1, keepdims=True)
            result = mm(weight.astype(BF16), vals[window, :]) / total
            high, mid, low = split3(top + jnp.log(total))
            extra = jnp.where(
                lane == 0, high, jnp.where(lane == 1, mid, jnp.where(lane == 2, low, 0.0))
            )
            pieces.append(jnp.concatenate([result, extra], axis=1).astype(BF16))
        packed = jnp.concatenate(pieces, axis=0)
        back = mm(into_t[0, k], packed).astype(BF16)
        mixed[k] = back.reshape(blocks, BLOCK // blocks, 2 * HD)
        return carry

    lax.fori_loop(0, blocks, attend, 0)

    def back_tokens(a):
        source = mixed[:, a].reshape(BLOCK, 2 * HD)
        moved = mm(out_of_t[0, a], source)
        return moved[:, :HD], jnp.sum(moved[:, HD:], axis=-1, keepdims=True)

    @pl.when(step == 0)
    def _():
        def body(a, carry):
            where = pl.ds(pl.multiple_of(a * BLOCK, BLOCK), BLOCK)
            value, lse = back_tokens(a)
            first_out[where, :] = value
            first_lse[where, :] = jnp.broadcast_to(lse, (BLOCK, HD))
            return carry

        lax.fori_loop(0, blocks, body, 0)

    @pl.when(step == 1)
    def _():
        def body(a, carry):
            where = pl.ds(pl.multiple_of(a * BLOCK, BLOCK), BLOCK)
            value, lse = back_tokens(a)
            lse_a = first_lse[where, :]
            top = jnp.maximum(lse_a, lse)
            both = top + jnp.log(jnp.exp(lse_a - top) + jnp.exp(lse - top))
            value = first_out[where, :] * jnp.exp(lse_a - both) + value * jnp.exp(lse - both)
            high, mid, low = split3(both)
            lane = lax.broadcasted_iota(jnp.int32, (BLOCK, HD), 1)
            extra = jnp.where(
                lane == 0, high, jnp.where(lane == 1, mid, jnp.where(lane == 2, low, 0.0))
            )
            packed = jnp.concatenate([value, extra], axis=1).astype(BF16)
            store_run(pos_ref, mix_ref, a, packed, rows)
            return carry

        lax.fori_loop(0, blocks, body, 0)


def backward_kernel(
    slots, rows, pos_ref, own_ref, sib_ref, sorted_ref, out_of, into, out_of_t, into_t,
    out_ref, tok, mixed, keys, vals, grads, query_use, key_grad, val_grad, acc, sems,
):
    seq = tok.shape[0]
    blocks = seq // BLOCK
    step = pl.program_id(0)

    @pl.when(step == 0)
    def _():
        load_tokens(pos_ref, own_ref, sib_ref, tok, sems, slots, rows)

    permute_in(tok, out_of, mixed, blocks)

    def place(k, carry):
        base = pl.multiple_of(k * BLOCK, BLOCK)
        grads[pl.ds(base, BLOCK), :] = mm(
            into[0, k], mixed[k].reshape(BLOCK, 2 * HD)
        ).astype(BF16)
        query = sorted_ref[0, pl.ds(base, BLOCK), 0:HD].astype(F32)
        unit = query * lax.rsqrt(jnp.mean(query * query, axis=-1, keepdims=True) + 1e-06)
        where = pl.ds(pl.multiple_of(base + GROUP, GROUP), BLOCK)
        keys[where, :] = unit.astype(BF16)
        vals[where, :] = sorted_ref[0, pl.ds(base, BLOCK), HD:]
        return carry

    lax.fori_loop(0, blocks, place, 0)
    keys[0:GROUP, :] = keys[seq : seq + GROUP, :]
    vals[0:GROUP, :] = vals[seq : seq + GROUP, :]
    key_grad[0:GROUP, :] = jnp.zeros((GROUP, HD), F32)
    val_grad[0:GROUP, :] = jnp.zeros((GROUP, HD), F32)

    def attend(k, carry):
        lane = lax.broadcasted_iota(jnp.int32, (GROUP, HD), 1)
        own = self_mask()
        for b in range(BLOCK // GROUP):
            base = pl.multiple_of(k * BLOCK + b * GROUP, GROUP)
            here = pl.ds(base, GROUP)
            window = pl.ds(base, 2 * GROUP)
            later = pl.ds(pl.multiple_of(base + GROUP, GROUP), GROUP)
            query = sorted_ref[0, here, 0:HD]
            grad = grads[here, 0:HD]
            stats = grads[here, HD:].astype(F32)
            delta = jnp.sum(jnp.where(lane < 3, stats, 0.0), axis=-1, keepdims=True)
            lse = jnp.sum(jnp.where(lane >= 3, stats, 0.0), axis=-1, keepdims=True)
            key = keys[window, :]
            scores = jnp.where(own, -1000000000.0, mm_t(query, key) * SCALE)
            probs = jnp.exp(scores - lse)
            prob_grad = mm_t(grad, vals[window, :])
            score_grad = (probs * (prob_grad - delta)).astype(BF16)
            query_use[here, :] = mm(score_grad, key) * SCALE
            key_part = t_mm(score_grad, query) * SCALE
            val_part = t_mm(probs.astype(BF16), grad)
            key_grad[here, :] += key_part[:GROUP]
            val_grad[here, :] += val_part[:GROUP]
            key_grad[later, :] = key_part[GROUP:]
            val_grad[later, :] = val_part[GROUP:]
        return carry

    lax.fori_loop(0, blocks, attend, 0)
    key_grad[seq : seq + GROUP, :] += key_grad[0:GROUP, :]
    val_grad[seq : seq + GROUP, :] += val_grad[0:GROUP, :]

    def gather_back(k, carry):
        base = pl.multiple_of(k * BLOCK, BLOCK)
        where = pl.ds(pl.multiple_of(base + GROUP, GROUP), BLOCK)
        query = sorted_ref[0, pl.ds(base, BLOCK), 0:HD].astype(F32)
        inv = lax.rsqrt(jnp.mean(query * query, axis=-1, keepdims=True) + 1e-06)
        grad = key_grad[where, :]
        inner = jnp.mean(grad * query, axis=-1, keepdims=True)
        total = query_use[pl.ds(base, BLOCK), :] + inv * (grad - query * (inner * inv * inv))
        packed = jnp.concatenate([total, val_grad[where, :]], axis=1).astype(BF16)
        back = mm(into_t[0, k], packed).astype(BF16)
        mixed[k] = back.reshape(blocks, BLOCK // blocks, 2 * HD)
        return carry

    lax.fori_loop(0, blocks, gather_back, 0)

    @pl.when(step == 0)
    def _():
        def body(a, carry):
            where = pl.ds(pl.multiple_of(a * BLOCK, BLOCK), BLOCK)
            acc[where, :] = mm(out_of_t[0, a], mixed[:, a].reshape(BLOCK, 2 * HD))
            return carry

        lax.fori_loop(0, blocks, body, 0)

    @pl.when(step == 1)
    def _():
        def body(a, carry):
            where = pl.ds(pl.multiple_of(a * BLOCK, BLOCK), BLOCK)
            total = acc[where, :] + mm(out_of_t[0, a], mixed[:, a].reshape(BLOCK, 2 * HD))
            store_run(pos_ref, out_ref, a, total.astype(BF16), rows)
            return carry

        lax.fori_loop(0, blocks, body, 0)


def table_specs(blocks):
    return [pl.BlockSpec((1, blocks, BLOCK, BLOCK), lambda r: (r, 0, 0, 0))] * 4


def params():
    return pltpu.CompilerParams(vmem_limit_bytes=VMEM_LIMIT)


def attention_forward(pos, own, sib, tables):
    slots, rows, width = own.shape
    seq = 2 * slots * rows
    blocks = seq // BLOCK
    return pl.pallas_call(
        functools.partial(forward_kernel, slots, rows),
        grid=(2,),
        out_shape=(
            jax.ShapeDtypeStruct((2, seq, width), BF16),
            jax.ShapeDtypeStruct((2, slots, rows, width), BF16),
        ),
        in_specs=[pl.BlockSpec(memory_space=pltpu.SMEM)]
        + [pl.BlockSpec(memory_space=pl.ANY)] * 2
        + table_specs(blocks),
        out_specs=(
            pl.BlockSpec((1, seq, width), lambda r: (r, 0, 0)),
            pl.BlockSpec((2, slots, rows, width), lambda r: (0, 0, 0, 0)),
        ),
        scratch_shapes=[
            pltpu.VMEM((seq, width), BF16),
            pltpu.VMEM((blocks, blocks, BLOCK // blocks, width), BF16),
            pltpu.VMEM((seq + GROUP, HD), BF16),
            pltpu.VMEM((seq + GROUP, HD), BF16),
            pltpu.VMEM((seq, HD), F32),
            pltpu.VMEM((seq, HD), F32),
            pltpu.SemaphoreType.DMA((2 * slots,)),
        ],
        compiler_params=params(),
        name="attend_forward",
    )(pos, own, sib, *tables)


def attention_backward(pos, own, sib, sorted_rows, tables):
    slots, rows, width = own.shape
    seq = 2 * slots * rows
    blocks = seq // BLOCK
    return pl.pallas_call(
        functools.partial(backward_kernel, slots, rows),
        grid=(2,),
        out_shape=jax.ShapeDtypeStruct((2, slots, rows, width), BF16),
        in_specs=[pl.BlockSpec(memory_space=pltpu.SMEM)]
        + [pl.BlockSpec(memory_space=pl.ANY)] * 2
        + [pl.BlockSpec((1, seq, width), lambda r: (r, 0, 0))]
        + table_specs(blocks),
        out_specs=pl.BlockSpec((2, slots, rows, width), lambda r: (0, 0, 0, 0)),
        scratch_shapes=[
            pltpu.VMEM((seq, width), BF16),
            pltpu.VMEM((blocks, blocks, BLOCK // blocks, width), BF16),
            pltpu.VMEM((seq + GROUP, HD), BF16),
            pltpu.VMEM((seq + GROUP, HD), BF16),
            pltpu.VMEM((seq, width), BF16),
            pltpu.VMEM((seq, HD), F32),
            pltpu.VMEM((seq + GROUP, HD), F32),
            pltpu.VMEM((seq + GROUP, HD), F32),
            pltpu.VMEM((seq, width), F32),
            pltpu.SemaphoreType.DMA((2 * slots,)),
        ],
        compiler_params=params(),
        name="attend_backward",
    )(pos, own, sib, sorted_rows, *tables)


def project_kernel(slots, rows, heads, pos_ref, normed_ref, weight_ref, *out_refs):
    for k in range(slots):
        unit = pos_ref[0] ^ k
        start = pl.multiple_of((unit // heads) * rows, rows)
        value = mm(normed_ref[pl.ds(start, rows), :], weight_ref[unit % heads])
        out_refs[k][...] = value.astype(BF16)


def project_units(pos, normed, weight, rows):
    heads, _, width = weight.shape
    slots = normed.shape[0] // rows * heads
    return pl.pallas_call(
        functools.partial(project_kernel, slots, rows, heads),
        out_shape=[jax.ShapeDtypeStruct((rows, width), BF16)] * slots,
        in_specs=[pl.BlockSpec(memory_space=pltpu.SMEM)]
        + [pl.BlockSpec(memory_space=pltpu.VMEM)] * 2,
        out_specs=[pl.BlockSpec(memory_space=pltpu.VMEM)] * slots,
        compiler_params=params(),
        name="project_units",
    )(pos, normed, weight)


def merge_kernel(slots, rows, heads, pos_ref, weight_ref, *refs):
    ins, (part_ref, tok_ref) = refs[:slots], refs[slots:]
    width = ins[0].shape[1]
    for k in range(slots):
        unit = pos_ref[0] ^ k
        start = pl.multiple_of((unit // heads) * rows, rows)
        lane = pl.multiple_of((unit % heads) * width, width)
        tok_ref[pl.ds(start, rows), pl.ds(lane, width)] = ins[k][...]
    part_ref[...] = mm_t(tok_ref[...], weight_ref[...]).astype(BF16)


def merge_units(pos, pieces, weight, seqs):
    slots = len(pieces)
    rows, width = pieces[0].shape
    heads = slots // seqs
    return pl.pallas_call(
        functools.partial(merge_kernel, slots, rows, heads),
        out_shape=(
            jax.ShapeDtypeStruct((seqs * rows, weight.shape[0]), BF16),
            jax.ShapeDtypeStruct((seqs * rows, heads * width), BF16),
        ),
        in_specs=[pl.BlockSpec(memory_space=pltpu.SMEM)]
        + [pl.BlockSpec(memory_space=pltpu.VMEM)] * (1 + slots),
        out_specs=(
            pl.BlockSpec(memory_space=pltpu.VMEM),
            pl.BlockSpec(memory_space=pltpu.VMEM),
        ),
        compiler_params=params(),
        name="merge_units",
    )(pos, weight, *pieces)


def reduce_rows(value):
    count = lax.axis_size("wide")
    index = lax.axis_index("wide")
    width = value.shape[1]
    block = value.shape[0] // count
    value = value.astype(BF16)
    bit = 1
    parts = count
    while bit < count:
        view = value.reshape(parts // 2, 2, block, width)
        mine = (index // bit) % 2
        sent = lax.dynamic_index_in_dim(view, 1 - mine, 1, keepdims=False)
        kept = lax.dynamic_index_in_dim(view, mine, 1, keepdims=False)
        value = kept.astype(F32) + swap(sent, "wide", bit).astype(F32)
        parts //= 2
        bit *= 2
        if bit < count:
            value = value.astype(BF16)
    return value.reshape(block, width)


def sum_all(value):
    for bit in range(lax.axis_size("wide").bit_length() - 1):
        value = value + swap(value, "wide", 1 << bit)
    return value + swap(value, "narrow", 1)


def shards(
    first_in, second_in, attn_norm_gain, attn_norm_bias, qk_weight, value_weight, out_weight,
    out_bias, ffn_norm_gain, ffn_norm_bias, up_weight, up_bias, down_weight, down_bias,
    bucket_perm, first_cot, second_cot,
):
    seqs, rows, half = first_in.shape
    toks = seqs * rows
    wide = lax.axis_size("wide")
    wide_index = lax.axis_index("wide")
    narrow_index = lax.axis_index("narrow")
    chip, core = wide_index // 2, wide_index % 2
    pos = jnp.stack([chip, core]).astype(jnp.int32)
    weight_rows, head_width = qk_weight.shape[1:]
    heads = head_width // HD
    width = 2 * half

    def whole(mine, other):
        other = other.astype(mine.dtype)
        return jnp.where(
            narrow_index == 0,
            jnp.concatenate([mine, other], axis=-1),
            jnp.concatenate([other, mine], axis=-1),
        )

    def widen(mine):
        return whole(mine, swap(mine.astype(BF16), "narrow", 1))

    def own_half(full):
        return lax.dynamic_slice_in_dim(full, narrow_index * half, half, full.ndim - 1)

    second = widen(second_in.reshape(toks, half))
    first = widen(first_in.reshape(toks, half))
    grad_second = widen(second_cot.reshape(toks, half))
    grad_first = widen(first_cot.reshape(toks, half))
    out_bias = whole(out_bias, swap(out_bias, "narrow", 1))
    down_bias = whole(down_bias, swap(down_bias, "narrow", 1))

    perm_parts = bucket_perm.reshape(2, ROUNDS // 2, seqs, rows)
    target = jnp.arange(wide)
    perm_send = jnp.transpose(perm_parts, (2, 0, 1, 3))
    perm_send = jnp.broadcast_to(
        perm_send[:, None], (seqs, heads, 2, ROUNDS // 2, rows)
    ).reshape(wide, ROUNDS // 2, rows)
    perm_got = lax.all_to_all(perm_send, "wide", 0, 0, tiled=True)
    tables = build_tables(jnp.transpose(perm_got, (1, 0, 2)).reshape(ROUNDS // 2, wide * rows))

    gathered = lax.all_gather(
        jnp.stack([qk_weight, value_weight, out_weight]), "wide", axis=0
    )

    def unit_weight(layer):
        pair = gathered[:, 0:2, layer].reshape(wide, 2, weight_rows, heads, HD)
        return jnp.transpose(pair, (3, 0, 2, 1, 4)).reshape(heads, wide * weight_rows, 2 * HD)

    unit_weights = [unit_weight(layer) for layer in range(LAYERS)]
    out_weights = [
        gathered[:, 2, layer].reshape(wide * weight_rows, head_width) for layer in range(LAYERS)
    ]
    saved = []
    for layer in range(LAYERS):
        normed = layer_norm(second, attn_norm_gain[layer], attn_norm_bias[layer]).astype(BF16)
        pieces = project_units(pos, normed, unit_weights[layer], rows)
        own = jnp.stack(chip_exchange(pieces))
        sib = swap(own, "wide", 1)
        sorted_rows, mix = attention_forward(pos, own, sib, tables)
        got = swap(mix[1], "wide", 1)
        lse_a = jnp.sum(mix[0, :, :, HD:].astype(F32), axis=-1, keepdims=True)
        lse_b = jnp.sum(got[:, :, HD:].astype(F32), axis=-1, keepdims=True)
        top = jnp.maximum(lse_a, lse_b)
        lse = top + jnp.log(jnp.exp(lse_a - top) + jnp.exp(lse_b - top))
        attn = mix[0, :, :, :HD].astype(F32) * jnp.exp(lse_a - lse) + got[:, :, :HD].astype(
            F32
        ) * jnp.exp(lse_b - lse)
        attn_low = attn.astype(BF16)
        back = chip_exchange([attn_low[k] for k in range(wide // 2)])
        part, attn_tok = merge_units(pos, back, out_weights[layer], seqs)
        other = swap(part, "narrow", 1)
        first = first + (part.astype(F32) + other.astype(F32)) + out_bias[layer]
        ffn_in = layer_norm(first, ffn_norm_gain[layer], ffn_norm_bias[layer]).astype(BF16)
        pre_act = mm(ffn_in, up_weight[layer]) + up_bias[layer]
        hidden = jax.nn.gelu(pre_act, approximate=True).astype(BF16)
        part = mm_t(hidden, down_weight[layer]).astype(BF16)
        other = swap(part, "narrow", 1)
        saved.append((second, normed, sorted_rows, attn, lse, attn_tok, first, ffn_in, pre_act, hidden))
        second = second + (part.astype(F32) + other.astype(F32)) + down_bias[layer]
    first_out, second_out = own_half(first), own_half(second)

    weight_grads = [None] * LAYERS
    small_grads = [None] * LAYERS
    for layer in reversed(range(LAYERS)):
        second_l, normed, sorted_rows, attn, lse, attn_tok, first_l, ffn_in, pre_act, hidden = saved[layer]
        branch = grad_second.astype(BF16)
        down_bias_grad = jnp.sum(own_half(grad_second), axis=0)
        hidden_grad = mm(branch, down_weight[layer])
        pre_grad = jax.vjp(lambda u: jax.nn.gelu(u, approximate=True), pre_act)[1](hidden_grad)[0]
        up_bias_grad = jnp.sum(pre_grad, axis=0)
        pre_low = pre_grad.astype(BF16)
        part = mm_t(pre_low, up_weight[layer]).astype(BF16)
        other = swap(part, "narrow", 1)
        down_weight_grad = reduce_rows(t_mm(branch, hidden))
        up_weight_grad = reduce_rows(t_mm(ffn_in, pre_low))
        ffn_in_grad = part.astype(F32) + other.astype(F32)
        stream_part, unit = layer_norm_back(first_l, ffn_norm_gain[layer], ffn_in_grad)
        ffn_gain_grad = jnp.sum(own_half(ffn_in_grad * unit), axis=0)
        ffn_bias_grad = jnp.sum(own_half(ffn_in_grad), axis=0)
        grad_first = grad_first + stream_part
        out_low = grad_first.astype(BF16)
        out_bias_grad = jnp.sum(own_half(grad_first), axis=0)
        by_head = jnp.transpose(out_weights[layer].reshape(width, heads, HD), (1, 0, 2))
        pieces = project_units(pos, out_low, by_head, rows)
        attn_grad = jnp.stack(chip_exchange(pieces))
        delta = jnp.sum(attn * attn_grad.astype(F32), axis=-1, keepdims=True)
        lane = jnp.arange(HD)
        extra = jnp.zeros(attn.shape, F32)
        for place, column in enumerate(exact_split3(delta) + exact_split3(lse)):
            extra = jnp.where(lane == place, column, extra)
        own = jnp.concatenate([attn_grad, extra.astype(BF16)], axis=-1)
        sib = swap(own, "wide", 1)
        grads = attention_backward(pos, own, sib, sorted_rows, tables)
        total = grads[0].astype(F32) + swap(grads[1], "wide", 1).astype(F32)
        total = total.astype(BF16)
        back = chip_exchange([total[k] for k in range(wide // 2)])
        flat = jnp.transpose(unit_weights[layer], (1, 0, 2)).reshape(width, heads * 2 * HD)
        part, grad_tok = merge_units(pos, back, flat, seqs)
        other = swap(part, "narrow", 1)
        out_weight_grad = reduce_rows(t_mm(out_low, attn_tok))
        unit_weight_grad = reduce_rows(t_mm(normed, grad_tok))
        normed_grad = part.astype(F32) + other.astype(F32)
        stream_part, unit = layer_norm_back(second_l, attn_norm_gain[layer], normed_grad)
        attn_gain_grad = jnp.sum(own_half(normed_grad * unit), axis=0)
        attn_bias_grad = jnp.sum(own_half(normed_grad), axis=0)
        grad_second = grad_second + stream_part
        by_unit = unit_weight_grad.reshape(weight_rows, heads, 2, HD)
        weight_grads[layer] = (
            by_unit[:, :, 0].reshape(weight_rows, head_width),
            by_unit[:, :, 1].reshape(weight_rows, head_width),
            out_weight_grad,
            up_weight_grad,
            down_weight_grad,
        )
        own_parts = jnp.concatenate(
            [
                jnp.stack(
                    [attn_gain_grad, attn_bias_grad, ffn_gain_grad, ffn_bias_grad,
                     out_bias_grad, down_bias_grad]
                ),
                up_bias_grad.reshape(-1, half),
            ]
        )
        blank = jnp.zeros_like(own_parts)
        both = jnp.where(
            narrow_index == 0, jnp.stack([own_parts, blank]), jnp.stack([blank, own_parts])
        )
        small_grads[layer] = sum_all(both)

    def full_small(row):
        return jnp.stack([small_grads[layer][:, row].reshape(width) for layer in range(LAYERS)])

    def own_small(low, high):
        return jnp.stack(
            [
                lax.dynamic_index_in_dim(small_grads[layer], narrow_index, 0, keepdims=False)[
                    low:high
                ].reshape(-1)
                for layer in range(LAYERS)
            ]
        )

    def stacked(slot):
        return jnp.stack([weight_grads[layer][slot] for layer in range(LAYERS)])

    shape = (seqs, rows, half)
    return (
        first_out.reshape(shape),
        second_out.reshape(shape),
        own_half(grad_first).reshape(shape),
        own_half(grad_second).reshape(shape),
        full_small(0),
        full_small(1),
        stacked(0),
        stacked(1),
        stacked(2),
        own_small(4, 5),
        full_small(2),
        full_small(3),
        stacked(3),
        own_small(6, 6 + up_bias.shape[1] // half),
        stacked(4),
        own_small(5, 6),
    )


def solution(mesh):
    streams = P(None, "wide", "narrow")
    features = P(None, "narrow")
    hidden = P(None, None, "narrow")
    return jax.shard_map(
        shards,
        mesh=mesh,
        in_specs=(
            streams, streams, P(), P(), streams, streams, streams, features, P(), P(),
            hidden, features, hidden, features, P(None, None, "wide"), streams, streams,
        ),
        out_specs=(
            streams, streams, streams, streams, P(), P(), streams, streams, streams,
            features, P(), P(), streams, features, streams, features,
        ),
        check_vma=False,
    )
```

time: 3080 us -> 1080 us (0.35)
  waiting for transfers between devices: 1510 us -> 322 us
  local copies, waits for them, and re-layouts: 813 us -> 98.3 us
  Pallas kernels: 0 us -> 307 us
  matrix products: 183 us -> 64.6 us
  starting transfers between devices: 283 us -> 167 us
  other arithmetic: 193 us -> 92.8 us
  blocking collectives: 62.6 us -> 0 us
    reduce_scatter x14 -> x0, waiting for transfers between devices: 715 us -> none  [the longest x2 215 us: sum_weights(): lax.psum_scatter(up_part, 'wide', scatter_dimension=1, tiled=True)]
    gather x120 -> x0, local copies, waits for them, and re-layouts: 430 us -> none  [the longest x112 389 us: pick_rows(): return array[round_idx, seq_idx, index]]
    pallas_call x0 -> x12, Pallas kernels: none -> 307 us  [the longest x2 143 us: attention_backward(): pl.pallas_call(functools.partial(backward_kernel, slots, rows), grid=(2,)...]
    ppermute x8 -> x120, waiting for transfers between devices: 6.89 us -> 271 us  [swap(): lax.ppermute(value, axis, [(source, source ^ mask) for source in range(co...]
    all_to_all x49 -> x1, starting transfers between devices: 265 us -> 5.91 us  [shards(): perm_got = lax.all_to_all(perm_send, 'wide', 0, 0, tiled=True)]
    all_gather x14 -> x1, waiting for transfers between devices: 303 us -> 45.1 us  [shards(): lax.all_gather(jnp.stack([qk_weight, value_weight, out_weight]), 'wide',...]
    all_to_all x49 -> x1, waiting for transfers between devices: 251 us -> 6.04 us  [shards(): perm_got = lax.all_to_all(perm_send, 'wide', 0, 0, tiled=True)]
    psum x4 -> x0, waiting for transfers between devices: 231 us -> none  [full_grad(): return lax.psum(partial_sum, 'narrow')]
  transfers between devices with their start and end apart: 89 -> 122, of which waited for: 61 -> 51; matrix products, arithmetic and copies ran while one was open for 30% -> 16% of each run, Pallas kernels for 0% -> 15%
where the time goes in v1:
time: 1080 us; the launch traced here: 1070 us
  waiting for transfers between devices  322 us (30%)
  Pallas kernels  307 us (28%)
  starting transfers between devices  167 us (15%)
  local copies, waits for them, and re-layouts  98.3 us (9%)
  other arithmetic  92.8 us (9%)
  matrix products  64.6 us (6%)
  between operations  17.5 us (2%)
    ppermute x120, waiting for transfers between devices, swap(): lax.ppermute(value, axis, [(source, source ^ mask) for source in range(co...  271 us
    ppermute x120, starting transfers between devices, swap(): lax.ppermute(value, axis, [(source, source ^ mask) for source in range(co...  161 us
    pallas_call x2, Pallas kernels, attention_backward(): pl.pallas_call(functools.partial(backward_kernel, slots, rows), grid=(2,)...  143 us
    pallas_call x2, Pallas kernels, attention_forward(): pl.pallas_call(functools.partial(forward_kernel, slots, rows), grid=(2,),...  134 us
    dot_general x16, matrix products, dot(): lax.dot_general(left, right, (dims, ((), ())), preferred_element_type=F32)  62.9 us
    all_gather x1, waiting for transfers between devices, shards(): lax.all_gather(jnp.stack([qk_weight, value_weight, out_weight]), 'wide',...  45.1 us
    unnamed x352, local copies, waits for them, and re-layouts  32.4 us
  transfers between devices with their start and end apart: 122, of which 51 were waited for; matrix products, arithmetic and copies ran while one was open for 16% of the time, Pallas kernels for 15%

profile of v1, /device:TPU:0, one launch (start us, length us, event | category | flops | bytes accessed | tf_op | source)
XLA Modules:
  0.0 1069.1 jit_solution(9737996104444257580)
XLA Ops:
  14.2 5.9 all-to-all-start
  20.7 6.0 all-to-all-done
  30.4 45.1 %all-gather.3.cloned.1.call-done = bf16[48,2,64,512]{3,2,1,0:T(8,128)(2,1)} async-done(((bf16[3,2,64,512]{3,2,1,0:T(8,128)(2,1)}), bf16[48,2,64,512]{3,2,1,0:T(8,128)(2,1)}) %all-gather.3.cloned.1.call-update) | async-done | bytes 6291472 | tf_op jit(solution)/shard_map/all_gather | solution.py:530
  108.9 7.6 collective-permute-done.5
  121.1 7.3 fusion
  128.4 67.2 %attend_forward.2 = (bf16[2,4096,256]{2,1,0:T(8,128)(2,1)}, bf16[2,8,256,256]{3,2,1,0:T(8,128)(2,1)}) custom-call(s32[2]{0:T(128)} %pad_add_fusion.pos_ref, bf16[8,256,256]{2,1,0:T(8,128)(2,1)} %copy-done.53, bf16[8,256,256]{2,1,0:T(8,128)(2,1)} %collective-permute-done.9.sib_ref, bf16[2,16,256,256]{3,2,1,0:T(8,128)(2,1)} %get-tuple-element.241.out_of, ...), custom_call_target="tpu_custom_call" | custom-call | tf_op jit(solution)/shard_map/attend_forward/pallas_call | solution.py:345
  228.3 8.9 collective-permute-done
  237.2 19.5 %collective-permute-done.18 = bf16[512,1024]{1,0:T(8,128)(2,1)S(1)} collective-permute-done((bf16[512,1024]{1,0:T(8,128)(2,1)}, bf16[512,1024]{1,0:T(8,128)(2,1)S(1)}, u32[]{:S(2)}, u32[]{:S(2)}) %collective-permute-start.18) | collective-permute-done | bytes 1048608 | tf_op jit(solution)/shard_map/ppermute | solution.py:23
  258.0 5.5 fusion.35
  282.6 7.4 collective-permute-done.20
  311.5 7.6 collective-permute-done.25
  327.0 67.1 %attend_forward.3 = (bf16[2,4096,256]{2,1,0:T(8,128)(2,1)}, bf16[2,8,256,256]{3,2,1,0:T(8,128)(2,1)}) custom-call(s32[2]{0:T(128)} %pad_add_fusion.pos_ref, bf16[8,256,256]{2,1,0:T(8,128)(2,1)} %copy-done.54, bf16[8,256,256]{2,1,0:T(8,128)(2,1)} %copy-done.60, bf16[2,16,256,256]{3,2,1,0:T(8,128)(2,1)} %get-tuple-element.241.out_of, ...), custom_call_target="tpu_custom_call" | custom-call | tf_op jit(solution)/shard_map/attend_forward/pallas_call | solution.py:345
  440.4 5.3 collective-permute-done.38
  454.7 5.1 fusion.149
  478.8 6.0 fusion.70
  486.5 10.2 collective-permute-done.42
  515.0 5.8 collective-permute-start.45
  558.7 71.5 %attend_backward.2 = bf16[2,8,256,256]{3,2,1,0:T(8,128)(2,1)} custom-call(s32[2]{0:T(128)} %pad_add_fusion.pos_ref, bf16[8,256,256]{2,1,0:T(8,128)(2,1)} %copy-done.34, bf16[8,256,256]{2,1,0:T(8,128)(2,1)} %copy-done.57, bf16[2,4096,256]{2,1,0:T(8,128)(2,1)} %get-tuple-element.88.sorted_ref, bf16[2,16,256,256]{3,2,1,0:T(8,128)(2,1)} %get-tuple-element.241.out_of, ...), custom_call_target="tpu_custom_call" | custom-call | tf_op jit(solution)/shard_map/attend_backward/pallas_call | solution.py:377
  641.1 22.6 %collective-permute-done.109 = bf16[4,64,2048]{2,1,0:T(8,128)(2,1)S(1)} collective-permute-done((bf16[4,64,2048]{2,1,0:T(8,128)(2,1)S(1)}, bf16[4,64,2048]{2,1,0:T(8,128)(2,1)S(1)}, u32[]{:S(2)}, u32[]{:S(2)}) %collective-permute-start.109) | collective-permute-done | bytes 1048608 | tf_op jit(solution)/shard_map/ppermute | solution.py:23
  671.9 8.7 collective-permute-done.55.refs_4_
  696.2 6.2 collective-permute-start.119
  702.7 18.1 %collective-permute-done.119 = bf16[1,64,2048]{2,1,0:T(8,128)(2,1)S(1)} collective-permute-done((bf16[1,64,2048]{2,1,0:T(8,128)(2,1)S(1)}, bf16[1,64,2048]{2,1,0:T(8,128)(2,1)S(1)}, u32[]{:S(2)}, u32[]{:S(2)}) %collective-permute-start.119) | collective-permute-done | bytes 262176 | tf_op jit(solution)/shard_map/ppermute | solution.py:23
  730.7 8.6 fusion.150
  742.6 5.5 convolution_convert_fusion.1
  773.7 11.4 %collective-permute-done.87 = f32[2,10,512]{2,1,0:T(8,128)S(1)} collective-permute-done((f32[2,10,512]{2,1,0:T(8,128)S(1)}, f32[2,10,512]{2,1,0:T(8,128)S(1)}, u32[]{:S(2)}, u32[]{:S(2)}) %collective-permute-start.87) | collective-permute-done | bytes 40992 | tf_op jit(solution)/shard_map/ppermute | solution.py:23
  852.8 71.2 %attend_backward.3 = bf16[2,8,256,256]{3,2,1,0:T(8,128)(2,1)} custom-call(s32[2]{0:T(128)} %pad_add_fusion.pos_ref, bf16[8,256,256]{2,1,0:T(8,128)(2,1)} %copy-done.35, bf16[8,256,256]{2,1,0:T(8,128)(2,1)} %copy-done.58, bf16[2,4096,256]{2,1,0:T(8,128)(2,1)} %get-tuple-element.98.sorted_ref, bf16[2,16,256,256]{3,2,1,0:T(8,128)(2,1)} %get-tuple-element.241.out_of, ...), custom_call_target="tpu_custom_call" | custom-call | tf_op jit(solution)/shard_map/attend_backward/pallas_call | solution.py:377
  934.7 22.8 %collective-permute-done.105 = bf16[4,64,2048]{2,1,0:T(8,128)(2,1)S(1)} collective-permute-done((bf16[4,64,2048]{2,1,0:T(8,128)(2,1)S(1)}, bf16[4,64,2048]{2,1,0:T(8,128)(2,1)S(1)}, u32[]{:S(2)}, u32[]{:S(2)}) %collective-permute-start.105) | collective-permute-done | bytes 1048608 | tf_op jit(solution)/shard_map/ppermute | solution.py:23
  966.4 7.8 collective-permute-done.73.refs_4_
  988.0 6.3 collective-permute-start.115
  995.1 17.4 %collective-permute-done.115 = bf16[1,64,2048]{2,1,0:T(8,128)(2,1)S(1)} collective-permute-done((bf16[1,64,2048]{2,1,0:T(8,128)(2,1)S(1)}, bf16[1,64,2048]{2,1,0:T(8,128)(2,1)S(1)}, u32[]{:S(2)}, u32[]{:S(2)}) %collective-permute-start.115) | collective-permute-done | bytes 262176 | tf_op jit(solution)/shard_map/ppermute | solution.py:23
  1039.1 5.2 collective-permute-done.89
  1045.9 6.5 collective-permute-done.90
  (823 shorter events, 474.4 us)
Async XLA Ops:
  7.2 68.3 %all-gather.3.cloned.1.call-start = ((), (), s32[]{:S(2)}) async-start(), calls=%async_computation.1 | async-start | bytes 6684672 | tf_op jit(solution)/shard_map/all_gather | solution.py:530
  227.5 29.2 %collective-permute-start.18 = (bf16[512,1024]{1,0:T(8,128)(2,1)}, bf16[512,1024]{1,0:T(8,128)(2,1)S(1)}, u32[]{:S(2)}, u32[]{:S(2)}) collective-permute-start(bf16[512,1024]{1,0:T(8,128)(2,1)} %get-tuple-element.69), channel_id=1, source_target_pairs={{0,1},{1,0},{2,3},{3,2},{4,5},{5,4},{6,7},{7,6},{8,9},{9,8},{10,11... | collective-permute-start | bytes 3145736 | tf_op jit(solution)/shard_map/ppermute | solution.py:23
  267.3 22.7 %collective-permute-start.20 = (bf16[512,1024]{1,0:T(8,128)(2,1)}, bf16[512,1024]{1,0:T(8,128)(2,1)}, u32[]{:S(2)}, u32[]{:S(2)}) collective-permute-start(bf16[512,1024]{1,0:T(8,128)(2,1)} %fusion.64), channel_id=1, source_target_pairs={{0,1},{1,0},{2,3},{3,2},{4,5},{5,4},{6,7},{7,6},{8,9},{9,8},{10,11... | collective-permute-start | bytes 3145736 | tf_op jit(solution)/shard_map/ppermute | solution.py:23
  396.7 28.0 %collective-permute-start.41 = (bf16[512,512]{1,0:T(8,128)(2,1)}, bf16[512,512]{1,0:T(8,128)(2,1)}, u32[]{:S(2)}, u32[]{:S(2)}) collective-permute-start(bf16[512,512]{1,0:T(8,128)(2,1)} %bitcast_convert_fusion.1), channel_id=1, source_target_pairs={{0,1},{1,0},{2,3},{3,2},{4,5},{5,4},{6,7},{7,6},{8,9},{9,8},{10,11... | collective-permute-start | bytes 1572872 | tf_op jit(solution)/shard_map/ppermute | solution.py:23
  423.3 22.5 %collective-permute-start.38 = (bf16[512,1024]{1,0:T(8,128)(2,1)}, bf16[512,1024]{1,0:T(8,128)(2,1)}, u32[]{:S(2)}, u32[]{:S(2)}) collective-permute-start(bf16[512,1024]{1,0:T(8,128)(2,1)} %get-tuple-element.79), channel_id=1, source_target_pairs={{0,1},{1,0},{2,3},{3,2},{4,5},{5,4},{6,7},{7,6},{8,9},{9,8},{10,11... | collective-permute-start | bytes 3145736 | tf_op jit(solution)/shard_map/ppermute | solution.py:23
  471.2 25.6 %collective-permute-start.42 = (bf16[512,1024]{1,0:T(8,128)(2,1)S(1)}, bf16[512,1024]{1,0:T(8,128)(2,1)}, u32[]{:S(2)}, u32[]{:S(2)}) collective-permute-start(bf16[512,1024]{1,0:T(8,128)(2,1)S(1)} %fusion.67), channel_id=1, source_target_pairs={{0,1},{1,0},{2,3},{3,2},{4,5},{5,4},{6,7},{7,6},{8,9},{9,8},{10,11... | collective-permute-start | bytes 3145736 | tf_op jit(solution)/shard_map/ppermute | solution.py:23
  475.8 78.5 %collective-permute-start.116 = (bf16[8,64,2048]{2,1,0:T(8,128)(2,1)}, bf16[8,64,2048]{2,1,0:T(8,128)(2,1)}, u32[]{:S(2)}, u32[]{:S(2)}) collective-permute-start(bf16[8,64,2048]{2,1,0:T(8,128)(2,1)} %dynamic-slice_bitcast_fusion), channel_id=1, source_target_pairs={{0,2},{2,0},{4,6},{6,4},{8,10},{10,8},{12,14},{14,12},{16,18},{18,... | collective-permute-start | bytes 6291464 | tf_op jit(solution)/shard_map/ppermute | solution.py:23
  477.3 154.4 %collective-permute-start.108 = (bf16[8,64,2048]{2,1,0:T(8,128)(2,1)}, bf16[8,64,2048]{2,1,0:T(8,128)(2,1)}, u32[]{:S(2)}, u32[]{:S(2)}) collective-permute-start(bf16[8,64,2048]{2,1,0:T(8,128)(2,1)} %dynamic-slice_bitcast_fusion.2), channel_id=1, source_target_pairs={{0,2},{2,0},{4,6},{6,4},{8,10},{10,8},{12,14},{14,12},{16,18},{18,... | collective-permute-start | bytes 6291464 | tf_op jit(solution)/shard_map/ppermute | solution.py:23
  484.8 30.2 %collective-permute-start.39 = (bf16[512,1024]{1,0:T(8,128)(2,1)}, bf16[512,1024]{1,0:T(8,128)(2,1)}, u32[]{:S(2)}, u32[]{:S(2)}) collective-permute-start(bf16[512,1024]{1,0:T(8,128)(2,1)} %fusion.70), channel_id=1, source_target_pairs={{0,1},{1,0},{2,3},{3,2},{4,5},{5,4},{6,7},{7,6},{8,9},{9,8},{10,11... | collective-permute-start | bytes 3145736 | tf_op jit(solution)/shard_map/ppermute | solution.py:23
  556.8 79.2 %collective-permute-start.117 = (bf16[4,64,2048]{2,1,0:T(8,128)(2,1)S(1)}, bf16[4,64,2048]{2,1,0:T(8,128)(2,1)S(1)}, u32[]{:S(2)}, u32[]{:S(2)}) collective-permute-start(bf16[4,64,2048]{2,1,0:T(8,128)(2,1)S(1)} %dynamic-slice_bitcast_fusion.4), channel_id=1, source_target_pairs={{0,4},{2,6},{4,0},{6,2},{8,12},{10,14},{12,8},{14,10},{16,20},{18,... | collective-permute-start | bytes 3145736 | tf_op jit(solution)/shard_map/ppermute | solution.py:23
  634.8 28.8 %collective-permute-start.109 = (bf16[4,64,2048]{2,1,0:T(8,128)(2,1)S(1)}, bf16[4,64,2048]{2,1,0:T(8,128)(2,1)S(1)}, u32[]{:S(2)}, u32[]{:S(2)}) collective-permute-start(bf16[4,64,2048]{2,1,0:T(8,128)(2,1)S(1)} %dynamic-slice_bitcast_fusion.6), channel_id=1, source_target_pairs={{0,4},{2,6},{4,0},{6,2},{8,12},{10,14},{12,8},{14,10},{16,20},{18,... | collective-permute-start | bytes 3145736 | tf_op jit(solution)/shard_map/ppermute | solution.py:23
  636.5 59.2 %collective-permute-start.118 = (bf16[2,64,2048]{2,1,0:T(8,128)(2,1)S(1)}, bf16[2,64,2048]{2,1,0:T(8,128)(2,1)S(1)}, u32[]{:S(2)}, u32[]{:S(2)}) collective-permute-start(bf16[2,64,2048]{2,1,0:T(8,128)(2,1)S(1)} %dynamic-slice_bitcast_fusion.10), channel_id=1, source_target_pairs={{0,8},{2,10},{4,12},{6,14},{8,0},{10,2},{12,4},{14,6},{16,24},{18,... | collective-permute-start | bytes 1572872 | tf_op jit(solution)/shard_map/ppermute | solution.py:23
  637.6 28.5 %collective-permute-start.52 = (bf16[256,256]{1,0:T(8,128)(2,1)S(1)}, bf16[256,256]{1,0:T(8,128)(2,1)S(1)}, u32[]{:S(2)}, u32[]{:S(2)}) collective-permute-start(bf16[256,256]{1,0:T(8,128)(2,1)S(1)} %get-tuple-element.169), channel_id=1, source_target_pairs={{0,4},{2,6},{4,0},{6,2},{8,12},{10,14},{12,8},{14,10},{16,20},{18,... | collective-permute-start | bytes 393224 | tf_op jit(solution)/shard_map/ppermute | solution.py:23
  638.5 29.1 %collective-permute-start.53 = (bf16[256,256]{1,0:T(8,128)(2,1)S(1)}, bf16[256,256]{1,0:T(8,128)(2,1)S(1)}, u32[]{:S(2)}, u32[]{:S(2)}) collective-permute-start(bf16[256,256]{1,0:T(8,128)(2,1)S(1)} %get-tuple-element.168), channel_id=1, source_target_pairs={{0,8},{2,10},{4,12},{6,14},{8,0},{10,2},{12,4},{14,6},{16,24},{18,... | collective-permute-start | bytes 393224 | tf_op jit(solution)/shard_map/ppermute | solution.py:23
  640.5 28.9 %collective-permute-start.54 = (bf16[256,256]{1,0:T(8,128)(2,1)S(1)}, bf16[256,256]{1,0:T(8,128)(2,1)S(1)}, u32[]{:S(2)}, u32[]{:S(2)}) collective-permute-start(bf16[256,256]{1,0:T(8,128)(2,1)S(1)} %get-tuple-element.167), channel_id=1, source_target_pairs={{0,12},{2,14},{4,8},{6,10},{8,4},{10,6},{12,0},{14,2},{16,28},{18,... | collective-permute-start | bytes 393224 | tf_op jit(solution)/shard_map/ppermute | solution.py:23
  688.7 38.2 %collective-permute-start.59 = (bf16[512,1024]{1,0:T(8,128)(2,1)}, bf16[512,1024]{1,0:T(8,128)(2,1)S(1)}, u32[]{:S(2)}, u32[]{:S(2)}) collective-permute-start(bf16[512,1024]{1,0:T(8,128)(2,1)} %get-tuple-element.89), channel_id=1, source_target_pairs={{0,1},{1,0},{2,3},{3,2},{4,5},{5,4},{6,7},{7,6},{8,9},{9,8},{10,11... | collective-permute-start | bytes 3145736 | tf_op jit(solution)/shard_map/ppermute | solution.py:23
  695.7 52.5 %collective-permute-start.92 = (bf16[8,64,1024]{2,1,0:T(8,128)(2,1)}, bf16[8,64,1024]{2,1,0:T(8,128)(2,1)}, u32[]{:S(2)}, u32[]{:S(2)}) collective-permute-start(bf16[8,64,1024]{2,1,0:T(8,128)(2,1)} %dynamic-slice_bitcast_fusion.8), channel_id=1, source_target_pairs={{0,2},{2,0},{4,6},{6,4},{8,10},{10,8},{12,14},{14,12},{16,18},{18,... | collective-permute-start | bytes 3145736 | tf_op jit(solution)/shard_map/ppermute | solution.py:23
  696.2 24.5 %collective-permute-start.119 = (bf16[1,64,2048]{2,1,0:T(8,128)(2,1)S(1)}, bf16[1,64,2048]{2,1,0:T(8,128)(2,1)S(1)}, u32[]{:S(2)}, u32[]{:S(2)}) collective-permute-start(bf16[1,64,2048]{2,1,0:T(8,128)(2,1)S(1)} %constant_dynamic-slice_fusion), channel_id=1, source_target_pairs={{0,16},{2,18},{4,20},{6,22},{8,24},{10,26},{12,28},{14,30},{16,0},... | collective-permute-start | bytes 786440 | tf_op jit(solution)/shard_map/ppermute | solution.py:23
  702.6 23.4 %collective-permute-start.111 = (bf16[1,64,2048]{2,1,0:T(8,128)(2,1)S(1)}, bf16[1,64,2048]{2,1,0:T(8,128)(2,1)S(1)}, u32[]{:S(2)}, u32[]{:S(2)}) collective-permute-start(bf16[1,64,2048]{2,1,0:T(8,128)(2,1)S(1)} %constant_dynamic-slice_fusion.2), channel_id=1, source_target_pairs={{0,16},{2,18},{4,20},{6,22},{8,24},{10,26},{12,28},{14,30},{16,0},... | collective-permute-start | bytes 786440 | tf_op jit(solution)/shard_map/ppermute | solution.py:23
  759.7 37.9 %collective-permute-start.60 = (bf16[512,1024]{1,0:T(8,128)(2,1)S(1)}, bf16[512,1024]{1,0:T(8,128)(2,1)}, u32[]{:S(2)}, u32[]{:S(2)}) collective-permute-start(bf16[512,1024]{1,0:T(8,128)(2,1)S(1)} %fusion.61), channel_id=1, source_target_pairs={{0,1},{1,0},{2,3},{3,2},{4,5},{5,4},{6,7},{7,6},{8,9},{9,8},{10,11... | collective-permute-start | bytes 3145736 | tf_op jit(solution)/shard_map/ppermute | solution.py:23
  764.5 83.3 %collective-permute-start.112 = (bf16[8,64,2048]{2,1,0:T(8,128)(2,1)}, bf16[8,64,2048]{2,1,0:T(8,128)(2,1)}, u32[]{:S(2)}, u32[]{:S(2)}) collective-permute-start(bf16[8,64,2048]{2,1,0:T(8,128)(2,1)} %dynamic-slice_bitcast_fusion.1), channel_id=1, source_target_pairs={{0,2},{2,0},{4,6},{6,4},{8,10},{10,8},{12,14},{14,12},{16,18},{18,... | collective-permute-start | bytes 6291464 | tf_op jit(solution)/shard_map/ppermute | solution.py:23
  773.7 151.7 %collective-permute-start.104 = (bf16[8,64,2048]{2,1,0:T(8,128)(2,1)}, bf16[8,64,2048]{2,1,0:T(8,128)(2,1)}, u32[]{:S(2)}, u32[]{:S(2)}) collective-permute-start(bf16[8,64,2048]{2,1,0:T(8,128)(2,1)} %dynamic-slice_bitcast_fusion.3), channel_id=1, source_target_pairs={{0,2},{2,0},{4,6},{6,4},{8,10},{10,8},{12,14},{14,12},{16,18},{18,... | collective-permute-start | bytes 6291464 | tf_op jit(solution)/shard_map/ppermute | solution.py:23
  850.2 78.9 %collective-permute-start.113 = (bf16[4,64,2048]{2,1,0:T(8,128)(2,1)S(1)}, bf16[4,64,2048]{2,1,0:T(8,128)(2,1)S(1)}, u32[]{:S(2)}, u32[]{:S(2)}) collective-permute-start(bf16[4,64,2048]{2,1,0:T(8,128)(2,1)S(1)} %dynamic-slice_bitcast_fusion.5), channel_id=1, source_target_pairs={{0,4},{2,6},{4,0},{6,2},{8,12},{10,14},{12,8},{14,10},{16,20},{18,... | collective-permute-start | bytes 3145736 | tf_op jit(solution)/shard_map/ppermute | solution.py:23
  928.6 28.8 %collective-permute-start.105 = (bf16[4,64,2048]{2,1,0:T(8,128)(2,1)S(1)}, bf16[4,64,2048]{2,1,0:T(8,128)(2,1)S(1)}, u32[]{:S(2)}, u32[]{:S(2)}) collective-permute-start(bf16[4,64,2048]{2,1,0:T(8,128)(2,1)S(1)} %dynamic-slice_bitcast_fusion.7), channel_id=1, source_target_pairs={{0,4},{2,6},{4,0},{6,2},{8,12},{10,14},{12,8},{14,10},{16,20},{18,... | collective-permute-start | bytes 3145736 | tf_op jit(solution)/shard_map/ppermute | solution.py:23
  929.6 57.7 %collective-permute-start.114 = (bf16[2,64,2048]{2,1,0:T(8,128)(2,1)S(1)}, bf16[2,64,2048]{2,1,0:T(8,128)(2,1)S(1)}, u32[]{:S(2)}, u32[]{:S(2)}) collective-permute-start(bf16[2,64,2048]{2,1,0:T(8,128)(2,1)S(1)} %dynamic-slice_bitcast_fusion.11), channel_id=1, source_target_pairs={{0,8},{2,10},{4,12},{6,14},{8,0},{10,2},{12,4},{14,6},{16,24},{18,... | collective-permute-start | bytes 1572872 | tf_op jit(solution)/shard_map/ppermute | solution.py:23
  931.2 28.6 %collective-permute-start.70 = (bf16[256,256]{1,0:T(8,128)(2,1)S(1)}, bf16[256,256]{1,0:T(8,128)(2,1)S(1)}, u32[]{:S(2)}, u32[]{:S(2)}) collective-permute-start(bf16[256,256]{1,0:T(8,128)(2,1)S(1)} %get-tuple-element.161), channel_id=1, source_target_pairs={{0,4},{2,6},{4,0},{6,2},{8,12},{10,14},{12,8},{14,10},{16,20},{18,... | collective-permute-start | bytes 393224 | tf_op jit(solution)/shard_map/ppermute | solution.py:23
  932.3 28.5 %collective-permute-start.71 = (bf16[256,256]{1,0:T(8,128)(2,1)S(1)}, bf16[256,256]{1,0:T(8,128)(2,1)S(1)}, u32[]{:S(2)}, u32[]{:S(2)}) collective-permute-start(bf16[256,256]{1,0:T(8,128)(2,1)S(1)} %get-tuple-element.160), channel_id=1, source_target_pairs={{0,8},{2,10},{4,12},{6,14},{8,0},{10,2},{12,4},{14,6},{16,24},{18,... | collective-permute-start | bytes 393224 | tf_op jit(solution)/shard_map/ppermute | solution.py:23
  934.3 29.1 %collective-permute-start.72 = (bf16[256,256]{1,0:T(8,128)(2,1)S(1)}, bf16[256,256]{1,0:T(8,128)(2,1)S(1)}, u32[]{:S(2)}, u32[]{:S(2)}) collective-permute-start(bf16[256,256]{1,0:T(8,128)(2,1)S(1)} %get-tuple-element.159), channel_id=1, source_target_pairs={{0,12},{2,14},{4,8},{6,10},{8,4},{10,6},{12,0},{14,2},{16,28},{18,... | collective-permute-start | bytes 393224 | tf_op jit(solution)/shard_map/ppermute | solution.py:23
  982.5 30.9 %collective-permute-start.77 = (bf16[512,1024]{1,0:T(8,128)(2,1)}, bf16[512,1024]{1,0:T(8,128)(2,1)S(1)}, u32[]{:S(2)}, u32[]{:S(2)}) collective-permute-start(bf16[512,1024]{1,0:T(8,128)(2,1)} %get-tuple-element.99), channel_id=1, source_target_pairs={{0,1},{1,0},{2,3},{3,2},{4,5},{5,4},{6,7},{7,6},{8,9},{9,8},{10,11... | collective-permute-start | bytes 3145736 | tf_op jit(solution)/shard_map/ppermute | solution.py:23
  987.3 40.8 %collective-permute-start.88 = (bf16[8,64,1024]{2,1,0:T(8,128)(2,1)}, bf16[8,64,1024]{2,1,0:T(8,128)(2,1)}, u32[]{:S(2)}, u32[]{:S(2)}) collective-permute-start(bf16[8,64,1024]{2,1,0:T(8,128)(2,1)} %dynamic-slice_bitcast_fusion.9), channel_id=1, source_target_pairs={{0,2},{2,0},{4,6},{6,4},{8,10},{10,8},{12,14},{14,12},{16,18},{18,... | collective-permute-start | bytes 3145736 | tf_op jit(solution)/shard_map/ppermute | solution.py:23
  988.0 24.6 %collective-permute-start.115 = (bf16[1,64,2048]{2,1,0:T(8,128)(2,1)S(1)}, bf16[1,64,2048]{2,1,0:T(8,128)(2,1)S(1)}, u32[]{:S(2)}, u32[]{:S(2)}) collective-permute-start(bf16[1,64,2048]{2,1,0:T(8,128)(2,1)S(1)} %constant_dynamic-slice_fusion.1), channel_id=1, source_target_pairs={{0,16},{2,18},{4,20},{6,22},{8,24},{10,26},{12,28},{14,30},{16,0},... | collective-permute-start | bytes 786440 | tf_op jit(solution)/shard_map/ppermute | solution.py:23
  995.1 22.6 %collective-permute-start.107 = (bf16[1,64,2048]{2,1,0:T(8,128)(2,1)}, bf16[1,64,2048]{2,1,0:T(8,128)(2,1)}, u32[]{:S(2)}, u32[]{:S(2)}) collective-permute-start(bf16[1,64,2048]{2,1,0:T(8,128)(2,1)} %constant_dynamic-slice_fusion.3), channel_id=1, source_target_pairs={{0,16},{2,18},{4,20},{6,22},{8,24},{10,26},{12,28},{14,30},{16,0},... | collective-permute-start | bytes 786440 | tf_op jit(solution)/shard_map/ppermute | solution.py:23
  (249 other events, 3361.5 us)
Sparse Core Ops, SparseCore 0:
  10.9 64.5 all-gather.2

commit v2 on v1

v2 whole, which is shorter than its diff:
```python
import functools

import jax
import jax.numpy as jnp
from jax import lax
from jax.experimental import pallas as pl
from jax.experimental.pallas import tpu as pltpu
from jax.sharding import PartitionSpec as P

HD = 128
GROUP = 64
ROUNDS = 4
LAYERS = 2
BLOCK = 256
F32 = jnp.float32
BF16 = jnp.bfloat16
SCALE = HD ** (-0.5)
VMEM_LIMIT = 56 * 1024 * 1024
PAIRS = 8
CHUNKS = 2
FFN_STEPS = 4


def swap(value, axis, mask):
    count = lax.axis_size(axis)
    return lax.ppermute(value, axis, [(source, source ^ mask) for source in range(count)])


def dot(left, right, dims):
    return lax.dot_general(left, right, (dims, ((), ())), preferred_element_type=F32)


def mm(left, right):
    return dot(left, right, ((1,), (0,)))


def mm_t(left, right):
    return dot(left, right, ((1,), (1,)))


def t_mm(left, right):
    return dot(left, right, ((0,), (0,)))


def chip_exchange(units):
    count = lax.axis_size("wide")
    groups = [list(range(core, count, 2)) for core in range(2)]
    return lax.all_to_all(units, "wide", 0, 0, tiled=True, axis_index_groups=groups)


def split3(value):
    high = value.astype(BF16)
    rest = value - high.astype(F32)
    mid = rest.astype(BF16)
    low = (rest - mid.astype(F32)).astype(BF16)
    return high.astype(F32), mid.astype(F32), low.astype(F32)


def layer_norm(stream, gain, shift):
    centre = stream - jnp.mean(stream, axis=-1, keepdims=True)
    spread = jnp.mean(centre * centre, axis=-1, keepdims=True)
    return centre * lax.rsqrt(spread + 1e-05) * gain + shift


def layer_norm_back(stream, gain, grad):
    centre = stream - jnp.mean(stream, axis=-1, keepdims=True)
    inv = lax.rsqrt(jnp.mean(centre * centre, axis=-1, keepdims=True) + 1e-05)
    unit = centre * inv
    scaled = grad * gain
    back = inv * (
        scaled
        - jnp.mean(scaled, axis=-1, keepdims=True)
        - unit * jnp.mean(scaled * unit, axis=-1, keepdims=True)
    )
    return back, unit


def build_tables(tokens):
    rounds, seq = tokens.shape
    blocks = seq // BLOCK
    rank_rows = BLOCK // blocks
    tokens = tokens.reshape(rounds, blocks, BLOCK)
    run = tokens // BLOCK
    row = tokens % BLOCK
    onehot = (run[..., None] == jnp.arange(blocks, dtype=jnp.int32)).astype(BF16)
    before = (jnp.arange(BLOCK)[:, None] > jnp.arange(BLOCK)[None, :]).astype(BF16)
    counts = jnp.einsum("jl,rkla->rkja", before, onehot, preferred_element_type=F32)
    rank = jnp.sum(onehot.astype(F32) * counts, axis=-1).astype(jnp.int32)
    slot = run * rank_rows + rank
    iota = jnp.arange(BLOCK, dtype=jnp.int32)
    into = (slot[..., None] == iota).astype(BF16)
    into_t = (slot[..., None, :] == iota[:, None]).astype(BF16)
    wants = jnp.einsum("rknj,rkj->rkn", into_t, row.astype(BF16), preferred_element_type=F32)
    wants = wants.reshape(rounds, blocks, blocks, rank_rows)
    wants = jnp.transpose(wants, (0, 2, 1, 3)).reshape(rounds, blocks, BLOCK).astype(jnp.int32)
    out_of = (wants[..., None] == iota).astype(BF16)
    out_of_t = (wants[..., None, :] == iota[:, None]).astype(BF16)
    return jnp.transpose(out_of, (1, 0, 2, 3)), into, out_of_t, into_t


def token_copies(pos_ref, sources, tok, sems):
    core = pos_ref[0]
    chunks = len(sources) // 2
    slots, rows, _ = sources[0].shape
    copies = []
    for place, source in enumerate(sources):
        chunk, half = place // 2, place % 2
        for k in range(slots):
            device = 2 * k + (core ^ half)
            start = pl.multiple_of((device * chunks + chunk) * rows, rows)
            copies.append(
                pltpu.make_async_copy(
                    source.at[k], tok.at[pl.ds(start, rows)], sems.at[len(copies)]
                )
            )
    return copies


def table_copies(sources, targets, sems):
    return [
        pltpu.make_async_copy(source, target, sems.at[k])
        for k, (source, target) in enumerate(zip(sources, targets))
    ]


def store_run(pos_ref, buffer, run, value):
    core = pos_ref[0]
    _, chunks, _, rows, _ = buffer.shape
    for part in range(BLOCK // rows):
        device = run * (BLOCK // (rows * chunks)) + part // chunks
        buffer[(device & 1) ^ core, part % chunks, device >> 1] = value[
            part * rows : (part + 1) * rows
        ]


def send_halves(buffer, own_hbm, sib_hbm, sems):
    copies = [
        pltpu.make_async_copy(buffer.at[1], sib_hbm, sems.at[0]),
        pltpu.make_async_copy(buffer.at[0], own_hbm, sems.at[1]),
    ]
    for copy in copies:
        copy.start()
    for copy in copies:
        copy.wait()


def spread(first, count, width):
    row = lax.broadcasted_iota(jnp.int32, (HD, width), 0)
    return jnp.where((row >= first) & (row < first + count), 1.0, 0.0).astype(BF16)


def pack_stats(columns):
    lane = lax.broadcasted_iota(jnp.int32, columns[0].shape, 1)
    extra = jnp.zeros(columns[0].shape, F32)
    for place, column in enumerate(columns):
        extra = jnp.where(lane == place, column, extra)
    return extra


def permute_in(tok, out_of, mixed, blocks):
    rank = BLOCK // blocks
    for a in range(blocks):
        source = tok[a * BLOCK : (a + 1) * BLOCK, :]
        moved = mm(out_of[a].reshape(2 * BLOCK, BLOCK), source).astype(BF16)
        for r in range(2):
            mixed[r, :, a] = moved[r * BLOCK : (r + 1) * BLOCK].reshape(blocks, rank, 2 * HD)


def split_rows(tile):
    lane = lax.broadcasted_iota(jnp.int32, tile.shape, 1)
    zero = jnp.zeros_like(tile)
    return jnp.concatenate(
        [jnp.where(lane < GROUP, tile, zero), jnp.where(lane >= GROUP, tile, zero)], axis=0
    )


def split_lanes(tile):
    row = lax.broadcasted_iota(jnp.int32, tile.shape, 0)
    zero = jnp.zeros_like(tile)
    return jnp.concatenate(
        [jnp.where(row < GROUP, tile, zero), jnp.where(row >= GROUP, tile, zero)], axis=1
    )


def side_by_side(ref, base):
    return jnp.concatenate(
        [ref[base : base + 2 * GROUP, :], ref[base + GROUP : base + 3 * GROUP, :]], axis=1
    )


def one_above(ref, base):
    return jnp.concatenate(
        [ref[base : base + 2 * GROUP, :], ref[base + GROUP : base + 3 * GROUP, :]], axis=0
    )


def self_mask():
    row = lax.broadcasted_iota(jnp.int32, (2 * GROUP, 2 * GROUP), 0)
    lane = lax.broadcasted_iota(jnp.int32, (2 * GROUP, 2 * GROUP), 1)
    return row == lane % GROUP + GROUP


def unit_keys(query):
    return query * lax.rsqrt(jnp.mean(query * query, axis=-1, keepdims=True) + 1e-06)


def forward_kernel(chunks, extras, pos_ref, *refs):
    sources, refs = refs[: 2 * chunks], refs[2 * chunks + extras :]
    (
        out_of_hbm, into_hbm, out_of_t_hbm, into_t_hbm, sorted_hbm, own_hbm, sib_hbm,
        tok, mixed, keys, vals, placed, buffer, out_of, into, out_of_t, into_t,
        tok_sems, table_sems, out_sems, send_sems,
    ) = refs
    seq = tok.shape[0]
    blocks = seq // BLOCK
    rank = BLOCK // blocks
    loads = token_copies(pos_ref, sources, tok, tok_sems)
    tables = table_copies(
        (out_of_hbm, into_hbm, into_t_hbm, out_of_t_hbm), (out_of, into, into_t, out_of_t), table_sems
    )
    for copy in loads:
        copy.start()
    for copy in tables:
        copy.start()
    for copy in loads:
        copy.wait()
    tables[0].wait()
    permute_in(tok, out_of, mixed, blocks)
    tables[1].wait()
    outs = []
    for r in range(2):
        for k in range(blocks):
            base = k * BLOCK
            rows_sorted = mm(into[r, k], mixed[r, k].reshape(BLOCK, 2 * HD))
            placed[r, base : base + BLOCK, :] = rows_sorted.astype(BF16)
            where = slice(base + GROUP, base + GROUP + BLOCK)
            keys[r, where, :] = unit_keys(rows_sorted[:, :HD]).astype(BF16)
            vals[r, where, :] = rows_sorted[:, HD:].astype(BF16)
        keys[r, 0:GROUP, :] = keys[r, seq : seq + GROUP, :]
        vals[r, 0:GROUP, :] = vals[r, seq : seq + GROUP, :]
        outs.append(pltpu.make_async_copy(placed.at[r], sorted_hbm.at[r], out_sems.at[r]))
        outs[-1].start()
    tables[2].wait()
    own = jnp.concatenate([self_mask()] * PAIRS, axis=1)
    wide = PAIRS * 2 * GROUP
    for r in range(2):
        for first in range(0, seq, wide):
            bases = [first + p * 2 * GROUP for p in range(PAIRS)]
            flipped = [placed[r, base : base + 2 * GROUP, 0:HD].T for base in bases]
            raw = jnp.concatenate(
                [
                    mm(side_by_side(keys.at[r], base), split_rows(tile))
                    for base, tile in zip(bases, flipped)
                ],
                axis=1,
            )
            scores = jnp.where(own, -1000000000.0, raw * SCALE)
            top = jnp.max(scores, axis=0, keepdims=True)
            weight = jnp.exp(scores - top)
            total = jnp.sum(weight, axis=0, keepdims=True)
            probs = (weight * (1.0 / total)).astype(BF16)
            row = lax.broadcasted_iota(jnp.int32, (8, wide), 0)
            stats = jnp.zeros((8, wide), F32)
            for place, part in enumerate(split3(top + jnp.log(total))):
                stats = jnp.where(row == place, part, stats)
            stats = jnp.concatenate([stats, jnp.zeros((HD - 8, wide), F32)], axis=0)
            lanes = [slice(p * 2 * GROUP, (p + 1) * 2 * GROUP) for p in range(PAIRS)]
            turned = [probs[:, lane].T for lane in lanes]
            extra = [stats[:, lane].T.astype(BF16) for lane in lanes]
            result = [
                mm(split_lanes(tile), one_above(vals.at[r], base)).astype(BF16)
                for tile, base in zip(turned, bases)
            ]
            packed = jnp.concatenate(
                [jnp.concatenate(pair, axis=1) for pair in zip(result, extra)], axis=0
            )
            for part in range(wide // BLOCK):
                k = first // BLOCK + part
                back = mm(into_t[r, k], packed[part * BLOCK : (part + 1) * BLOCK]).astype(BF16)
                mixed[r, k] = back.reshape(blocks, rank, 2 * HD)
    tables[3].wait()
    zero = jnp.zeros((HD, HD), BF16)
    ones = spread(0, 3, HD)
    ones = jnp.concatenate(
        [jnp.concatenate([ones, zero], axis=1), jnp.concatenate([zero, ones], axis=1)], axis=0
    )
    for a in range(blocks):
        moved = [mm(out_of_t[r, a], mixed[r, :, a].reshape(BLOCK, 2 * HD)) for r in range(2)]
        lse = mm(jnp.concatenate([m[:, HD:] for m in moved], axis=1).astype(BF16), ones)
        lse_a, lse_b = lse[:, :HD], lse[:, HD:]
        top = jnp.maximum(lse_a, lse_b)
        weight_a, weight_b = jnp.exp(lse_a - top), jnp.exp(lse_b - top)
        total = weight_a + weight_b
        value = (moved[0][:, :HD] * weight_a + moved[1][:, :HD] * weight_b) * (1.0 / total)
        extra = pack_stats(split3(top + jnp.log(total)))
        store_run(pos_ref, buffer, a, jnp.concatenate([value, extra], axis=1).astype(BF16))
    send_halves(buffer, own_hbm, sib_hbm, send_sems)
    for copy in outs:
        copy.wait()


def backward_kernel(chunks, extras, pos_ref, *refs):
    sources, refs = refs[: 2 * chunks], refs[2 * chunks + extras :]
    (
        sorted_hbm, out_of_hbm, into_hbm, out_of_t_hbm, into_t_hbm, own_hbm, sib_hbm,
        tok, mixed, keys, vals, placed, grads, query_use, key_grad, val_grad, buffer,
        out_of, into, out_of_t, into_t, tok_sems, table_sems, in_sems, send_sems,
    ) = refs
    seq = tok.shape[0]
    blocks = seq // BLOCK
    rank = BLOCK // blocks
    loads = token_copies(pos_ref, sources, tok, tok_sems)
    tables = table_copies(
        (out_of_hbm, into_hbm, into_t_hbm, out_of_t_hbm), (out_of, into, into_t, out_of_t), table_sems
    )
    sorted_in = pltpu.make_async_copy(sorted_hbm, placed, in_sems.at[0])
    for copy in loads:
        copy.start()
    tables[0].start()
    sorted_in.start()
    for copy in tables[1:]:
        copy.start()
    for copy in loads:
        copy.wait()
    tables[0].wait()
    permute_in(tok, out_of, mixed, blocks)
    sorted_in.wait()
    tables[1].wait()
    for r in range(2):
        for k in range(blocks):
            here = slice(k * BLOCK, (k + 1) * BLOCK)
            where = slice(k * BLOCK + GROUP, (k + 1) * BLOCK + GROUP)
            grads[r, here, :] = mm(into[r, k], mixed[r, k].reshape(BLOCK, 2 * HD)).astype(BF16)
            keys[r, where, :] = unit_keys(placed[r, here, 0:HD].astype(F32)).astype(BF16)
            vals[r, where, :] = placed[r, here, HD:]
        keys[r, 0:GROUP, :] = keys[r, seq : seq + GROUP, :]
        vals[r, 0:GROUP, :] = vals[r, seq : seq + GROUP, :]
        key_grad[r, 0:GROUP, :] = jnp.zeros((GROUP, HD), F32)
        val_grad[r, 0:GROUP, :] = jnp.zeros((GROUP, HD), F32)
    own = jnp.concatenate([self_mask()] * PAIRS, axis=1)
    wide = PAIRS * 2 * GROUP
    lanes = [slice(p * 2 * GROUP, (p + 1) * 2 * GROUP) for p in range(PAIRS)]
    for r in range(2):
        for first in range(0, seq, wide):
            bases = [first + p * 2 * GROUP for p in range(PAIRS)]
            query = [placed[r, base : base + 2 * GROUP, 0:HD] for base in bases]
            grad = [grads[r, base : base + 2 * GROUP, 0:HD] for base in bases]
            stats = jnp.concatenate(
                [
                    grads[r, base : base + 2 * GROUP, HD:].astype(F32).T[0:8] for base in bases
                ],
                axis=1,
            )
            delta = stats[0:1] + stats[1:2] + stats[2:3]
            lse = stats[3:4] + stats[4:5] + stats[5:6]
            query_t = [split_rows(tile.T) for tile in query]
            grad_t = [split_rows(tile.T) for tile in grad]
            raw = jnp.concatenate(
                [mm(side_by_side(keys.at[r], base), tile) for base, tile in zip(bases, query_t)],
                axis=1,
            )
            prob_grad = jnp.concatenate(
                [mm(side_by_side(vals.at[r], base), tile) for base, tile in zip(bases, grad_t)],
                axis=1,
            )
            probs = jnp.exp(jnp.where(own, -1000000000.0, raw * SCALE) - lse)
            score_grad = (probs * (prob_grad - delta)).astype(BF16)
            probs = probs.astype(BF16)
            turned = [score_grad[:, lane].T for lane in lanes]
            for tile, base in zip(turned, bases):
                query_use[r, base : base + 2 * GROUP, :] = (
                    mm(split_lanes(tile), one_above(keys.at[r], base)) * SCALE
                )
            key_parts = [
                mm(split_rows(score_grad[:, lane]), tile) * SCALE for lane, tile in zip(lanes, query)
            ]
            val_parts = [mm(split_rows(probs[:, lane]), tile) for lane, tile in zip(lanes, grad)]
            for target, parts in ((key_grad, key_parts), (val_grad, val_parts)):
                target[r, first : first + GROUP, :] += parts[0][:GROUP]
                for p, (part, base) in enumerate(zip(parts, bases)):
                    target[r, base + GROUP : base + 2 * GROUP, :] = (
                        part[GROUP : 2 * GROUP] + part[2 * GROUP : 3 * GROUP]
                    )
                    last = part[3 * GROUP :]
                    if p + 1 < PAIRS:
                        last = last + parts[p + 1][:GROUP]
                    target[r, base + 2 * GROUP : base + 3 * GROUP, :] = last
        key_grad[r, seq : seq + GROUP, :] += key_grad[r, 0:GROUP, :]
        val_grad[r, seq : seq + GROUP, :] += val_grad[r, 0:GROUP, :]
    tables[2].wait()
    for r in range(2):
        for k in range(blocks):
            here = slice(k * BLOCK, (k + 1) * BLOCK)
            where = slice(k * BLOCK + GROUP, (k + 1) * BLOCK + GROUP)
            query = placed[r, here, 0:HD].astype(F32)
            inv = lax.rsqrt(jnp.mean(query * query, axis=-1, keepdims=True) + 1e-06)
            grad = key_grad[r, where, :]
            inner = jnp.mean(grad * query, axis=-1, keepdims=True)
            total = query_use[r, here, :] + inv * (grad - query * (inner * inv * inv))
            packed = jnp.concatenate([total, val_grad[r, where, :]], axis=1).astype(BF16)
            back = mm(into_t[r, k], packed).astype(BF16)
            mixed[r, k] = back.reshape(blocks, rank, 2 * HD)
    tables[3].wait()
    for a in range(blocks):
        total = mm(out_of_t[0, a], mixed[0, :, a].reshape(BLOCK, 2 * HD)) + mm(
            out_of_t[1, a], mixed[1, :, a].reshape(BLOCK, 2 * HD)
        )
        store_run(pos_ref, buffer, a, total.astype(BF16))
    send_halves(buffer, own_hbm, sib_hbm, send_sems)


def params():
    return pltpu.CompilerParams(vmem_limit_bytes=VMEM_LIMIT)


def cost(flops, moved):
    return pl.CostEstimate(flops=int(flops), bytes_accessed=int(moved), transcendentals=0)


IN_SMEM = pl.BlockSpec(memory_space=pltpu.SMEM)
IN_VMEM = pl.BlockSpec(memory_space=pltpu.VMEM)
ANYWHERE = pl.BlockSpec(memory_space=pl.ANY)


def bf16_out(*shape):
    return jax.ShapeDtypeStruct(shape, BF16)


def f32_out(*shape):
    return jax.ShapeDtypeStruct(shape, F32)


def table_scratch(blocks):
    return [
        pltpu.VMEM((blocks, 2, BLOCK, BLOCK), BF16),
        pltpu.VMEM((2, blocks, BLOCK, BLOCK), BF16),
        pltpu.VMEM((2, blocks, BLOCK, BLOCK), BF16),
        pltpu.VMEM((2, blocks, BLOCK, BLOCK), BF16),
    ]


def attention_forward(pos, sources, tables, after):
    chunks = len(sources) // 2
    slots, rows, width = sources[0].shape
    seq = 2 * slots * rows * chunks
    blocks = seq // BLOCK
    half = bf16_out(chunks, slots, rows, width)
    return pl.pallas_call(
        functools.partial(forward_kernel, chunks, len(after)),
        out_shape=(bf16_out(2, seq, width), half, half),
        in_specs=[IN_SMEM] + [ANYWHERE] * (2 * chunks + len(after) + 4),
        out_specs=(ANYWHERE, ANYWHERE, ANYWHERE),
        scratch_shapes=[
            pltpu.VMEM((seq, width), BF16),
            pltpu.VMEM((2, blocks, blocks, BLOCK // blocks, width), BF16),
            pltpu.VMEM((2, seq + GROUP, HD), BF16),
            pltpu.VMEM((2, seq + GROUP, HD), BF16),
            pltpu.VMEM((2, seq, width), BF16),
            pltpu.VMEM((2, chunks, slots, rows, width), BF16),
            *table_scratch(blocks),
            pltpu.SemaphoreType.DMA((2 * slots * chunks,)),
            pltpu.SemaphoreType.DMA((4,)),
            pltpu.SemaphoreType.DMA((2,)),
            pltpu.SemaphoreType.DMA((2,)),
        ],
        compiler_params=params(),
        cost_estimate=cost(16e9, 24e6),
        name="attend_forward",
    )(pos, *sources, *after, *tables)


def attention_backward(pos, sources, sorted_rows, tables, after):
    chunks = len(sources) // 2
    slots, rows, width = sources[0].shape
    seq = 2 * slots * rows * chunks
    blocks = seq // BLOCK
    half = bf16_out(chunks, slots, rows, width)
    return pl.pallas_call(
        functools.partial(backward_kernel, chunks, len(after)),
        out_shape=(half, half),
        in_specs=[IN_SMEM] + [ANYWHERE] * (2 * chunks + len(after) + 5),
        out_specs=(ANYWHERE, ANYWHERE),
        scratch_shapes=[
            pltpu.VMEM((seq, width), BF16),
            pltpu.VMEM((2, blocks, blocks, BLOCK // blocks, width), BF16),
            pltpu.VMEM((2, seq + GROUP, HD), BF16),
            pltpu.VMEM((2, seq + GROUP, HD), BF16),
            pltpu.VMEM((2, seq, width), BF16),
            pltpu.VMEM((2, seq, width), BF16),
            pltpu.VMEM((2, seq, HD), F32),
            pltpu.VMEM((2, seq + GROUP, HD), F32),
            pltpu.VMEM((2, seq + GROUP, HD), F32),
            pltpu.VMEM((2, chunks, slots, rows, width), BF16),
            *table_scratch(blocks),
            pltpu.SemaphoreType.DMA((2 * slots * chunks,)),
            pltpu.SemaphoreType.DMA((4,)),
            pltpu.SemaphoreType.DMA((1,)),
            pltpu.SemaphoreType.DMA((2,)),
        ],
        compiler_params=params(),
        cost_estimate=cost(18e9, 26e6),
        name="attend_backward",
    )(pos, *sources, *after, sorted_rows, *tables)


def unit_slices(seqs, heads, rows, width):
    return [
        (slice(seq * rows, (seq + 1) * rows), slice(head * width, (head + 1) * width))
        for seq in range(seqs)
        for head in range(heads)
    ]


def column_block(rows, width, place):
    return pl.BlockSpec((rows, width), lambda i: (0, place))


def whole_block(array):
    return pl.BlockSpec(array.shape, lambda i: (0,) * len(array.shape))


def pack_kernel(count, *refs):
    out_ref = refs[-1]
    start = 0
    for ref in refs[:count]:
        out_ref[:, start : start + ref.shape[1]] = ref[...]
        start += ref.shape[1]


def pack_columns(pieces, after):
    rows, columns = pieces[0].shape[0], sum(piece.shape[1] for piece in pieces)
    return pl.pallas_call(
        functools.partial(pack_kernel, len(pieces)),
        out_shape=bf16_out(rows, columns),
        in_specs=[IN_VMEM] * len(pieces) + [ANYWHERE] * len(after),
        out_specs=IN_VMEM,
        compiler_params=params(),
        name="pack_columns",
    )(*pieces, *after)


def lower_kernel(count, *refs):
    for source, target in zip(refs[:count], refs[-count:]):
        target[...] = source[...].astype(BF16)


def lower_arrays(arrays, after):
    return pl.pallas_call(
        functools.partial(lower_kernel, len(arrays)),
        out_shape=[bf16_out(*array.shape) for array in arrays],
        in_specs=[IN_VMEM] * len(arrays) + [ANYWHERE] * len(after),
        out_specs=[IN_VMEM] * len(arrays),
        compiler_params=params(),
        name="lower_arrays",
    )(*arrays, *after)


def widen_kernel(pos_ref, mine_ref, other_ref, *out_refs):
    seqs, rows, half = mine_ref.shape
    count = rows // len(out_refs)
    mine_at = pl.ds(pl.multiple_of(pos_ref[1] * half, half), half)
    other_at = pl.ds(pl.multiple_of((1 - pos_ref[1]) * half, half), half)
    for q, out_ref in enumerate(out_refs):
        for seq in range(seqs):
            at = slice(seq * count, (seq + 1) * count)
            source = slice(q * count, (q + 1) * count)
            out_ref[at, mine_at] = mine_ref[seq, source]
            out_ref[at, other_at] = other_ref[seq, source].astype(F32)


def widen_chunks(pos, mine, other):
    seqs, rows, half = mine.shape
    out = f32_out(seqs * rows // CHUNKS, 2 * half)
    return list(
        pl.pallas_call(
            widen_kernel,
            out_shape=[out] * CHUNKS,
            in_specs=[IN_SMEM, IN_VMEM, IN_VMEM],
            out_specs=[IN_VMEM] * CHUNKS,
            compiler_params=params(),
            cost_estimate=cost(1e6, 4e6),
            name="widen_chunks",
        )(pos, mine, other)
    )


def narrow_kernel(layer, pos_ref, *refs):
    refs, out_ref = refs[:-1], refs[-1]
    seqs, rows, half = out_ref.shape
    count = rows // CHUNKS
    lanes = pl.ds(pl.multiple_of(pos_ref[1] * half, half), half)
    for q in range(CHUNKS):
        for seq in range(seqs):
            at = slice(seq * count, (seq + 1) * count)
            value = refs[q][at, lanes]
            if layer is not None:
                own, other = refs[CHUNKS + 2 * q : CHUNKS + 2 * q + 2]
                value = value + (own[at, lanes].astype(F32) + other[at, lanes].astype(F32))
                value = value + refs[-1][layer : layer + 1, lanes]
            out_ref[seq, q * count : (q + 1) * count] = value


def narrow_chunks(pos, chunks, seqs, layer=None, parts=()):
    toks, width = chunks[0].shape
    return pl.pallas_call(
        functools.partial(narrow_kernel, layer),
        out_shape=f32_out(seqs, toks * CHUNKS // seqs, width // 2),
        in_specs=[IN_SMEM] + [IN_VMEM] * (CHUNKS + len(parts)),
        out_specs=IN_VMEM,
        compiler_params=params(),
        cost_estimate=cost(1e6, 4e6),
        name="narrow_chunks",
    )(pos, *chunks, *parts)


def enter_kernel(
    seqs, layer, parts, after, stream_ref, gain_ref, shift_ref, weight_ref, *refs
):
    stream = stream_ref[...]
    if parts:
        own_ref, other_ref, bias_ref, *refs = refs
        stream = stream + (own_ref[...].astype(F32) + other_ref[...].astype(F32))
        stream = stream + bias_ref[layer - 1 : layer]
    refs = refs[after:]
    if parts:
        refs[0][...] = stream
    normed_ref, out_ref = refs[-2:]
    row = slice(layer, layer + 1)
    normed = layer_norm(stream, gain_ref[row], shift_ref[row]).astype(BF16)
    normed_ref[...] = normed
    flat = mm(normed, weight_ref[...]).astype(BF16)
    slots, rows, width = out_ref.shape
    for k, at in enumerate(unit_slices(seqs, slots // seqs, rows, width)):
        out_ref[k] = flat[at]


def enter_attention(seqs, layer, stream, gain, shift, weight, place, columns, parts=(), after=()):
    toks, width = stream.shape
    slots = seqs * columns // (2 * HD)
    shapes = [bf16_out(toks, width), bf16_out(slots, toks // seqs, 2 * HD)]
    if parts:
        shapes = [f32_out(toks, width)] + shapes
    results = pl.pallas_call(
        functools.partial(enter_kernel, seqs, layer, len(parts) > 0, len(after)),
        grid=(1,),
        out_shape=shapes,
        in_specs=[whole_block(stream), whole_block(gain), whole_block(shift)]
        + [column_block(width, columns, place)]
        + [whole_block(part) for part in parts]
        + [ANYWHERE] * len(after),
        out_specs=[whole_block(shape) for shape in shapes],
        compiler_params=params(),
        cost_estimate=cost(2 * toks * width * columns, 5e6),
        name="enter_attention",
    )(stream, gain, shift, weight, *parts, *after)
    return results if parts else (stream, *results)


def merge_kernel(seqs, weight_ref, in_ref, *refs):
    part_ref, tok_ref = refs[-2:]
    slots, rows, width = in_ref.shape
    for k, at in enumerate(unit_slices(seqs, slots // seqs, rows, width)):
        tok_ref[at] = in_ref[k]
    part_ref[...] = mm_t(tok_ref[...], weight_ref[...]).astype(BF16)


def merge_units(seqs, units, weight, place, after=()):
    slots, rows, width = units.shape
    toks, columns = seqs * rows, slots // seqs * width
    shapes = (bf16_out(toks, weight.shape[0]), bf16_out(toks, columns))
    return pl.pallas_call(
        functools.partial(merge_kernel, seqs),
        grid=(1,),
        out_shape=shapes,
        in_specs=[column_block(weight.shape[0], columns, place), whole_block(units)]
        + [ANYWHERE] * len(after),
        out_specs=[whole_block(shape) for shape in shapes],
        compiler_params=params(),
        cost_estimate=cost(2 * toks * columns * weight.shape[0], 3e6),
        name="merge_units",
    )(weight, units, *after)


def both_stats(own, got):
    zero = jnp.zeros((HD, HD), BF16)
    ones = spread(0, 3, HD)
    ones = jnp.concatenate(
        [jnp.concatenate([ones, zero], axis=1), jnp.concatenate([zero, ones], axis=1)], axis=0
    )
    lse = mm(jnp.concatenate([own, got], axis=1), ones)
    return lse[:, :HD], lse[:, HD:]


def combine_kernel(own_ref, got_ref, attn_ref, stats_ref, *out_refs):
    chunks, slots, rows, _ = own_ref.shape
    for q in range(chunks):
        for k in range(slots):
            lse_a, lse_b = both_stats(own_ref[q, k, :, HD:], got_ref[q, k, :, HD:])
            top = jnp.maximum(lse_a, lse_b)
            weight_a, weight_b = jnp.exp(lse_a - top), jnp.exp(lse_b - top)
            total = weight_a + weight_b
            own = own_ref[q, k, :, :HD].astype(F32)
            got = got_ref[q, k, :, :HD].astype(F32)
            value = (own * weight_a + got * weight_b) * (1.0 / total)
            attn_ref[q, k] = value
            zero = jnp.zeros_like(total)
            stats_ref[q, k] = pack_stats(
                (zero, zero, zero) + split3(top + jnp.log(total))
            ).astype(BF16)
            out_refs[q][k] = value.astype(BF16)


def combine_cores(own, got):
    chunks, slots, rows, _ = own.shape
    results = pl.pallas_call(
        combine_kernel,
        out_shape=[f32_out(chunks, slots, rows, HD), bf16_out(chunks, slots, rows, HD)]
        + [bf16_out(slots, rows, HD)] * chunks,
        in_specs=[IN_VMEM] * 2,
        out_specs=[IN_VMEM] * (2 + chunks),
        compiler_params=params(),
        cost_estimate=cost(1e8, 5e6),
        name="combine_cores",
    )(own, got)
    return results[0], results[1], results[2:]


def join_kernel(attn_ref, stats_ref, in_ref, *refs):
    out_ref = refs[-1]
    for k in range(in_ref.shape[0]):
        grad = in_ref[k]
        delta = jnp.sum(attn_ref[0, k] * grad.astype(F32), axis=-1, keepdims=True)
        delta = jnp.broadcast_to(delta, grad.shape)
        extra = pack_stats(split3(delta)) + stats_ref[0, k].astype(F32)
        out_ref[k] = jnp.concatenate([grad, extra.astype(BF16)], axis=1)


def join_grads(chunk, attn, stats, units, after=()):
    slots, rows, _ = units.shape
    spec = pl.BlockSpec((1, slots, rows, HD), lambda i: (chunk, 0, 0, 0))
    return pl.pallas_call(
        join_kernel,
        grid=(1,),
        out_shape=bf16_out(slots, rows, 2 * HD),
        in_specs=[spec, spec, pl.BlockSpec((slots, rows, HD), lambda i: (0, 0, 0))]
        + [ANYWHERE] * len(after),
        out_specs=pl.BlockSpec((slots, rows, 2 * HD), lambda i: (0, 0, 0)),
        compiler_params=params(),
        cost_estimate=cost(1e7, 2e6),
        name="join_grads",
    )(attn, stats, units, *after)


def add_kernel(own_ref, got_ref, *out_refs):
    for q, out_ref in enumerate(out_refs):
        total = own_ref[q].astype(F32) + got_ref[q].astype(F32)
        out_ref[...] = total.astype(BF16)


def add_cores(own, got):
    chunks, slots, rows, width = own.shape
    return pl.pallas_call(
        add_kernel,
        out_shape=[bf16_out(slots, rows, width)] * chunks,
        in_specs=[IN_VMEM] * 2,
        out_specs=[IN_VMEM] * chunks,
        compiler_params=params(),
        cost_estimate=cost(1e6, 3e6),
        name="add_cores",
    )(own, got)


def ffn_kernel(
    layer, stream_ref, own_ref, other_ref, bias_ref, gain_ref, shift_ref, up_ref, up_bias_ref,
    down_ref, new_ref, normed_ref, pre_ref, part_ref, acc,
):
    step = pl.program_id(0)
    row = slice(layer, layer + 1)

    @pl.when(step == 0)
    def _():
        stream = stream_ref[...] + (own_ref[...].astype(F32) + other_ref[...].astype(F32))
        stream = stream + bias_ref[row]
        new_ref[...] = stream
        normed_ref[...] = layer_norm(stream, gain_ref[row], shift_ref[row]).astype(BF16)

    pre = mm(normed_ref[...], up_ref[0]) + up_bias_ref[row]
    pre_ref[...] = pre
    hidden = jax.nn.gelu(pre, approximate=True).astype(BF16)
    part = mm_t(hidden, down_ref[0])

    @pl.when(step == 0)
    def _():
        acc[...] = part

    @pl.when(step > 0)
    def _():
        acc[...] += part

    @pl.when(step == pl.num_programs(0) - 1)
    def _():
        part_ref[...] = acc[...].astype(BF16)


def feed_forward(layer, stream, own, other, bias, gain, shift, up, up_bias, down):
    toks, width = stream.shape
    hidden = up.shape[2]
    step = hidden // FFN_STEPS
    full = pl.BlockSpec((toks, width), lambda i: (0, 0))
    slab = pl.BlockSpec((1, width, step), lambda i: (layer, 0, i))
    return pl.pallas_call(
        functools.partial(ffn_kernel, layer),
        grid=(FFN_STEPS,),
        out_shape=(
            f32_out(toks, width), bf16_out(toks, width), f32_out(toks, hidden), bf16_out(toks, width),
        ),
        in_specs=[
            full, full, full, whole_block(bias), whole_block(gain), whole_block(shift), slab,
            pl.BlockSpec((LAYERS, step), lambda i: (0, i)), slab,
        ],
        out_specs=(full, full, pl.BlockSpec((toks, step), lambda i: (0, i)), full),
        scratch_shapes=[pltpu.VMEM((toks, width), F32)],
        compiler_params=params(),
        cost_estimate=cost(4 * toks * width * hidden, 14e6),
        name="feed_forward",
    )(stream, own, other, bias, gain, shift, up, up_bias, down)


def ffn_back_kernel(
    grad_ref, up_ref, down_ref, pre_ref,
    branch_ref, hidden_ref, low_ref, down_bias_ref, up_bias_ref, part_ref, acc,
):
    step = pl.program_id(0)

    @pl.when(step == 0)
    def _():
        grad = grad_ref[...]
        branch_ref[...] = grad.astype(BF16)
        down_bias_ref[...] = jnp.sum(grad, axis=0, keepdims=True)

    hidden_grad = mm(branch_ref[...], down_ref[0])
    pre = pre_ref[...]
    root = 0.7978845608028654
    square = pre * pre
    bend = jnp.tanh(root * (pre + 0.044715 * (square * pre)))
    half = 0.5 * (1.0 + bend)
    hidden_ref[...] = (pre * half).astype(BF16)
    slope = half + 0.5 * pre * (1.0 - bend * bend) * (root * (1.0 + 3 * 0.044715 * square))
    pre_grad = hidden_grad * slope
    up_bias_ref[...] = jnp.sum(pre_grad, axis=0, keepdims=True)
    low = pre_grad.astype(BF16)
    low_ref[...] = low
    part = mm_t(low, up_ref[0])

    @pl.when(step == 0)
    def _():
        acc[...] = part

    @pl.when(step > 0)
    def _():
        acc[...] += part

    @pl.when(step == pl.num_programs(0) - 1)
    def _():
        part_ref[...] = acc[...].astype(BF16)


def feed_back(layer, grad, up, down, pre):
    toks, width = grad.shape
    hidden = down.shape[2]
    step = hidden // FFN_STEPS
    full = pl.BlockSpec((toks, width), lambda i: (0, 0))
    slab = pl.BlockSpec((1, width, step), lambda i: (layer, 0, i))
    tall = pl.BlockSpec((toks, step), lambda i: (0, i))
    return pl.pallas_call(
        ffn_back_kernel,
        grid=(FFN_STEPS,),
        out_shape=(
            bf16_out(toks, width), bf16_out(toks, hidden), bf16_out(toks, hidden),
            f32_out(1, width), f32_out(1, hidden), bf16_out(toks, width),
        ),
        in_specs=[full, slab, slab, tall],
        out_specs=(
            full, tall, tall, pl.BlockSpec((1, width), lambda i: (0, 0)),
            pl.BlockSpec((1, step), lambda i: (0, i)), full,
        ),
        scratch_shapes=[pltpu.VMEM((toks, width), F32)],
        compiler_params=params(),
        cost_estimate=cost(4 * toks * width * hidden, 15e6),
        name="feed_back",
    )(grad, up, down, pre)


def products_kernel(counts, *refs):
    out_ref, turned = refs[-2:]
    step = pl.program_id(0)
    start = 0
    for place, count in enumerate(counts):
        lefts = refs[2 * CHUNKS * place : 2 * CHUNKS * place + CHUNKS]
        rights = refs[2 * CHUNKS * place + CHUNKS : 2 * CHUNKS * (place + 1)]

        @pl.when(step == start)
        def _(lefts=lefts):
            for q, left in enumerate(lefts):
                toks = left.shape[0]
                turned[:, q * toks : (q + 1) * toks] = left[...].T

        @pl.when((step >= start) & (step < start + count))
        def _(rights=rights):
            right = jnp.concatenate([right[...] for right in rights], axis=0)
            out_ref[...] = mm(turned[...], right).astype(BF16)

        start += count


def weight_products(pairs, columns, at=0, target=None, after=()):
    block = min(right[0].shape[1] for _, right in pairs)
    block = min(block, 512)
    counts = [right[0].shape[1] // block for _, right in pairs]
    toks, rows = pairs[0][0][0].shape
    specs, operands, start = [], [], 0
    for (left, right), count in zip(pairs, counts):
        specs += [pl.BlockSpec((toks, rows), lambda i: (0, 0))] * CHUNKS
        specs += [
            pl.BlockSpec(
                (toks, block),
                lambda i, start=start, count=count: (0, jnp.clip(i - start, 0, count - 1)),
            )
        ] * CHUNKS
        operands += [*left, *right]
        start += count
    more = [*after] if target is None else [target, *after]
    return pl.pallas_call(
        functools.partial(products_kernel, counts),
        grid=(start,),
        out_shape=bf16_out(rows, columns),
        in_specs=specs + [ANYWHERE] * len(more),
        out_specs=pl.BlockSpec((rows, block), lambda i: (0, i + at // block)),
        scratch_shapes=[pltpu.VMEM((rows, CHUNKS * toks), BF16)],
        input_output_aliases={} if target is None else {len(operands): 0},
        compiler_params=params(),
        cost_estimate=cost(2 * rows * CHUNKS * toks * start * block, 20e6),
        name="weight_products",
    )(*operands, *more)


def norm_back(
    layer, stream_ref, own_ref, other_ref, grad_ref, gain_ref, gain_out, shift_out
):
    grad = own_ref[...].astype(F32) + other_ref[...].astype(F32)
    back, unit = layer_norm_back(stream_ref[...], gain_ref[layer : layer + 1], grad)
    gain_out[...] = jnp.sum(grad * unit, axis=0, keepdims=True)
    shift_out[...] = jnp.sum(grad, axis=0, keepdims=True)
    return grad_ref[...] + back


def leave_kernel(
    seqs, layer, after, stream_ref, own_ref, other_ref, grad_ref, gain_ref, weight_ref, *refs
):
    new_ref, low_ref, gain_out, shift_out, bias_out, out_ref = refs[after:]
    grad = norm_back(
        layer, stream_ref, own_ref, other_ref, grad_ref, gain_ref, gain_out, shift_out
    )
    new_ref[...] = grad
    bias_out[...] = jnp.sum(grad, axis=0, keepdims=True)
    low = grad.astype(BF16)
    low_ref[...] = low
    flat = mm(low, weight_ref[...]).astype(BF16)
    slots, rows, width = out_ref.shape
    for k, at in enumerate(unit_slices(seqs, slots // seqs, rows, width)):
        out_ref[k] = flat[at]


def leave_ffn(
    seqs, layer, stream, own, other, grad, gain, weight, place, columns, after=()
):
    toks, width = stream.shape
    shapes = [f32_out(toks, width), bf16_out(toks, width)] + [f32_out(1, width)] * 3
    shapes.append(bf16_out(seqs * columns // HD, toks // seqs, HD))
    operands = (stream, own, other, grad, gain)
    return pl.pallas_call(
        functools.partial(leave_kernel, seqs, layer, len(after)),
        grid=(1,),
        out_shape=shapes,
        in_specs=[whole_block(operand) for operand in operands]
        + [column_block(width, columns, place)]
        + [ANYWHERE] * len(after),
        out_specs=[whole_block(shape) for shape in shapes],
        compiler_params=params(),
        cost_estimate=cost(2 * toks * width * columns, 6e6),
        name="leave_ffn",
    )(*operands, weight, *after)


def finish_kernel(
    layer, stream_ref, own_ref, other_ref, grad_ref, gain_ref, new_ref, gain_out, shift_out
):
    new_ref[...] = norm_back(
        layer, stream_ref, own_ref, other_ref, grad_ref, gain_ref, gain_out, shift_out
    )


def finish_attention(layer, stream, own, other, grad, gain):
    toks, width = stream.shape
    return pl.pallas_call(
        functools.partial(finish_kernel, layer),
        out_shape=(f32_out(toks, width), f32_out(1, width), f32_out(1, width)),
        in_specs=[IN_VMEM] * 5,
        out_specs=(IN_VMEM,) * 3,
        compiler_params=params(),
        cost_estimate=cost(1e7, 4e6),
        name="finish_attention",
    )(stream, own, other, grad, gain)


def reduce_rows(value):
    count = lax.axis_size("wide")
    index = lax.axis_index("wide")
    width = value.shape[1]
    block = value.shape[0] // count
    value = value.astype(BF16)
    bit = 1
    parts = count
    while bit < count:
        view = value.reshape(parts // 2, 2, block, width)
        mine = (index // bit) % 2
        sent = lax.dynamic_index_in_dim(view, 1 - mine, 1, keepdims=False)
        kept = lax.dynamic_index_in_dim(view, mine, 1, keepdims=False)
        value = kept.astype(F32) + swap(sent, "wide", bit).astype(F32)
        parts //= 2
        bit *= 2
        if bit < count:
            value = value.astype(BF16)
    return value.reshape(block, width)


def sum_rows(value, widths):
    total = lax.psum_scatter(value, "wide", scatter_dimension=0, tiled=True).astype(F32)
    ends = [0]
    for width in widths:
        ends.append(ends[-1] + width)
    return [total[:, low:high] for low, high in zip(ends, ends[1:])]


def sum_wide(value):
    for bit in range(lax.axis_size("wide").bit_length() - 1):
        value = value + swap(value, "wide", 1 << bit)
    return value


def shards(
    first_in, second_in, attn_norm_gain, attn_norm_bias, qk_weight, value_weight, out_weight,
    out_bias, ffn_norm_gain, ffn_norm_bias, up_weight, up_bias, down_weight, down_bias,
    bucket_perm, first_cot, second_cot,
):
    seqs, rows, half = first_in.shape
    wide = lax.axis_size("wide")
    wide_index = lax.axis_index("wide")
    narrow_index = lax.axis_index("narrow")
    pos = jnp.stack([wide_index % 2, narrow_index]).astype(jnp.int32)
    weight_rows, head_width = qk_weight.shape[1:]
    heads = head_width // HD
    width = 2 * half
    hidden_width = up_bias.shape[1]
    chunks = range(CHUNKS)

    def own_half(full):
        return lax.dynamic_slice_in_dim(full, narrow_index * half, half, full.ndim - 1)

    def flat_weight(layer):
        pair = jnp.stack([qk_weight[layer], value_weight[layer]], axis=1)
        pair = pair.reshape(weight_rows, 2, heads, HD)
        return jnp.transpose(pair, (0, 2, 1, 3)).reshape(weight_rows, 2 * head_width)

    def widen(streams, after):
        return [
            widen_chunks(pos, stream, swap(sent, "narrow", 1))
            for stream, sent in zip(streams, lower_arrays(streams, after))
        ]

    second, first = widen((second_in, first_in), [])
    early = lax.all_gather(
        jnp.concatenate([flat_weight(0), out_weight[0]], axis=1), "wide", axis=0, tiled=True
    )

    perm_parts = bucket_perm.reshape(2, ROUNDS // 2, seqs, rows)
    perm_send = jnp.transpose(perm_parts, (2, 0, 1, 3))
    perm_send = jnp.broadcast_to(
        perm_send[:, None], (seqs, heads, 2, ROUNDS // 2, rows)
    ).reshape(wide, ROUNDS // 2, rows)
    perm_got = lax.all_to_all(perm_send, "wide", 0, 0, tiled=True)
    tables = build_tables(jnp.transpose(perm_got, (1, 0, 2)).reshape(ROUNDS // 2, wide * rows))

    unit_columns = 2 * head_width
    gathered = [early]
    biases = jnp.stack([out_bias, down_bias])
    other = swap(biases, "narrow", 1)
    out_bias, down_bias = jnp.where(
        narrow_index == 0,
        jnp.concatenate([biases, other], axis=-1),
        jnp.concatenate([other, biases], axis=-1),
    )

    saved = []
    ffn_parts = [() for _ in chunks]
    afters = [[], [*tables, *first, out_bias, down_bias]]
    for layer in range(LAYERS):
        normed, sources = [], []
        for q in chunks:
            second[q], normed_q, units = enter_attention(
                seqs, layer, second[q], attn_norm_gain, attn_norm_bias, gathered[layer], 0,
                unit_columns, ffn_parts[q], afters[min(q, 1)] if layer == 0 else (),
            )
            normed.append(normed_q)
            own = chip_exchange(units)
            sources += [own, swap(own, "wide", 1)]
        sorted_rows, own, sib = attention_forward(pos, sources, tables, ())
        attn, stats, units = combine_cores(own, swap(sib, "wide", 1))
        after = []
        if layer == 0:
            grad_second, grad_first = widen((second_cot, first_cot), sources[-2:-1])
            after = [*grad_second, *grad_first]
        if layer + 1 < LAYERS:
            pieces = pack_columns([flat_weight(layer + 1), out_weight[layer + 1]], units[:1])
            gathered.append(lax.all_gather(pieces, "wide", axis=0, tiled=True))
        second_now, attn_tok, ffn_in, pre_act = list(second), [], [], []
        backs = [chip_exchange(units[q]) for q in chunks]
        for q in chunks:
            part, attn_tok_q = merge_units(seqs, backs[q], gathered[layer], 2, after)
            attn_tok.append(attn_tok_q)
            first[q], ffn_in_q, pre_q, part = feed_forward(
                layer, first[q], part, swap(part, "narrow", 1), out_bias,
                ffn_norm_gain, ffn_norm_bias, up_weight, up_bias, down_weight,
            )
            ffn_in.append(ffn_in_q)
            pre_act.append(pre_q)
            ffn_parts[q] = (part, swap(part, "narrow", 1), down_bias)
        saved.append((second_now, normed, sorted_rows, attn, stats, attn_tok, list(first), ffn_in, pre_act))
    first_out = narrow_chunks(pos, first, seqs)
    last_parts = [part for q in chunks for part in ffn_parts[q][:2]] + [down_bias]
    second_out = narrow_chunks(pos, second, seqs, LAYERS - 1, last_parts)

    summed, waiting, done = [], [], []
    small_grads = [None] * LAYERS
    after = []
    for layer in reversed(range(LAYERS)):
        second_l, normed, sorted_rows, attn, stats, attn_tok, first_l, ffn_in, pre_act = saved[layer]
        branch, hidden, low, parts = [], [], [], []
        down_bias_grad, up_bias_grad = 0.0, 0.0
        for q in chunks:
            branch_q, hidden_q, low_q, down_bias_q, up_bias_q, part = feed_back(
                layer, grad_second[q], up_weight, down_weight, pre_act[q]
            )
            branch.append(branch_q)
            hidden.append(hidden_q)
            low.append(low_q)
            parts.append((part, swap(part, "narrow", 1)))
            down_bias_grad += down_bias_q
            up_bias_grad += up_bias_q
        pairs = waiting + [(ffn_in, low), (branch, hidden)]
        widths = [right[0].shape[1] for _, right in pairs]
        columns = sum(widths) + head_width
        products = weight_products(pairs, columns, after=done)
        out_low, units = [], []
        ffn_gain_grad, ffn_bias_grad, out_bias_grad = 0.0, 0.0, 0.0
        for q in chunks:
            *results, units_q = leave_ffn(
                seqs, layer, first_l[q], *parts[q], grad_first[q], ffn_norm_gain,
                gathered[layer], 2, head_width, [*units, products] if q > 0 else (),
            )
            grad_first[q] = results[0]
            out_low.append(results[1])
            ffn_gain_grad += results[2]
            ffn_bias_grad += results[3]
            out_bias_grad += results[4]
            units.append(chip_exchange(units_q))
        products = weight_products(
            [(out_low, attn_tok)], columns, columns - head_width, products
        )
        summed += sum_rows(products, widths + [head_width])
        sources = []
        for q in chunks:
            own = join_grads(q, attn, stats, units[q], [products] if q > 0 else ())
            sources += [own, swap(own, "wide", 1)]
        early_small = jnp.concatenate(
            [
                own_half(grad)
                for grad in (ffn_gain_grad, ffn_bias_grad, out_bias_grad, down_bias_grad)
            ]
            + [up_bias_grad.reshape(-1, half)]
        )
        own, sib = attention_backward(pos, sources, sorted_rows, tables, [early_small])
        units = add_cores(own, swap(sib, "wide", 1))
        grad_tok, attn_gain_grad, attn_bias_grad = [], 0.0, 0.0
        backs = [chip_exchange(units[q]) for q in chunks]
        for q in chunks:
            part, grad_tok_q = merge_units(
                seqs, backs[q], gathered[layer], 0, grad_second[:1] if q > 0 and layer == 0 else ()
            )
            grad_tok.append(grad_tok_q)
            grad_second[q], gain_q, shift_q = finish_attention(
                layer, second_l[q], part, swap(part, "narrow", 1), grad_second[q], attn_norm_gain
            )
            attn_gain_grad += gain_q
            attn_bias_grad += shift_q
        waiting = [(normed, grad_tok)]
        done = summed[-1:]
        late_small = jnp.concatenate([own_half(attn_gain_grad), own_half(attn_bias_grad)])
        small_grads[layer] = jnp.concatenate([late_small, early_small])
    summed.append(reduce_rows(weight_products(waiting, unit_columns)))
    first_grad = narrow_chunks(pos, grad_first, seqs)
    second_grad = narrow_chunks(pos, grad_second, seqs)

    small = sum_wide(jnp.stack(small_grads))
    other = swap(small[:, :4], "narrow", 1)
    paired = jnp.where(
        narrow_index == 0,
        jnp.concatenate([small[:, :4], other], axis=-1),
        jnp.concatenate([other, small[:, :4]], axis=-1),
    )
    order = [(4, 5, 6, 7), (0, 1, 2, 3)]
    weight_grads = [None] * LAYERS
    for layer in range(LAYERS):
        up_sum, down_sum, out_sum, unit_sum = [summed[at] for at in order[layer]]
        by_unit = unit_sum.reshape(weight_rows, heads, 2, HD)
        weight_grads[layer] = (
            by_unit[:, :, 0].reshape(weight_rows, head_width),
            by_unit[:, :, 1].reshape(weight_rows, head_width),
            out_sum,
            up_sum,
            down_sum,
        )

    def stacked(slot):
        return jnp.stack([weight_grads[layer][slot] for layer in range(LAYERS)])

    return (
        first_out,
        second_out,
        first_grad,
        second_grad,
        paired[:, 0],
        paired[:, 1],
        stacked(0),
        stacked(1),
        stacked(2),
        small[:, 4],
        paired[:, 2],
        paired[:, 3],
        stacked(3),
        small[:, 6:].reshape(LAYERS, hidden_width),
        stacked(4),
        small[:, 5],
    )


def solution(mesh):
    streams = P(None, "wide", "narrow")
    features = P(None, "narrow")
    hidden = P(None, None, "narrow")
    return jax.shard_map(
        shards,
        mesh=mesh,
        in_specs=(
            streams, streams, P(), P(), streams, streams, streams, features, P(), P(),
            hidden, features, hidden, features, P(None, None, "wide"), streams, streams,
        ),
        out_specs=(
            streams, streams, streams, streams, P(), P(), streams, streams, streams,
            features, P(), P(), streams, features, streams, features,
        ),
        check_vma=False,
    )
```

time: 1080 us -> 774 us (0.72)
  waiting for transfers between devices: 322 us -> 176 us
  blocking collectives: 0 us -> 83.2 us
  other arithmetic: 92.8 us -> 21.4 us
  starting transfers between devices: 167 us -> 104 us
  matrix products: 64.6 us -> 1.66 us
  local copies, waits for them, and re-layouts: 98.3 us -> 45.3 us
    ppermute x120 -> x42, waiting for transfers between devices: 271 us -> 120 us  [swap(): lax.ppermute(value, axis, [(source, source ^ mask) for source in range(co...]
    ppermute x120 -> x42, starting transfers between devices: 161 us -> 40.3 us  [swap(): lax.ppermute(value, axis, [(source, source ^ mask) for source in range(co...]
    all_to_all x0 -> x3, blocking collectives: none -> 83.2 us  [chip_exchange(): lax.all_to_all(units, 'wide', 0, 0, tiled=True, axis_index_groups=groups)]
    dot_general x16 -> x0, matrix products: 62.9 us -> none  [dot(): lax.dot_general(left, right, (dims, ((), ())), preferred_element_type=F32)]
    all_to_all x0 -> x13, starting transfers between devices: none -> 57.5 us  [chip_exchange(): lax.all_to_all(units, 'wide', 0, 0, tiled=True, axis_index_groups=groups)]
    all_to_all x0 -> x13, waiting for transfers between devices: none -> 49.9 us  [chip_exchange(): lax.all_to_all(units, 'wide', 0, 0, tiled=True, axis_index_groups=groups)]
    all_gather x1 -> x2, waiting for transfers between devices: 45.1 us -> 5.25 us  [the longest x1 5.25 us: shards(): lax.all_gather(jnp.concatenate([flat_weight(0), out_weight[0]], axis=1),...]
    reduce_sum x25 -> x0, other arithmetic: 21.7 us -> none  [the longest x4 5.55 us: layer_norm_back(): jnp.mean(scaled, axis=-1, keepdims=True)]
  transfers between devices with their start and end apart: 122 -> 60, of which waited for: 51 -> 33; matrix products, arithmetic and copies ran while one was open for 16% -> 4% of each run, Pallas kernels for 15% -> 33%
where the time goes in v2:
time: 774 us; the launch traced here: 764 us
  Pallas kernels  317 us (41%)
  waiting for transfers between devices  176 us (23%)
  starting transfers between devices  104 us (13%)
  blocking collectives  83.2 us (11%)
  local copies, waits for them, and re-layouts  45.3 us (6%)
  other arithmetic  21.4 us (3%)
  between operations  15.1 us (2%)
    ppermute x42, waiting for transfers between devices, swap(): lax.ppermute(value, axis, [(source, source ^ mask) for source in range(co...  120 us
    all_to_all x3, blocking collectives, chip_exchange(): lax.all_to_all(units, 'wide', 0, 0, tiled=True, axis_index_groups=groups)  83.2 us
    all_to_all x13, starting transfers between devices, chip_exchange(): lax.all_to_all(units, 'wide', 0, 0, tiled=True, axis_index_groups=groups)  57.5 us
    all_to_all x13, waiting for transfers between devices, chip_exchange(): lax.all_to_all(units, 'wide', 0, 0, tiled=True, axis_index_groups=groups)  49.9 us
    pallas_call x2, Pallas kernels, attention_backward(): pl.pallas_call(functools.partial(backward_kernel, chunks, len(after)), ou...  44.9 us
    ppermute x42, starting transfers between devices, swap(): lax.ppermute(value, axis, [(source, source ^ mask) for source in range(co...  40.3 us
    pallas_call x2, Pallas kernels, attention_forward(): pl.pallas_call(functools.partial(forward_kernel, chunks, len(after)), out...  38.4 us
    pallas_call x4, Pallas kernels, feed_back(): pl.pallas_call(ffn_back_kernel, grid=(FFN_STEPS,), out_shape=(bf16_out(to...  37.7 us
  transfers between devices with their start and end apart: 60, of which 33 were waited for; matrix products, arithmetic and copies ran while one was open for 4% of the time, Pallas kernels for 33%

profile of v2, /device:TPU:0, one launch (start us, length us, event | category | flops | bytes accessed | tf_op | source)
XLA Modules:
  0.0 763.8 jit_solution(10063743281659191188)
XLA Ops:
  31.6 19.3 %collective-permute-done.1.other_ref = bf16[2,256,512]{2,1,0:T(8,128)(2,1)S(1)} collective-permute-done((bf16[2,256,512]{2,1,0:T(8,128)(2,1)}, bf16[2,256,512]{2,1,0:T(8,128)(2,1)S(1)}, u32[]{:S(2)}, u32[]{:S(2)}) %collective-permute-start.1) | collective-permute-done | bytes 524320 | tf_op jit(solution)/shard_map/ppermute | solution.py:26
  91.4 14.3 %all-to-all-done.2.refs_2_ = bf16[8,128,256]{2,1,0:T(8,128)(2,1)S(1)} async-done(((bf16[8,128,256]{2,1,0:T(8,128)(2,1)}), bf16[8,128,256]{2,1,0:T(8,128)(2,1)S(1)}, u32[]{:S(2)}, u32[]{:S(2)}) %all-to-all-start.2) | async-done | bytes 524320 | tf_op jit(solution)/shard_map/all_to_all | solution.py:48
  108.4 19.2 %attend_forward.2 = (bf16[2,4096,256]{2,1,0:T(8,128)(2,1)}, bf16[2,8,128,256]{3,2,1,0:T(8,128)(2,1)}, bf16[2,8,128,256]{3,2,1,0:T(8,128)(2,1)}) custom-call(s32[2]{0:T(128)} %pad_add_fusion.pos_ref, bf16[8,128,256]{2,1,0:T(8,128)(2,1)} %copy-done.28, bf16[8,128,256]{2,1,0:T(8,128)(2,1)} %copy-done.71, bf16[8,128,256]{2,1,0:T(8,128)(2,1)} %copy-done.3, ...), custom_call_target="tpu_custom_call" | custom-call | flops 16000000000 | bytes 24000000 | tf_op jit(solution)/shard_map/attend_forward/pallas_call | solution.py:448
  145.6 9.3 %collective-permute-done.7.other_ref = bf16[2,256,512]{2,1,0:T(8,128)(2,1)S(1)} collective-permute-done((bf16[2,256,512]{2,1,0:T(8,128)(2,1)}, bf16[2,256,512]{2,1,0:T(8,128)(2,1)S(1)}, u32[]{:S(2)}, u32[]{:S(2)}) %collective-permute-start.7) | collective-permute-done | bytes 524320 | tf_op jit(solution)/shard_map/ppermute | solution.py:26
  158.5 6.8 collective-permute-done.6.other_ref
  177.3 8.2 %collective-permute-done.8.other_ref = bf16[256,1024]{1,0:T(8,128)(2,1)S(1)} collective-permute-done((bf16[256,1024]{1,0:T(8,128)(2,1)}, bf16[256,1024]{1,0:T(8,128)(2,1)S(1)}, u32[]{:S(2)}, u32[]{:S(2)}) %collective-permute-start.8) | collective-permute-done | bytes 524320 | tf_op jit(solution)/shard_map/ppermute | solution.py:26
  186.3 9.1 %feed_forward.4 = (f32[256,1024]{1,0:T(8,128)}, bf16[256,1024]{1,0:T(8,128)(2,1)}, f32[256,2048]{1,0:T(8,128)}, bf16[256,1024]{1,0:T(8,128)(2,1)}) custom-call(f32[256,1024]{1,0:T(8,128)} %get-tuple-element.153.refs_4_.stream_ref, bf16[256,1024]{1,0:T(8,128)(2,1)} %get-tuple-element.169.own_ref, bf16[256,1024]{1,0:T(8,128)(2,1)} %copy-done.24, ...), custom_call_target="tpu_custom_call" | custom-call | flops 2147483648 | bytes 14000000 | tf_op jit(solution)/shard_map/feed_forward/pallas_call | solution.py:811
  200.7 9.8 %collective-permute-done.9.refs_1_ = bf16[256,1024]{1,0:T(8,128)(2,1)S(1)} collective-permute-done((bf16[256,1024]{1,0:T(8,128)(2,1)}, bf16[256,1024]{1,0:T(8,128)(2,1)S(1)}, u32[]{:S(2)}, u32[]{:S(2)}) %collective-permute-start.9) | collective-permute-done | bytes 524320 | tf_op jit(solution)/shard_map/ppermute | solution.py:26
  220.0 9.1 %feed_forward.5 = (f32[256,1024]{1,0:T(8,128)}, bf16[256,1024]{1,0:T(8,128)(2,1)}, f32[256,2048]{1,0:T(8,128)}, bf16[256,1024]{1,0:T(8,128)(2,1)}) custom-call(f32[256,1024]{1,0:T(8,128)} %get-tuple-element.158.refs_5_.stream_ref, bf16[256,1024]{1,0:T(8,128)(2,1)} %get-tuple-element.174.own_ref, bf16[256,1024]{1,0:T(8,128)(2,1)} %copy-done.21, ...), custom_call_target="tpu_custom_call" | custom-call | flops 2147483648 | bytes 14000000 | tf_op jit(solution)/shard_map/feed_forward/pallas_call | solution.py:811
  230.7 10.0 %collective-permute-done.12.refs_1_ = bf16[256,1024]{1,0:T(8,128)(2,1)S(1)} collective-permute-done((bf16[256,1024]{1,0:T(8,128)(2,1)}, bf16[256,1024]{1,0:T(8,128)(2,1)S(1)}, u32[]{:S(2)}, u32[]{:S(2)}) %collective-permute-start.12) | collective-permute-done | bytes 524320 | tf_op jit(solution)/shard_map/ppermute | solution.py:26
  249.7 10.9 %all-to-all-done.6.refs_2_ = bf16[8,128,256]{2,1,0:T(8,128)(2,1)S(1)} async-done(((bf16[8,128,256]{2,1,0:T(8,128)(2,1)}), bf16[8,128,256]{2,1,0:T(8,128)(2,1)S(1)}, u32[]{:S(2)}, u32[]{:S(2)}) %all-to-all-start.6) | async-done | bytes 524320 | tf_op jit(solution)/shard_map/all_to_all | solution.py:48
  263.3 19.2 %attend_forward.3 = (bf16[2,4096,256]{2,1,0:T(8,128)(2,1)}, bf16[2,8,128,256]{3,2,1,0:T(8,128)(2,1)}, bf16[2,8,128,256]{3,2,1,0:T(8,128)(2,1)}) custom-call(s32[2]{0:T(128)} %pad_add_fusion.pos_ref, bf16[8,128,256]{2,1,0:T(8,128)(2,1)} %copy-done.29, bf16[8,128,256]{2,1,0:T(8,128)(2,1)} %copy-done.70, bf16[8,128,256]{2,1,0:T(8,128)(2,1)} %copy-done.30, ...), custom_call_target="tpu_custom_call" | custom-call | flops 16000000000 | bytes 24000000 | tf_op jit(solution)/shard_map/attend_forward/pallas_call | solution.py:448
  290.6 13.5 %all_to_all.85.in_ref = bf16[8,128,128]{2,1,0:T(8,128)(2,1)} all-to-all(bf16[8,128,128]{2,1,0:T(8,128)(2,1)} %get-tuple-element.179), channel_id=1, replica_groups={{0,4,8,12,16,20,24,28},{2,6,10,14,18,22,26,30},{1,5,9,13,17,21,25,29},{..., dimensions={0} | all-to-all | bytes 524288 | tf_op jit(solution)/shard_map/all_to_all | solution.py:48
  326.1 9.1 %feed_forward.6 = (f32[256,1024]{1,0:T(8,128)}, bf16[256,1024]{1,0:T(8,128)(2,1)}, f32[256,2048]{1,0:T(8,128)}, bf16[256,1024]{1,0:T(8,128)(2,1)}) custom-call(f32[256,1024]{1,0:T(8,128)} %get-tuple-element.170.stream_ref, bf16[256,1024]{1,0:T(8,128)(2,1)} %get-tuple-element.180.own_ref, bf16[256,1024]{1,0:T(8,128)(2,1)} %copy-done.23, ...), custom_call_target="tpu_custom_call" | custom-call | flops 2147483648 | bytes 14000000 | tf_op jit(solution)/shard_map/feed_forward/pallas_call | solution.py:811
  335.2 9.4 %feed_back.4 = (bf16[256,1024]{1,0:T(8,128)(2,1)}, bf16[256,2048]{1,0:T(8,128)(2,1)}, bf16[256,2048]{1,0:T(8,128)(2,1)}, f32[1,1024]{1,0:T(1,128)}, f32[1,2048]{1,0:T(1,128)}, /*index=5*/bf16[256,1024]{1,0:T(8,128)(2,1)}) custom-call(f32[256,1024]{1,0:T(8,128)} %get-tuple-element.164.refs_0_.grad_ref, bf16[2,1024,2048]{2,1,0:T(8,128)(2,1)} %up_ref.15, ...), custom_call_target="tpu_custom_call" | custom-call | flops 2147483648 | bytes 15000000 | tf_op jit(solution)/shard_map/feed_back/pallas_call | solution.py:875
  347.2 9.1 %feed_forward.7 = (f32[256,1024]{1,0:T(8,128)}, bf16[256,1024]{1,0:T(8,128)(2,1)}, f32[256,2048]{1,0:T(8,128)}, bf16[256,1024]{1,0:T(8,128)(2,1)}) custom-call(f32[256,1024]{1,0:T(8,128)} %get-tuple-element.182.stream_ref, bf16[256,1024]{1,0:T(8,128)(2,1)} %get-tuple-element.184.own_ref, bf16[256,1024]{1,0:T(8,128)(2,1)} %copy-done.20, ...), custom_call_target="tpu_custom_call" | custom-call | flops 2147483648 | bytes 14000000 | tf_op jit(solution)/shard_map/feed_forward/pallas_call | solution.py:811
  356.3 9.4 %feed_back.5 = (bf16[256,1024]{1,0:T(8,128)(2,1)}, bf16[256,2048]{1,0:T(8,128)(2,1)}, bf16[256,2048]{1,0:T(8,128)(2,1)}, f32[1,1024]{1,0:T(1,128)}, f32[1,2048]{1,0:T(1,128)}, /*index=5*/bf16[256,1024]{1,0:T(8,128)(2,1)}) custom-call(f32[256,1024]{1,0:T(8,128)} %get-tuple-element.165.refs_1_.grad_ref, bf16[2,1024,2048]{2,1,0:T(8,128)(2,1)} %up_ref.15, ...), custom_call_target="tpu_custom_call" | custom-call | flops 2147483648 | bytes 15000000 | tf_op jit(solution)/shard_map/feed_back/pallas_call | solution.py:875
  371.3 6.0 all-to-all-start.9
  377.3 11.3 %weight_products.5.refs_1_.refs_4_ = bf16[1024,4608]{1,0:T(8,128)(2,1)} custom-call(bf16[256,1024]{1,0:T(8,128)(2,1)} %get-tuple-element.197.refs_0_, bf16[256,1024]{1,0:T(8,128)(2,1)} %get-tuple-element.198.refs_1_, bf16[256,2048]{1,0:T(8,128)(2,1)} %get-tuple-element.199.refs_2_, bf16[256,2048]{1,0:T(8,128)(2,1)} %get-tuple-element.200.refs_3_, ...), custom_call_target="tpu_custom_call" | custom-call | flops 4294967296 | bytes 20000000 | tf_op jit(solution)/shard_map/weight_products/pallas_call | solution.py:933
  397.1 6.3 all-to-all-start.10
  417.5 22.3 %attend_backward.2 = (bf16[2,8,128,256]{3,2,1,0:T(8,128)(2,1)}, bf16[2,8,128,256]{3,2,1,0:T(8,128)(2,1)}) custom-call(s32[2]{0:T(128)} %pad_add_fusion.pos_ref, bf16[8,128,256]{2,1,0:T(8,128)(2,1)} %join_grads.4.refs_0_, bf16[8,128,256]{2,1,0:T(8,128)(2,1)} %copy-done.66, bf16[8,128,256]{2,1,0:T(8,128)(2,1)} %join_grads.5.refs_2_, ...), custom_call_target="tpu_custom_call" | custom-call | flops 17999998976 | bytes 26000000 | tf_op jit(solution)/shard_map/attend_backward/pallas_call | solution.py:478
  446.4 34.8 %all_to_all.86.in_ref = bf16[8,128,256]{2,1,0:T(8,128)(2,1)} all-to-all(bf16[8,128,256]{2,1,0:T(8,128)(2,1)} %get-tuple-element.223), channel_id=1, replica_groups={{0,4,8,12,16,20,24,28},{2,6,10,14,18,22,26,30},{1,5,9,13,17,21,25,29},{..., dimensions={0} | all-to-all | bytes 1048576 | tf_op jit(solution)/shard_map/all_to_all | solution.py:48
  489.6 9.3 %all-to-all-done.12.in_ref = bf16[8,128,256]{2,1,0:T(8,128)(2,1)S(1)} async-done(((bf16[8,128,256]{2,1,0:T(8,128)(2,1)}), bf16[8,128,256]{2,1,0:T(8,128)(2,1)S(1)}, u32[]{:S(2)}, u32[]{:S(2)}) %all-to-all-start.12) | async-done | bytes 524320 | tf_op jit(solution)/shard_map/all_to_all | solution.py:48
  509.7 9.4 %feed_back.6 = (bf16[256,1024]{1,0:T(8,128)(2,1)}, bf16[256,2048]{1,0:T(8,128)(2,1)}, bf16[256,2048]{1,0:T(8,128)(2,1)}, f32[1,1024]{1,0:T(1,128)}, f32[1,2048]{1,0:T(1,128)}, /*index=5*/bf16[256,1024]{1,0:T(8,128)(2,1)}) custom-call(f32[256,1024]{1,0:T(8,128)} %get-tuple-element.225.grad_ref, bf16[2,1024,2048]{2,1,0:T(8,128)(2,1)} %up_ref.15, ...), custom_call_target="tpu_custom_call" | custom-call | flops 2147483648 | bytes 15000000 | tf_op jit(solution)/shard_map/feed_back/pallas_call | solution.py:875
  523.6 9.5 %feed_back.7 = (bf16[256,1024]{1,0:T(8,128)(2,1)}, bf16[256,2048]{1,0:T(8,128)(2,1)}, bf16[256,2048]{1,0:T(8,128)(2,1)}, f32[1,1024]{1,0:T(1,128)}, f32[1,2048]{1,0:T(1,128)}, /*index=5*/bf16[256,1024]{1,0:T(8,128)(2,1)}) custom-call(f32[256,1024]{1,0:T(8,128)} %get-tuple-element.232.grad_ref, bf16[2,1024,2048]{2,1,0:T(8,128)(2,1)} %up_ref.15, ...), custom_call_target="tpu_custom_call" | custom-call | flops 2147483648 | bytes 15000000 | tf_op jit(solution)/shard_map/feed_back/pallas_call | solution.py:875
  545.9 13.9 %weight_products.7.refs_1_.refs_4_ = bf16[1024,5632]{1,0:T(8,128)(2,1)} custom-call(bf16[256,1024]{1,0:T(8,128)(2,1)} %get-tuple-element.237.refs_0_, bf16[256,1024]{1,0:T(8,128)(2,1)} %get-tuple-element.238.refs_1_, bf16[256,1024]{1,0:T(8,128)(2,1)} %get-tuple-element.239.refs_2_, bf16[256,1024]{1,0:T(8,128)(2,1)} %get-tuple-element.240.refs_3_, ...), custom_call_target="tpu_custom_call" | custom-call | flops 5368709120 | bytes 20000000 | tf_op jit(solution)/shard_map/weight_products/pallas_call | solution.py:933
  568.2 6.3 all-to-all-start.14
  588.4 22.6 %attend_backward.3 = (bf16[2,8,128,256]{3,2,1,0:T(8,128)(2,1)}, bf16[2,8,128,256]{3,2,1,0:T(8,128)(2,1)}) custom-call(s32[2]{0:T(128)} %pad_add_fusion.pos_ref, bf16[8,128,256]{2,1,0:T(8,128)(2,1)} %join_grads.6.refs_0_, bf16[8,128,256]{2,1,0:T(8,128)(2,1)} %copy-done.67, bf16[8,128,256]{2,1,0:T(8,128)(2,1)} %join_grads.7.refs_2_, ...), custom_call_target="tpu_custom_call" | custom-call | flops 17999998976 | bytes 26000000 | tf_op jit(solution)/shard_map/attend_backward/pallas_call | solution.py:478
  617.6 35.0 %all_to_all.87.in_ref = bf16[8,128,256]{2,1,0:T(8,128)(2,1)} all-to-all(bf16[8,128,256]{2,1,0:T(8,128)(2,1)} %get-tuple-element.270), channel_id=1, replica_groups={{0,4,8,12,16,20,24,28},{2,6,10,14,18,22,26,30},{1,5,9,13,17,21,25,29},{..., dimensions={0} | all-to-all | bytes 1048576 | tf_op jit(solution)/shard_map/all_to_all | solution.py:48
  660.3 12.6 %collective-permute-done.31.other_ref = bf16[256,1024]{1,0:T(8,128)(2,1)S(1)} collective-permute-done((bf16[256,1024]{1,0:T(8,128)(2,1)}, bf16[256,1024]{1,0:T(8,128)(2,1)S(1)}, u32[]{:S(2)}, u32[]{:S(2)}) %collective-permute-start.31) | collective-permute-done | bytes 524320 | tf_op jit(solution)/shard_map/ppermute | solution.py:26
  689.6 7.1 collective-permute-done.32.other_ref
  708.6 8.3 %collective-permute-done.17.refs_3_ = bf16[256,1024]{1,0:T(8,128)(2,1)} collective-permute-done((bf16[256,1024]{1,0:T(8,128)(2,1)S(1)}, bf16[256,1024]{1,0:T(8,128)(2,1)}, u32[]{:S(2)}, u32[]{:S(2)}) %collective-permute-start.17) | collective-permute-done | bytes 524320 | tf_op jit(solution)/shard_map/ppermute | solution.py:26
  (393 shorter events, 338.2 us)
Async XLA Ops:
  7.2 52.6 %all-gather.3.cloned.1.call-start = ((), (), s32[]{:S(2)}) async-start(), calls=%async_computation.19 | async-start | bytes 3342336 | tf_op jit(solution)/shard_map/all_gather | solution.py:1082
  12.4 15.5 %collective-permute-start.3 = (f32[2,2,512]{2,1,0:T(2,128)S(1)}, f32[2,2,512]{2,1,0:T(2,128)S(1)}, u32[]{:S(2)}, u32[]{:S(2)}) collective-permute-start(f32[2,2,512]{2,1,0:T(2,128)S(1)} %pad_maximum_fusion.7), channel_id=1, source_target_pairs={{0,1},{1,0},{2,3},{3,2},{4,5},{5,4},{6,7},{7,6},{8,9},{9,8},{10,11... | collective-permute-start | bytes 24584 | tf_op jit(solution)/shard_map/ppermute | solution.py:26
  25.2 52.6 %collective-permute-start = (bf16[2,256,512]{2,1,0:T(8,128)(2,1)}, bf16[2,256,512]{2,1,0:T(8,128)(2,1)S(1)}, u32[]{:S(2)}, u32[]{:S(2)}) collective-permute-start(bf16[2,256,512]{2,1,0:T(8,128)(2,1)} %get-tuple-element.152), channel_id=1, source_target_pairs={{0,1},{1,0},{2,3},{3,2},{4,5},{5,4},{6,7},{7,6},{8,9},{9,8},{10,11... | collective-permute-start | bytes 1572872 | tf_op jit(solution)/shard_map/ppermute | solution.py:26
  25.8 25.1 %collective-permute-start.1 = (bf16[2,256,512]{2,1,0:T(8,128)(2,1)}, bf16[2,256,512]{2,1,0:T(8,128)(2,1)S(1)}, u32[]{:S(2)}, u32[]{:S(2)}) collective-permute-start(bf16[2,256,512]{2,1,0:T(8,128)(2,1)} %get-tuple-element.154), channel_id=1, source_target_pairs={{0,1},{1,0},{2,3},{3,2},{4,5},{5,4},{6,7},{7,6},{8,9},{9,8},{10,11... | collective-permute-start | bytes 1572872 | tf_op jit(solution)/shard_map/ppermute | solution.py:26
  63.5 21.7 %all-to-all-start = ((bf16[8,128,256]{2,1,0:T(8,128)(2,1)}), bf16[8,128,256]{2,1,0:T(8,128)(2,1)S(1)}, u32[]{:S(2)}, u32[]{:S(2)}) async-start(bf16[8,128,256]{2,1,0:T(8,128)(2,1)} %get-tuple-element.156), calls=%async_computation | async-start | bytes 1048576 | tf_op jit(solution)/shard_map/all_to_all | solution.py:48
  85.2 20.6 %all-to-all-start.2 = ((bf16[8,128,256]{2,1,0:T(8,128)(2,1)}), bf16[8,128,256]{2,1,0:T(8,128)(2,1)S(1)}, u32[]{:S(2)}, u32[]{:S(2)}) async-start(bf16[8,128,256]{2,1,0:T(8,128)(2,1)} %get-tuple-element.159), calls=%async_computation.2 | async-start | bytes 1048576 | tf_op jit(solution)/shard_map/all_to_all | solution.py:48
  91.1 119.4 %all-gather.5.cloned.1.call-start = ((), (), s32[]{:S(2)}) async-start(), calls=%async_computation.20 | async-start | bytes 3342336 | tf_op jit(solution)/shard_map/all_gather | solution.py:1125
  141.4 23.9 %collective-permute-start.6 = (bf16[2,256,512]{2,1,0:T(8,128)(2,1)}, bf16[2,256,512]{2,1,0:T(8,128)(2,1)S(1)}, u32[]{:S(2)}, u32[]{:S(2)}) collective-permute-start(bf16[2,256,512]{2,1,0:T(8,128)(2,1)} %get-tuple-element.163), channel_id=1, source_target_pairs={{0,1},{1,0},{2,3},{3,2},{4,5},{5,4},{6,7},{7,6},{8,9},{9,8},{10,11... | collective-permute-start | bytes 1572872 | tf_op jit(solution)/shard_map/ppermute | solution.py:26
  141.9 27.0 %all-to-all-start.3 = ((bf16[8,128,128]{2,1,0:T(8,128)(2,1)}), bf16[8,128,128]{2,1,0:T(8,128)(2,1)S(1)}, u32[]{:S(2)}, u32[]{:S(2)}) async-start(bf16[8,128,128]{2,1,0:T(8,128)(2,1)} %get-tuple-element.162.refs_2_), calls=%async_computation.3 | async-start | bytes 524288 | tf_op jit(solution)/shard_map/all_to_all | solution.py:48
  173.6 23.4 %all-to-all-start.5 = ((bf16[8,128,128]{2,1,0:T(8,128)(2,1)}), bf16[8,128,128]{2,1,0:T(8,128)(2,1)S(1)}, u32[]{:S(2)}, u32[]{:S(2)}) async-start(bf16[8,128,128]{2,1,0:T(8,128)(2,1)} %get-tuple-element.173), calls=%async_computation.5 | async-start | bytes 524288 | tf_op jit(solution)/shard_map/all_to_all | solution.py:48
  195.4 15.1 %collective-permute-start.9 = (bf16[256,1024]{1,0:T(8,128)(2,1)}, bf16[256,1024]{1,0:T(8,128)(2,1)S(1)}, u32[]{:S(2)}, u32[]{:S(2)}) collective-permute-start(bf16[256,1024]{1,0:T(8,128)(2,1)} %get-tuple-element.171.refs_0_), channel_id=1, source_target_pairs={{0,1},{1,0},{2,3},{3,2},{4,5},{5,4},{6,7},{7,6},{8,9},{9,8},{10,11... | collective-permute-start | bytes 1572872 | tf_op jit(solution)/shard_map/ppermute | solution.py:26
  200.2 18.9 %collective-permute-start.11 = (bf16[256,1024]{1,0:T(8,128)(2,1)}, bf16[256,1024]{1,0:T(8,128)(2,1)S(1)}, u32[]{:S(2)}, u32[]{:S(2)}) collective-permute-start(bf16[256,1024]{1,0:T(8,128)(2,1)} %get-tuple-element.174.own_ref), channel_id=1, source_target_pairs={{0,1},{1,0},{2,3},{3,2},{4,5},{5,4},{6,7},{7,6},{8,9},{9,8},{10,11... | collective-permute-start | bytes 1572872 | tf_op jit(solution)/shard_map/ppermute | solution.py:26
  215.4 30.2 %all-to-all-start.4 = ((bf16[8,128,256]{2,1,0:T(8,128)(2,1)}), bf16[8,128,256]{2,1,0:T(8,128)(2,1)S(1)}, u32[]{:S(2)}, u32[]{:S(2)}) async-start(bf16[8,128,256]{2,1,0:T(8,128)(2,1)} %get-tuple-element.172), calls=%async_computation.4 | async-start | bytes 1048576 | tf_op jit(solution)/shard_map/all_to_all | solution.py:48
  310.2 15.0 %collective-permute-start.15 = (bf16[256,1024]{1,0:T(8,128)(2,1)}, bf16[256,1024]{1,0:T(8,128)(2,1)S(1)}, u32[]{:S(2)}, u32[]{:S(2)}) collective-permute-start(bf16[256,1024]{1,0:T(8,128)(2,1)} %get-tuple-element.180.own_ref), channel_id=1, source_target_pairs={{0,1},{1,0},{2,3},{3,2},{4,5},{5,4},{6,7},{7,6},{8,9},{9,8},{10,11... | collective-permute-start | bytes 1572872 | tf_op jit(solution)/shard_map/ppermute | solution.py:26
  320.0 26.4 %collective-permute-start.16 = (bf16[256,1024]{1,0:T(8,128)(2,1)}, bf16[256,1024]{1,0:T(8,128)(2,1)S(1)}, u32[]{:S(2)}, u32[]{:S(2)}) collective-permute-start(bf16[256,1024]{1,0:T(8,128)(2,1)} %get-tuple-element.184.own_ref), channel_id=1, source_target_pairs={{0,1},{1,0},{2,3},{3,2},{4,5},{5,4},{6,7},{7,6},{8,9},{9,8},{10,11... | collective-permute-start | bytes 1572872 | tf_op jit(solution)/shard_map/ppermute | solution.py:26
  344.6 21.5 %collective-permute-start.19 = (bf16[256,1024]{1,0:T(8,128)(2,1)}, bf16[256,1024]{1,0:T(8,128)(2,1)S(1)}, u32[]{:S(2)}, u32[]{:S(2)}) collective-permute-start(bf16[256,1024]{1,0:T(8,128)(2,1)} %get-tuple-element.193.own_ref), channel_id=1, source_target_pairs={{0,1},{1,0},{2,3},{3,2},{4,5},{5,4},{6,7},{7,6},{8,9},{9,8},{10,11... | collective-permute-start | bytes 1572872 | tf_op jit(solution)/shard_map/ppermute | solution.py:26
  365.7 22.9 %collective-permute-start.21 = (bf16[256,1024]{1,0:T(8,128)(2,1)}, bf16[256,1024]{1,0:T(8,128)(2,1)S(1)}, u32[]{:S(2)}, u32[]{:S(2)}) collective-permute-start(bf16[256,1024]{1,0:T(8,128)(2,1)} %get-tuple-element.196.own_ref), channel_id=1, source_target_pairs={{0,1},{1,0},{2,3},{3,2},{4,5},{5,4},{6,7},{7,6},{8,9},{9,8},{10,11... | collective-permute-start | bytes 1572872 | tf_op jit(solution)/shard_map/ppermute | solution.py:26
  371.3 17.4 %all-to-all-start.9 = ((bf16[8,128,128]{2,1,0:T(8,128)(2,1)}), bf16[8,128,128]{2,1,0:T(8,128)(2,1)S(1)}, u32[]{:S(2)}, u32[]{:S(2)}) async-start(bf16[8,128,128]{2,1,0:T(8,128)(2,1)} %get-tuple-element.194), calls=%async_computation.9 | async-start | bytes 524288 | tf_op jit(solution)/shard_map/all_to_all | solution.py:48
  377.3 167.1 %reduce-scatter.3.cloned.1.call-start = ((), (), s32[]{:S(2)}) async-start(), calls=%async_computation.21 | async-start | bytes 10027008 | tf_op jit(solution)/shard_map/reduce_scatter | solution.py:1038
  481.1 17.7 %all-to-all-start.12 = ((bf16[8,128,256]{2,1,0:T(8,128)(2,1)}), bf16[8,128,256]{2,1,0:T(8,128)(2,1)S(1)}, u32[]{:S(2)}, u32[]{:S(2)}) async-start(bf16[8,128,256]{2,1,0:T(8,128)(2,1)} %get-tuple-element.230), calls=%async_computation.12 | async-start | bytes 1048576 | tf_op jit(solution)/shard_map/all_to_all | solution.py:48
  488.0 17.2 %collective-permute-start.24 = (bf16[256,1024]{1,0:T(8,128)(2,1)}, bf16[256,1024]{1,0:T(8,128)(2,1)S(1)}, u32[]{:S(2)}, u32[]{:S(2)}) collective-permute-start(bf16[256,1024]{1,0:T(8,128)(2,1)} %get-tuple-element.224.own_ref), channel_id=1, source_target_pairs={{0,1},{1,0},{2,3},{3,2},{4,5},{5,4},{6,7},{7,6},{8,9},{9,8},{10,11... | collective-permute-start | bytes 1572872 | tf_op jit(solution)/shard_map/ppermute | solution.py:26
  503.0 16.2 %collective-permute-start.26 = (bf16[256,1024]{1,0:T(8,128)(2,1)}, bf16[256,1024]{1,0:T(8,128)(2,1)S(1)}, u32[]{:S(2)}, u32[]{:S(2)}) collective-permute-start(bf16[256,1024]{1,0:T(8,128)(2,1)} %get-tuple-element.231.own_ref), channel_id=1, source_target_pairs={{0,1},{1,0},{2,3},{3,2},{4,5},{5,4},{6,7},{7,6},{8,9},{9,8},{10,11... | collective-permute-start | bytes 1572872 | tf_op jit(solution)/shard_map/ppermute | solution.py:26
  519.1 16.1 %collective-permute-start.25 = (bf16[256,1024]{1,0:T(8,128)(2,1)}, bf16[256,1024]{1,0:T(8,128)(2,1)S(1)}, u32[]{:S(2)}, u32[]{:S(2)}) collective-permute-start(bf16[256,1024]{1,0:T(8,128)(2,1)} %get-tuple-element.227.own_ref), channel_id=1, source_target_pairs={{0,1},{1,0},{2,3},{3,2},{4,5},{5,4},{6,7},{7,6},{8,9},{9,8},{10,11... | collective-permute-start | bytes 1572872 | tf_op jit(solution)/shard_map/ppermute | solution.py:26
  533.1 26.7 %collective-permute-start.27 = (bf16[256,1024]{1,0:T(8,128)(2,1)}, bf16[256,1024]{1,0:T(8,128)(2,1)S(1)}, u32[]{:S(2)}, u32[]{:S(2)}) collective-permute-start(bf16[256,1024]{1,0:T(8,128)(2,1)} %get-tuple-element.234.own_ref), channel_id=1, source_target_pairs={{0,1},{1,0},{2,3},{3,2},{4,5},{5,4},{6,7},{7,6},{8,9},{9,8},{10,11... | collective-permute-start | bytes 1572872 | tf_op jit(solution)/shard_map/ppermute | solution.py:26
  540.4 19.4 %all-to-all-start.13 = ((bf16[8,128,128]{2,1,0:T(8,128)(2,1)}), bf16[8,128,128]{2,1,0:T(8,128)(2,1)S(1)}, u32[]{:S(2)}, u32[]{:S(2)}) async-start(bf16[8,128,128]{2,1,0:T(8,128)(2,1)} %get-tuple-element.236), calls=%async_computation.13 | async-start | bytes 524288 | tf_op jit(solution)/shard_map/all_to_all | solution.py:48
  544.3 205.3 %reduce-scatter.5.cloned.1.call-start = ((), (), s32[]{:S(2)}) async-start(), calls=%async_computation.22 | async-start | bytes 12255232 | tf_op jit(solution)/shard_map/reduce_scatter | solution.py:1038
  652.6 25.0 %all-to-all-start.16 = ((bf16[8,128,256]{2,1,0:T(8,128)(2,1)}), bf16[8,128,256]{2,1,0:T(8,128)(2,1)S(1)}, u32[]{:S(2)}, u32[]{:S(2)}) async-start(bf16[8,128,256]{2,1,0:T(8,128)(2,1)} %get-tuple-element.273), calls=%async_computation.17 | async-start | bytes 1048576 | tf_op jit(solution)/shard_map/all_to_all | solution.py:48
  681.6 15.1 %collective-permute-start.32 = (bf16[256,1024]{1,0:T(8,128)(2,1)}, bf16[256,1024]{1,0:T(8,128)(2,1)S(1)}, u32[]{:S(2)}, u32[]{:S(2)}) collective-permute-start(bf16[256,1024]{1,0:T(8,128)(2,1)} %get-tuple-element.274.own_ref), channel_id=1, source_target_pairs={{0,1},{1,0},{2,3},{3,2},{4,5},{5,4},{6,7},{7,6},{8,9},{9,8},{10,11... | collective-permute-start | bytes 1572872 | tf_op jit(solution)/shard_map/ppermute | solution.py:26
  681.8 26.8 %collective-permute-start.18 = (bf16[256,1024]{1,0:T(8,128)(2,1)}, bf16[256,1024]{1,0:T(8,128)(2,1)}, u32[]{:S(2)}, u32[]{:S(2)}) collective-permute-start(bf16[256,1024]{1,0:T(8,128)(2,1)} %get-tuple-element.189.refs_4_), channel_id=1, source_target_pairs={{0,1},{1,0},{2,3},{3,2},{4,5},{5,4},{6,7},{7,6},{8,9},{9,8},{10,11... | collective-permute-start | bytes 1572872 | tf_op jit(solution)/shard_map/ppermute | solution.py:26
  683.7 33.2 %collective-permute-start.17 = (bf16[256,1024]{1,0:T(8,128)(2,1)S(1)}, bf16[256,1024]{1,0:T(8,128)(2,1)}, u32[]{:S(2)}, u32[]{:S(2)}) collective-permute-start(bf16[256,1024]{1,0:T(8,128)(2,1)S(1)} %copy-done.37), channel_id=1, source_target_pairs={{0,1},{1,0},{2,3},{3,2},{4,5},{5,4},{6,7},{7,6},{8,9},{9,8},{10,11... | collective-permute-start | bytes 1572872 | tf_op jit(solution)/shard_map/ppermute | solution.py:26
  689.3 32.6 %collective-permute-start.38 = (bf16[8,64,1024]{2,1,0:T(8,128)(2,1)S(1)}, bf16[8,64,1024]{2,1,0:T(8,128)(2,1)S(1)}, u32[]{:S(2)}, u32[]{:S(2)}) collective-permute-start(bf16[8,64,1024]{2,1,0:T(8,128)(2,1)S(1)} %dynamic-slice_bitcast_fusion), channel_id=1, source_target_pairs={{0,2},{2,0},{4,6},{6,4},{8,10},{10,8},{12,14},{14,12},{16,18},{18,... | collective-permute-start | bytes 3145736 | tf_op jit(solution)/shard_map/ppermute | solution.py:26
  704.1 16.2 %collective-permute-start.34 = (f32[2,10,512]{2,1,0:T(8,128)S(1)}, f32[2,10,512]{2,1,0:T(8,128)S(1)}, u32[]{:S(2)}, u32[]{:S(2)}) collective-permute-start(f32[2,10,512]{2,1,0:T(8,128)S(1)} %fusion.33), channel_id=1, source_target_pairs={{0,4},{2,6},{4,0},{6,2},{8,12},{10,14},{12,8},{14,10},{16,20},{18,... | collective-permute-start | bytes 122888 | tf_op jit(solution)/shard_map/ppermute | solution.py:26
  (102 other events, 641.7 us)
Sparse Core Ops, SparseCore 0:
  11.8 47.8 all-gather.2
  137.5 50.7 all-gather.4
  397.2 133.1 reduce-scatter.2
  568.3 148.9 reduce-scatter.4

commit v3 on v2

--- a/solution.py
+++ b/solution.py
@@ -17,8 +17,9 @@
 SCALE = HD ** (-0.5)
 VMEM_LIMIT = 56 * 1024 * 1024
 PAIRS = 8
+SHARE = 0.01
 CHUNKS = 2
-FFN_STEPS = 4
+FFN_STEPS = 2
 
 
 def swap(value, axis, mask):
@@ -414,7 +415,7 @@
 
 
 def cost(flops, moved):
-    return pl.CostEstimate(flops=int(flops), bytes_accessed=int(moved), transcendentals=0)
+    return pl.CostEstimate(flops=int(flops * SHARE), bytes_accessed=int(moved * SHARE), transcendentals=0)
 
 
 IN_SMEM = pl.BlockSpec(memory_space=pltpu.SMEM)
@@ -585,7 +586,7 @@
 
 
 def narrow_kernel(layer, pos_ref, *refs):
-    refs, out_ref = refs[:-1], refs[-1]
+    out_ref = refs[-1]
     seqs, rows, half = out_ref.shape
     count = rows // CHUNKS
     lanes = pl.ds(pl.multiple_of(pos_ref[1] * half, half), half)
@@ -594,23 +595,26 @@
             at = slice(seq * count, (seq + 1) * count)
             value = refs[q][at, lanes]
             if layer is not None:
-                own, other = refs[CHUNKS + 2 * q : CHUNKS + 2 * q + 2]
-                value = value + (own[at, lanes].astype(F32) + other[at, lanes].astype(F32))
-                value = value + refs[-1][layer : layer + 1, lanes]
+                own, other, bias = refs[CHUNKS + q], refs[2 * CHUNKS], refs[2 * CHUNKS + 1]
+                got = other[q * seqs * count + seq * count : q * seqs * count + (seq + 1) * count]
+                value = value + (own[at, lanes].astype(F32) + got.astype(F32))
+                value = value + bias[layer : layer + 1, lanes]
             out_ref[seq, q * count : (q + 1) * count] = value
 
 
-def narrow_chunks(pos, chunks, seqs, layer=None, parts=()):
+def narrow_chunks(pos, chunks, seqs, layer=None, parts=(), after=()):
     toks, width = chunks[0].shape
     return pl.pallas_call(
         functools.partial(narrow_kernel, layer),
         out_shape=f32_out(seqs, toks * CHUNKS // seqs, width // 2),
-        in_specs=[IN_SMEM] + [IN_VMEM] * (CHUNKS + len(parts)),
+        in_specs=[IN_SMEM]
+        + [IN_VMEM] * (CHUNKS + len(parts))
+        + [ANYWHERE] * len(after),
         out_specs=IN_VMEM,
         compiler_params=params(),
         cost_estimate=cost(1e6, 4e6),
         name="narrow_chunks",
-    )(pos, *chunks, *parts)
+    )(pos, *chunks, *parts, *after)
 
 
 def enter_kernel(
@@ -691,7 +695,8 @@
     return lse[:, :HD], lse[:, HD:]
 
 
-def combine_kernel(own_ref, got_ref, attn_ref, stats_ref, *out_refs):
+def combine_kernel(after, own_ref, got_ref, *refs):
+    attn_ref, stats_ref, *out_refs = refs[after:]
     chunks, slots, rows, _ = own_ref.shape
     for q in range(chunks):
         for k in range(slots):
@@ -710,18 +715,18 @@
             out_refs[q][k] = value.astype(BF16)
 
 
-def combine_cores(own, got):
+def combine_cores(own, got, after=()):
     chunks, slots, rows, _ = own.shape
     results = pl.pallas_call(
-        combine_kernel,
+        functools.partial(combine_kernel, len(after)),
         out_shape=[f32_out(chunks, slots, rows, HD), bf16_out(chunks, slots, rows, HD)]
         + [bf16_out(slots, rows, HD)] * chunks,
-        in_specs=[IN_VMEM] * 2,
+        in_specs=[IN_VMEM] * 2 + [ANYWHERE] * len(after),
         out_specs=[IN_VMEM] * (2 + chunks),
         compiler_params=params(),
         cost_estimate=cost(1e8, 5e6),
         name="combine_cores",
-    )(own, got)
+    )(own, got, *after)
     return results[0], results[1], results[2:]
 
 
@@ -751,29 +756,30 @@
     )(attn, stats, units, *after)
 
 
-def add_kernel(own_ref, got_ref, *out_refs):
-    for q, out_ref in enumerate(out_refs):
+def add_kernel(after, own_ref, got_ref, *refs):
+    for q, out_ref in enumerate(refs[after:]):
         total = own_ref[q].astype(F32) + got_ref[q].astype(F32)
         out_ref[...] = total.astype(BF16)
 
 
-def add_cores(own, got):
+def add_cores(own, got, after=()):
     chunks, slots, rows, width = own.shape
     return pl.pallas_call(
-        add_kernel,
+        functools.partial(add_kernel, len(after)),
         out_shape=[bf16_out(slots, rows, width)] * chunks,
-        in_specs=[IN_VMEM] * 2,
+        in_specs=[IN_VMEM] * 2 + [ANYWHERE] * len(after),
         out_specs=[IN_VMEM] * chunks,
         compiler_params=params(),
         cost_estimate=cost(1e6, 3e6),
         name="add_cores",
-    )(own, got)
+    )(own, got, *after)
 
 
 def ffn_kernel(
     layer, stream_ref, own_ref, other_ref, bias_ref, gain_ref, shift_ref, up_ref, up_bias_ref,
-    down_ref, new_ref, normed_ref, pre_ref, part_ref, acc,
+    down_ref, *refs,
 ):
+    new_ref, normed_ref, pre_ref, part_ref, acc = refs[-5:]
     step = pl.program_id(0)
     row = slice(layer, layer + 1)
 
@@ -802,7 +808,7 @@
         part_ref[...] = acc[...].astype(BF16)
 
 
-def feed_forward(layer, stream, own, other, bias, gain, shift, up, up_bias, down):
+def feed_forward(layer, stream, own, other, bias, gain, shift, up, up_bias, down, after=()):
     toks, width = stream.shape
     hidden = up.shape[2]
     step = hidden // FFN_STEPS
@@ -817,13 +823,14 @@
         in_specs=[
             full, full, full, whole_block(bias), whole_block(gain), whole_block(shift), slab,
             pl.BlockSpec((LAYERS, step), lambda i: (0, i)), slab,
-        ],
+        ]
+        + [ANYWHERE] * len(after),
         out_specs=(full, full, pl.BlockSpec((toks, step), lambda i: (0, i)), full),
         scratch_shapes=[pltpu.VMEM((toks, width), F32)],
         compiler_params=params(),
         cost_estimate=cost(4 * toks * width * hidden, 14e6),
         name="feed_forward",
-    )(stream, own, other, bias, gain, shift, up, up_bias, down)
+    )(stream, own, other, bias, gain, shift, up, up_bias, down, *after)
 
 
 def ffn_back_kernel(
@@ -992,25 +999,24 @@
     )(*operands, weight, *after)
 
 
-def finish_kernel(
-    layer, stream_ref, own_ref, other_ref, grad_ref, gain_ref, new_ref, gain_out, shift_out
-):
+def finish_kernel(layer, stream_ref, own_ref, other_ref, grad_ref, gain_ref, *refs):
+    new_ref, gain_out, shift_out = refs[-3:]
     new_ref[...] = norm_back(
         layer, stream_ref, own_ref, other_ref, grad_ref, gain_ref, gain_out, shift_out
     )
 
 
-def finish_attention(layer, stream, own, other, grad, gain):
+def finish_attention(layer, stream, own, other, grad, gain, after=()):
     toks, width = stream.shape
     return pl.pallas_call(
         functools.partial(finish_kernel, layer),
         out_shape=(f32_out(toks, width), f32_out(1, width), f32_out(1, width)),
-        in_specs=[IN_VMEM] * 5,
+        in_specs=[IN_VMEM] * 5 + [ANYWHERE] * len(after),
         out_specs=(IN_VMEM,) * 3,
         compiler_params=params(),
         cost_estimate=cost(1e7, 4e6),
         name="finish_attention",
-    )(stream, own, other, grad, gain)
+    )(stream, own, other, grad, gain, *after)
 
 
 def reduce_rows(value):
@@ -1019,6 +1025,7 @@
     width = value.shape[1]
     block = value.shape[0] // count
     value = value.astype(BF16)
+    stages = []
     bit = 1
     parts = count
     while bit < count:
@@ -1031,7 +1038,8 @@
         bit *= 2
         if bit < count:
             value = value.astype(BF16)
-    return value.reshape(block, width)
+        stages.append(value)
+    return stages[:-1] + [value.reshape(block, width)]
 
 
 def sum_rows(value, widths):
@@ -1072,13 +1080,9 @@
         pair = pair.reshape(weight_rows, 2, heads, HD)
         return jnp.transpose(pair, (0, 2, 1, 3)).reshape(weight_rows, 2 * head_width)
 
-    def widen(streams, after):
-        return [
-            widen_chunks(pos, stream, swap(sent, "narrow", 1))
-            for stream, sent in zip(streams, lower_arrays(streams, after))
-        ]
-
-    second, first = widen((second_in, first_in), [])
+    streams = (second_in, first_in, second_cot, first_cot)
+    others = [swap(sent, "narrow", 1) for sent in lower_arrays(streams, ())]
+    second, first = [widen_chunks(pos, streams[k], others[k]) for k in range(2)]
     early = lax.all_gather(
         jnp.concatenate([flat_weight(0), out_weight[0]], axis=1), "wide", axis=0, tiled=True
     )
@@ -1103,13 +1107,13 @@
 
     saved = []
     ffn_parts = [() for _ in chunks]
-    afters = [[], [*tables, *first, out_bias, down_bias]]
+    afters = [[], [*tables, *first, *others[2:], out_bias, down_bias]]
     for layer in range(LAYERS):
         normed, sources = [], []
         for q in chunks:
             second[q], normed_q, units = enter_attention(
                 seqs, layer, second[q], attn_norm_gain, attn_norm_bias, gathered[layer], 0,
-                unit_columns, ffn_parts[q], afters[min(q, 1)] if layer == 0 else (),
+                unit_columns, ffn_parts[q], afters[min(q, 1)],
             )
             normed.append(normed_q)
             own = chip_exchange(units)
@@ -1118,29 +1122,43 @@
         attn, stats, units = combine_cores(own, swap(sib, "wide", 1))
         after = []
         if layer == 0:
-            grad_second, grad_first = widen((second_cot, first_cot), sources[-2:-1])
+            grad_second, grad_first = [
+                widen_chunks(pos, streams[k], others[k]) for k in range(2, 4)
+            ]
             after = [*grad_second, *grad_first]
         if layer + 1 < LAYERS:
             pieces = pack_columns([flat_weight(layer + 1), out_weight[layer + 1]], units[:1])
             gathered.append(lax.all_gather(pieces, "wide", axis=0, tiled=True))
         second_now, attn_tok, ffn_in, pre_act = list(second), [], [], []
         backs = [chip_exchange(units[q]) for q in chunks]
+        merged = []
         for q in chunks:
-            part, attn_tok_q = merge_units(seqs, backs[q], gathered[layer], 2, after)
+            part, attn_tok_q = merge_units(
+                seqs, backs[q], gathered[layer], 2, after + attn_tok if q > 0 else ()
+            )
             attn_tok.append(attn_tok_q)
+            merged.append((part, swap(part, "narrow", 1)))
+        for q in chunks:
             first[q], ffn_in_q, pre_q, part = feed_forward(
-                layer, first[q], part, swap(part, "narrow", 1), out_bias,
-                ffn_norm_gain, ffn_norm_bias, up_weight, up_bias, down_weight,
+                layer, first[q], *merged[q], out_bias, ffn_norm_gain, ffn_norm_bias,
+                up_weight, up_bias, down_weight, attn_tok[1:] + ffn_in,
             )
             ffn_in.append(ffn_in_q)
             pre_act.append(pre_q)
-            ffn_parts[q] = (part, swap(part, "narrow", 1), down_bias)
+            if layer + 1 < LAYERS:
+                ffn_parts[q] = (part, swap(part, "narrow", 1), down_bias)
+            else:
+                ffn_parts[q] = part
+        afters = [ffn_in[1:], []]
         saved.append((second_now, normed, sorted_rows, attn, stats, attn_tok, list(first), ffn_in, pre_act))
     first_out = narrow_chunks(pos, first, seqs)
-    last_parts = [part for q in chunks for part in ffn_parts[q][:2]] + [down_bias]
-    second_out = narrow_chunks(pos, second, seqs, LAYERS - 1, last_parts)
-
-    summed, waiting, done = [], [], []
+    sent = [
+        lax.dynamic_slice_in_dim(part, (1 - narrow_index) * half, half, 1) for part in ffn_parts
+    ]
+    got = swap(jnp.concatenate(sent), "narrow", 1)
+    second_out = narrow_chunks(pos, second, seqs, LAYERS - 1, [*ffn_parts, got, down_bias])
+    summed, waiting = [], []
+    done = []
     small_grads = [None] * LAYERS
     after = []
     for layer in reversed(range(LAYERS)):
@@ -1160,13 +1178,16 @@
         pairs = waiting + [(ffn_in, low), (branch, hidden)]
         widths = [right[0].shape[1] for _, right in pairs]
         columns = sum(widths) + head_width
-        products = weight_products(pairs, columns, after=done)
+        if layer == 0:
+            products = [weight_products(pairs, columns)]
+        else:
+            products = []
         out_low, units = [], []
         ffn_gain_grad, ffn_bias_grad, out_bias_grad = 0.0, 0.0, 0.0
         for q in chunks:
             *results, units_q = leave_ffn(
                 seqs, layer, first_l[q], *parts[q], grad_first[q], ffn_norm_gain,
-                gathered[layer], 2, head_width, [*units, products] if q > 0 else (),
+                gathered[layer], 2, head_width, [*units, *products] if q > 0 else (),
             )
             grad_first[q] = results[0]
             out_low.append(results[1])
@@ -1174,13 +1195,14 @@
             ffn_bias_grad += results[3]
             out_bias_grad += results[4]
             units.append(chip_exchange(units_q))
-        products = weight_products(
-            [(out_low, attn_tok)], columns, columns - head_width, products
-        )
-        summed += sum_rows(products, widths + [head_width])
+        if layer == 0:
+            products = [
+                weight_products([(out_low, attn_tok)], columns, columns - head_width, *products)
+            ]
+            summed += sum_rows(*products, widths + [head_width])
         sources = []
         for q in chunks:
-            own = join_grads(q, attn, stats, units[q], [products] if q > 0 else ())
+            own = join_grads(q, attn, stats, units[q], products if q > 0 else ())
             sources += [own, swap(own, "wide", 1)]
         early_small = jnp.concatenate(
             [
@@ -1190,24 +1212,36 @@
             + [up_bias_grad.reshape(-1, half)]
         )
         own, sib = attention_backward(pos, sources, sorted_rows, tables, [early_small])
-        units = add_cores(own, swap(sib, "wide", 1))
+        units = add_cores(own, swap(sib, "wide", 1), done)
         grad_tok, attn_gain_grad, attn_bias_grad = [], 0.0, 0.0
         backs = [chip_exchange(units[q]) for q in chunks]
+        after = []
+        if layer > 0:
+            pairs.append((out_low, attn_tok))
+        merged = []
         for q in chunks:
-            part, grad_tok_q = merge_units(
-                seqs, backs[q], gathered[layer], 0, grad_second[:1] if q > 0 and layer == 0 else ()
-            )
+            part, grad_tok_q = merge_units(seqs, backs[q], gathered[layer], 0, after + grad_tok)
+            if layer > 0 and q == 0:
+                products = weight_products(pairs, columns, after=[grad_tok_q])
+                summed += sum_rows(products, widths + [head_width])
+                after = [products]
             grad_tok.append(grad_tok_q)
+            merged.append((part, swap(part, "narrow", 1)))
+        waiting = [(normed, grad_tok)]
+        stages = [None]
+        if layer == 0:
+            stages = reduce_rows(weight_products(waiting, unit_columns))
+            summed.append(stages[-1])
+        for q in chunks:
             grad_second[q], gain_q, shift_q = finish_attention(
-                layer, second_l[q], part, swap(part, "narrow", 1), grad_second[q], attn_norm_gain
+                layer, second_l[q], *merged[q], grad_second[q], attn_norm_gain,
+                stages[q + 1 : q + 2] if layer == 0 else (),
             )
             attn_gain_grad += gain_q
             attn_bias_grad += shift_q
-        waiting = [(normed, grad_tok)]
         done = summed[-1:]
         late_small = jnp.concatenate([own_half(attn_gain_grad), own_half(attn_bias_grad)])
         small_grads[layer] = jnp.concatenate([late_small, early_small])
-    summed.append(reduce_rows(weight_products(waiting, unit_columns)))
     first_grad = narrow_chunks(pos, grad_first, seqs)
     second_grad = narrow_chunks(pos, grad_second, seqs)
 

time: 774 us -> 769 us (level)
  waiting for transfers between devices: 176 us -> 210 us
  starting transfers between devices: 104 us -> 86.6 us
  blocking collectives: 83.2 us -> 68.7 us
  Pallas kernels: 317 us -> 308 us
    all_to_all x13 -> x12, waiting for transfers between devices: 49.9 us -> 97.3 us  [chip_exchange(): lax.all_to_all(units, 'wide', 0, 0, tiled=True, axis_index_groups=groups)]
    ppermute x42 -> x41, starting transfers between devices: 40.3 us -> 25.6 us  [swap(): lax.ppermute(value, axis, [(source, source ^ mask) for source in range(co...]
    all_to_all x3 -> x4, blocking collectives: 83.2 us -> 68.7 us  [chip_exchange(): lax.all_to_all(units, 'wide', 0, 0, tiled=True, axis_index_groups=groups)]
    ppermute x42 -> x41, waiting for transfers between devices: 120 us -> 109 us  [swap(): lax.ppermute(value, axis, [(source, source ^ mask) for source in range(co...]
    all_to_all x13 -> x12, starting transfers between devices: 57.5 us -> 54.3 us  [chip_exchange(): lax.all_to_all(units, 'wide', 0, 0, tiled=True, axis_index_groups=groups)]
    unnamed x156 -> x164, local copies, waits for them, and re-layouts: 31.1 us -> 28.6 us
    pallas_call x5 -> x4, Pallas kernels: 35.6 us -> 34.5 us  [weight_products(): pl.pallas_call(functools.partial(products_kernel, counts), grid=(start,),...]
  transfers between devices with their start and end apart: 60 -> 58, of which waited for: 33 -> 33; matrix products, arithmetic and copies ran while one was open for 4% -> 4% of each run, Pallas kernels for 33% -> 28%
where the time goes in v3:
time: 769 us; the launch traced here: 759 us
  Pallas kernels  308 us (40%)
  waiting for transfers between devices  210 us (27%)
  starting transfers between devices  86.6 us (11%)
  blocking collectives  68.7 us (9%)
  local copies, waits for them, and re-layouts  43.8 us (6%)
  other arithmetic  24.7 us (3%)
  between operations  15.2 us (2%)
    ppermute x41, waiting for transfers between devices, swap(): lax.ppermute(value, axis, [(source, source ^ mask) for source in range(co...  109 us
    all_to_all x12, waiting for transfers between devices, chip_exchange(): lax.all_to_all(units, 'wide', 0, 0, tiled=True, axis_index_groups=groups)  97.3 us
    all_to_all x4, blocking collectives, chip_exchange(): lax.all_to_all(units, 'wide', 0, 0, tiled=True, axis_index_groups=groups)  68.7 us
    all_to_all x12, starting transfers between devices, chip_exchange(): lax.all_to_all(units, 'wide', 0, 0, tiled=True, axis_index_groups=groups)  54.3 us
    pallas_call x2, Pallas kernels, attention_backward(): pl.pallas_call(functools.partial(backward_kernel, chunks, len(after)), ou...  42.6 us
    pallas_call x2, Pallas kernels, attention_forward(): pl.pallas_call(functools.partial(forward_kernel, chunks, len(after)), out...  38.4 us
    pallas_call x4, Pallas kernels, feed_back(): pl.pallas_call(ffn_back_kernel, grid=(FFN_STEPS,), out_shape=(bf16_out(to...  38.4 us
    pallas_call x4, Pallas kernels, weight_products(): pl.pallas_call(functools.partial(products_kernel, counts), grid=(start,),...  34.5 us
  transfers between devices with their start and end apart: 58, of which 33 were waited for; matrix products, arithmetic and copies ran while one was open for 4% of the time, Pallas kernels for 28%

profile of v3, /device:TPU:0, one launch (start us, length us, event | category | flops | bytes accessed | tf_op | source)
XLA Modules:
  0.0 759.0 jit_solution(1115678124053616230)
XLA Ops:
  33.6 18.8 %collective-permute-done.1.other_ref = bf16[2,256,512]{2,1,0:T(8,128)(2,1)S(1)} collective-permute-done((bf16[2,256,512]{2,1,0:T(8,128)(2,1)}, bf16[2,256,512]{2,1,0:T(8,128)(2,1)S(1)}, u32[]{:S(2)}, u32[]{:S(2)}) %collective-permute-start.1) | collective-permute-done | bytes 524320 | tf_op jit(solution)/shard_map/ppermute | solution.py:27
  86.2 5.9 all-to-all-start.2
  92.4 14.3 %all-to-all-done.2.refs_2_ = bf16[8,128,256]{2,1,0:T(8,128)(2,1)S(1)} async-done(((bf16[8,128,256]{2,1,0:T(8,128)(2,1)}), bf16[8,128,256]{2,1,0:T(8,128)(2,1)S(1)}, u32[]{:S(2)}, u32[]{:S(2)}) %all-to-all-start.2) | async-done | bytes 524320 | tf_op jit(solution)/shard_map/all_to_all | solution.py:49
  109.4 19.2 %attend_forward.2 = (bf16[2,4096,256]{2,1,0:T(8,128)(2,1)}, bf16[2,8,128,256]{3,2,1,0:T(8,128)(2,1)}, bf16[2,8,128,256]{3,2,1,0:T(8,128)(2,1)}) custom-call(s32[2]{0:T(128)} %pad_add_fusion.pos_ref, bf16[8,128,256]{2,1,0:T(8,128)(2,1)} %copy-done.7, bf16[8,128,256]{2,1,0:T(8,128)(2,1)} %copy-done.38, bf16[8,128,256]{2,1,0:T(8,128)(2,1)} %copy-done.9, ...), custom_call_target="tpu_custom_call" | custom-call | flops 160000000 | bytes 240000 | tf_op jit(solution)/shard_map/attend_forward/pallas_call | solution.py:449
  138.3 16.0 %all_to_all.85.in_ref = bf16[8,128,128]{2,1,0:T(8,128)(2,1)} all-to-all(bf16[8,128,128]{2,1,0:T(8,128)(2,1)} %get-tuple-element.164.refs_2_), channel_id=1, replica_groups={{0,4,8,12,16,20,24,28},{2,6,10,14,18,22,26,30},{1,5,9,13,17,21,25,29},{..., dimensions={0} | all-to-all | bytes 524288 | tf_op jit(solution)/shard_map/all_to_all | solution.py:49
  176.1 8.1 %feed_forward.4 = (f32[256,1024]{1,0:T(8,128)}, bf16[256,1024]{1,0:T(8,128)(2,1)}, f32[256,2048]{1,0:T(8,128)}, bf16[256,1024]{1,0:T(8,128)(2,1)}) custom-call(f32[256,1024]{1,0:T(8,128)} %get-tuple-element.153.refs_4_.stream_ref, bf16[256,1024]{1,0:T(8,128)(2,1)} %get-tuple-element.165.own_ref, bf16[256,1024]{1,0:T(8,128)(2,1)} %copy-done.32, ...), custom_call_target="tpu_custom_call" | custom-call | flops 21474836 | bytes 140000 | tf_op jit(solution)/shard_map/feed_forward/pallas_call | solution.py:817
  186.2 8.0 %feed_forward.5 = (f32[256,1024]{1,0:T(8,128)}, bf16[256,1024]{1,0:T(8,128)(2,1)}, f32[256,2048]{1,0:T(8,128)}, bf16[256,1024]{1,0:T(8,128)(2,1)}) custom-call(f32[256,1024]{1,0:T(8,128)} %get-tuple-element.158.refs_5_.stream_ref, bf16[256,1024]{1,0:T(8,128)(2,1)} %get-tuple-element.175.own_ref, bf16[256,1024]{1,0:T(8,128)(2,1)} %copy-done.37, ...), custom_call_target="tpu_custom_call" | custom-call | flops 21474836 | bytes 140000 | tf_op jit(solution)/shard_map/feed_forward/pallas_call | solution.py:817
  195.8 11.5 %collective-permute-done.12.refs_1_ = bf16[256,1024]{1,0:T(8,128)(2,1)S(1)} collective-permute-done((bf16[256,1024]{1,0:T(8,128)(2,1)}, bf16[256,1024]{1,0:T(8,128)(2,1)S(1)}, u32[]{:S(2)}, u32[]{:S(2)}) %collective-permute-start.12) | collective-permute-done | bytes 524320 | tf_op jit(solution)/shard_map/ppermute | solution.py:27
  218.8 10.6 %collective-permute-done.9.refs_1_ = bf16[256,1024]{1,0:T(8,128)(2,1)S(1)} collective-permute-done((bf16[256,1024]{1,0:T(8,128)(2,1)S(1)}, bf16[256,1024]{1,0:T(8,128)(2,1)S(1)}, u32[]{:S(2)}, u32[]{:S(2)}) %collective-permute-start.9) | collective-permute-done | bytes 524320 | tf_op jit(solution)/shard_map/ppermute | solution.py:27
  234.2 6.0 all-to-all-start.5
  240.4 10.7 %all-to-all-done.5.refs_0_ = bf16[8,128,256]{2,1,0:T(8,128)(2,1)S(1)} async-done(((bf16[8,128,256]{2,1,0:T(8,128)(2,1)}), bf16[8,128,256]{2,1,0:T(8,128)(2,1)S(1)}, u32[]{:S(2)}, u32[]{:S(2)}) %all-to-all-start.5) | async-done | bytes 524320 | tf_op jit(solution)/shard_map/all_to_all | solution.py:49
  253.8 19.2 %attend_forward.3 = (bf16[2,4096,256]{2,1,0:T(8,128)(2,1)}, bf16[2,8,128,256]{3,2,1,0:T(8,128)(2,1)}, bf16[2,8,128,256]{3,2,1,0:T(8,128)(2,1)}) custom-call(s32[2]{0:T(128)} %pad_add_fusion.pos_ref, bf16[8,128,256]{2,1,0:T(8,128)(2,1)} %copy-done.10, bf16[8,128,256]{2,1,0:T(8,128)(2,1)} %copy-done.41, bf16[8,128,256]{2,1,0:T(8,128)(2,1)} %copy-done.8, ...), custom_call_target="tpu_custom_call" | custom-call | flops 160000000 | bytes 240000 | tf_op jit(solution)/shard_map/attend_forward/pallas_call | solution.py:449
  281.0 13.5 %all_to_all.86.in_ref = bf16[8,128,128]{2,1,0:T(8,128)(2,1)} all-to-all(bf16[8,128,128]{2,1,0:T(8,128)(2,1)} %get-tuple-element.183), channel_id=1, replica_groups={{0,4,8,12,16,20,24,28},{2,6,10,14,18,22,26,30},{1,5,9,13,17,21,25,29},{..., dimensions={0} | all-to-all | bytes 524288 | tf_op jit(solution)/shard_map/all_to_all | solution.py:49
  300.7 6.5 all-to-all-done.8.in_ref
  316.5 8.0 %feed_forward.6 = (f32[256,1024]{1,0:T(8,128)}, bf16[256,1024]{1,0:T(8,128)(2,1)}, f32[256,2048]{1,0:T(8,128)}, bf16[256,1024]{1,0:T(8,128)(2,1)}) custom-call(f32[256,1024]{1,0:T(8,128)} %get-tuple-element.173.stream_ref, bf16[256,1024]{1,0:T(8,128)(2,1)} %get-tuple-element.184.own_ref, bf16[256,1024]{1,0:T(8,128)(2,1)} %copy-done.36, ...), custom_call_target="tpu_custom_call" | custom-call | flops 21474836 | bytes 140000 | tf_op jit(solution)/shard_map/feed_forward/pallas_call | solution.py:817
  324.5 9.2 %feed_back.4 = (bf16[256,1024]{1,0:T(8,128)(2,1)}, bf16[256,2048]{1,0:T(8,128)(2,1)}, bf16[256,2048]{1,0:T(8,128)(2,1)}, f32[1,1024]{1,0:T(1,128)}, f32[1,2048]{1,0:T(1,128)}, /*index=5*/bf16[256,1024]{1,0:T(8,128)(2,1)}) custom-call(f32[256,1024]{1,0:T(8,128)} %get-tuple-element.167.refs_0_.grad_ref, bf16[2,1024,2048]{2,1,0:T(8,128)(2,1)} %up_ref.15, ...), custom_call_target="tpu_custom_call" | custom-call | flops 21474836 | bytes 150000 | tf_op jit(solution)/shard_map/feed_back/pallas_call | solution.py:882
  334.6 8.0 %feed_forward.7 = (f32[256,1024]{1,0:T(8,128)}, bf16[256,1024]{1,0:T(8,128)(2,1)}, f32[256,2048]{1,0:T(8,128)}, bf16[256,1024]{1,0:T(8,128)(2,1)}) custom-call(f32[256,1024]{1,0:T(8,128)} %get-tuple-element.189.stream_ref, bf16[256,1024]{1,0:T(8,128)(2,1)} %get-tuple-element.190.own_ref, bf16[256,1024]{1,0:T(8,128)(2,1)} %copy-done.35, ...), custom_call_target="tpu_custom_call" | custom-call | flops 21474836 | bytes 140000 | tf_op jit(solution)/shard_map/feed_forward/pallas_call | solution.py:817
  342.6 9.2 %feed_back.5 = (bf16[256,1024]{1,0:T(8,128)(2,1)}, bf16[256,2048]{1,0:T(8,128)(2,1)}, bf16[256,2048]{1,0:T(8,128)(2,1)}, f32[1,1024]{1,0:T(1,128)}, f32[1,2048]{1,0:T(1,128)}, /*index=5*/bf16[256,1024]{1,0:T(8,128)(2,1)}) custom-call(f32[256,1024]{1,0:T(8,128)} %get-tuple-element.168.refs_1_.grad_ref, bf16[2,1024,2048]{2,1,0:T(8,128)(2,1)} %up_ref.15, ...), custom_call_target="tpu_custom_call" | custom-call | flops 21474836 | bytes 150000 | tf_op jit(solution)/shard_map/feed_back/pallas_call | solution.py:882
  359.1 6.0 all-to-all-start.9
  365.1 8.2 %all-to-all-done.9.in_ref.refs_0_ = bf16[8,128,128]{2,1,0:T(8,128)(2,1)S(1)} async-done(((bf16[8,128,128]{2,1,0:T(8,128)(2,1)}), bf16[8,128,128]{2,1,0:T(8,128)(2,1)S(1)}, u32[]{:S(2)}, u32[]{:S(2)}) %all-to-all-start.9) | async-done | bytes 262176 | tf_op jit(solution)/shard_map/all_to_all | solution.py:49
  396.2 21.2 %attend_backward.2 = (bf16[2,8,128,256]{3,2,1,0:T(8,128)(2,1)}, bf16[2,8,128,256]{3,2,1,0:T(8,128)(2,1)}) custom-call(s32[2]{0:T(128)} %pad_add_fusion.pos_ref, bf16[8,128,256]{2,1,0:T(8,128)(2,1)} %join_grads.4.refs_0_, bf16[8,128,256]{2,1,0:T(8,128)(2,1)} %copy-done.27, bf16[8,128,256]{2,1,0:T(8,128)(2,1)} %join_grads.5.refs_2_, ...), custom_call_target="tpu_custom_call" | custom-call | flops 180000000 | bytes 260000 | tf_op jit(solution)/shard_map/attend_backward/pallas_call | solution.py:479
  424.0 19.2 %all_to_all.87.in_ref = bf16[8,128,256]{2,1,0:T(8,128)(2,1)} all-to-all(bf16[8,128,256]{2,1,0:T(8,128)(2,1)} %get-tuple-element.218), channel_id=1, replica_groups={{0,4,8,12,16,20,24,28},{2,6,10,14,18,22,26,30},{1,5,9,13,17,21,25,29},{..., dimensions={0} | all-to-all | bytes 1048576 | tf_op jit(solution)/shard_map/all_to_all | solution.py:49
  446.4 13.0 %weight_products.4.refs_0_ = bf16[1024,4608]{1,0:T(8,128)(2,1)} custom-call(bf16[256,1024]{1,0:T(8,128)(2,1)} %get-tuple-element.191.refs_1_.refs_0_, bf16[256,1024]{1,0:T(8,128)(2,1)} %get-tuple-element.226.refs_1_, bf16[256,2048]{1,0:T(8,128)(2,1)} %get-tuple-element.227.refs_2_, bf16[256,2048]{1,0:T(8,128)(2,1)} %get-tuple-element.228.refs_3_, ...), custom_call_target="tpu_custom_call" | custom-call | flops 48318384 | bytes 200000 | tf_op jit(solution)/shard_map/weight_products/pallas_call | solution.py:940
  463.3 14.6 %all-to-all-done.12.in_ref = bf16[8,128,256]{2,1,0:T(8,128)(2,1)S(1)} async-done(((bf16[8,128,256]{2,1,0:T(8,128)(2,1)}), bf16[8,128,256]{2,1,0:T(8,128)(2,1)S(1)}, u32[]{:S(2)}, u32[]{:S(2)}) %all-to-all-start.12) | async-done | bytes 524320 | tf_op jit(solution)/shard_map/all_to_all | solution.py:49
  486.6 10.3 %feed_back.6 = (bf16[256,1024]{1,0:T(8,128)(2,1)}, bf16[256,2048]{1,0:T(8,128)(2,1)}, bf16[256,2048]{1,0:T(8,128)(2,1)}, f32[1,1024]{1,0:T(1,128)}, f32[1,2048]{1,0:T(1,128)}, /*index=5*/bf16[256,1024]{1,0:T(8,128)(2,1)}) custom-call(f32[256,1024]{1,0:T(8,128)} %get-tuple-element.220.grad_ref, bf16[2,1024,2048]{2,1,0:T(8,128)(2,1)} %up_ref.15, ...), custom_call_target="tpu_custom_call" | custom-call | flops 21474836 | bytes 150000 | tf_op jit(solution)/shard_map/feed_back/pallas_call | solution.py:882
  503.5 9.6 %feed_back.7 = (bf16[256,1024]{1,0:T(8,128)(2,1)}, bf16[256,2048]{1,0:T(8,128)(2,1)}, bf16[256,2048]{1,0:T(8,128)(2,1)}, f32[1,1024]{1,0:T(1,128)}, f32[1,2048]{1,0:T(1,128)}, /*index=5*/bf16[256,1024]{1,0:T(8,128)(2,1)}) custom-call(f32[256,1024]{1,0:T(8,128)} %get-tuple-element.237.grad_ref, bf16[2,1024,2048]{2,1,0:T(8,128)(2,1)} %up_ref.15, ...), custom_call_target="tpu_custom_call" | custom-call | flops 21474836 | bytes 150000 | tf_op jit(solution)/shard_map/feed_back/pallas_call | solution.py:882
  521.9 14.2 %weight_products.5.refs_1_.refs_4_ = bf16[1024,5632]{1,0:T(8,128)(2,1)} custom-call(bf16[256,1024]{1,0:T(8,128)(2,1)} %get-tuple-element.242.refs_0_, bf16[256,1024]{1,0:T(8,128)(2,1)} %get-tuple-element.243.refs_1_, bf16[256,1024]{1,0:T(8,128)(2,1)} %get-tuple-element.235.refs_12_.refs_1_.refs_2_, bf16[256,1024]{1,0:T(8,128)(2,1)} %get-tuple-element.244.refs_3_, ...), custom_call_target="tpu_custom_call" | custom-call | flops 53687092 | bytes 200000 | tf_op jit(solution)/shard_map/weight_products/pallas_call | solution.py:940
  553.1 10.9 %all-to-all-done.14.in_ref = bf16[8,128,128]{2,1,0:T(8,128)(2,1)S(1)} async-done(((bf16[8,128,128]{2,1,0:T(8,128)(2,1)}), bf16[8,128,128]{2,1,0:T(8,128)(2,1)S(1)}, u32[]{:S(2)}, u32[]{:S(2)}) %all-to-all-start.14) | async-done | bytes 262176 | tf_op jit(solution)/shard_map/all_to_all | solution.py:49
  570.0 21.4 %attend_backward.3 = (bf16[2,8,128,256]{3,2,1,0:T(8,128)(2,1)}, bf16[2,8,128,256]{3,2,1,0:T(8,128)(2,1)}) custom-call(s32[2]{0:T(128)} %pad_add_fusion.pos_ref, bf16[8,128,256]{2,1,0:T(8,128)(2,1)} %join_grads.6.refs_0_, bf16[8,128,256]{2,1,0:T(8,128)(2,1)} %copy-done.28, bf16[8,128,256]{2,1,0:T(8,128)(2,1)} %join_grads.7.refs_2_, ...), custom_call_target="tpu_custom_call" | custom-call | flops 180000000 | bytes 260000 | tf_op jit(solution)/shard_map/attend_backward/pallas_call | solution.py:479
  598.2 20.0 %all_to_all.88.in_ref = bf16[8,128,256]{2,1,0:T(8,128)(2,1)} all-to-all(bf16[8,128,256]{2,1,0:T(8,128)(2,1)} %get-tuple-element.270), channel_id=1, replica_groups={{0,4,8,12,16,20,24,28},{2,6,10,14,18,22,26,30},{1,5,9,13,17,21,25,29},{..., dimensions={0} | all-to-all | bytes 1048576 | tf_op jit(solution)/shard_map/all_to_all | solution.py:49
  625.0 26.0 %all-to-all-done.16.in_ref = bf16[8,128,256]{2,1,0:T(8,128)(2,1)S(1)} async-done(((bf16[8,128,256]{2,1,0:T(8,128)(2,1)}), bf16[8,128,256]{2,1,0:T(8,128)(2,1)S(1)}, u32[]{:S(2)}, u32[]{:S(2)}) %all-to-all-start.16) | async-done | bytes 524320 | tf_op jit(solution)/shard_map/all_to_all | solution.py:49
  671.2 19.2 %collective-permute-done.32 = bf16[4,64,1024]{2,1,0:T(8,128)(2,1)} collective-permute-done((bf16[4,64,1024]{2,1,0:T(8,128)(2,1)}, bf16[4,64,1024]{2,1,0:T(8,128)(2,1)}, u32[]{:S(2)}, u32[]{:S(2)}) %collective-permute-start.32) | collective-permute-done | bytes 524320 | tf_op jit(solution)/shard_map/ppermute | solution.py:27
  (399 shorter events, 327.2 us)
Async XLA Ops:
  7.2 52.6 %all-gather.3.cloned.1.call-start = ((), (), s32[]{:S(2)}) async-start(), calls=%async_computation.19 | async-start | bytes 3342336 | tf_op jit(solution)/shard_map/all_gather | solution.py:1086
  12.4 18.4 %collective-permute-start.5 = (f32[2,2,512]{2,1,0:T(2,128)S(1)}, f32[2,2,512]{2,1,0:T(2,128)S(1)}, u32[]{:S(2)}, u32[]{:S(2)}) collective-permute-start(f32[2,2,512]{2,1,0:T(2,128)S(1)} %pad_maximum_fusion.8), channel_id=1, source_target_pairs={{0,1},{1,0},{2,3},{3,2},{4,5},{5,4},{6,7},{7,6},{8,9},{9,8},{10,11... | collective-permute-start | bytes 24584 | tf_op jit(solution)/shard_map/ppermute | solution.py:27
  16.7 14.8 %all-to-all-start.1 = ((s32[16,2,256]{2,1,0:T(2,128)}), s32[16,2,256]{2,1,0:T(2,128)S(1)}, u32[]{:S(2)}, u32[]{:S(2)}) async-start(s32[16,2,256]{2,1,0:T(2,128)} %bitcast.6), calls=%async_computation.1 | async-start | bytes 65536 | tf_op jit(solution)/shard_map/all_to_all | solution.py:1095
  26.2 51.6 %collective-permute-start = (bf16[2,256,512]{2,1,0:T(8,128)(2,1)}, bf16[2,256,512]{2,1,0:T(8,128)(2,1)S(1)}, u32[]{:S(2)}, u32[]{:S(2)}) collective-permute-start(bf16[2,256,512]{2,1,0:T(8,128)(2,1)} %get-tuple-element.152), channel_id=1, source_target_pairs={{0,1},{1,0},{2,3},{3,2},{4,5},{5,4},{6,7},{7,6},{8,9},{9,8},{10,11... | collective-permute-start | bytes 1572872 | tf_op jit(solution)/shard_map/ppermute | solution.py:27
  26.8 25.6 %collective-permute-start.1 = (bf16[2,256,512]{2,1,0:T(8,128)(2,1)}, bf16[2,256,512]{2,1,0:T(8,128)(2,1)S(1)}, u32[]{:S(2)}, u32[]{:S(2)}) collective-permute-start(bf16[2,256,512]{2,1,0:T(8,128)(2,1)} %get-tuple-element.154), channel_id=1, source_target_pairs={{0,1},{1,0},{2,3},{3,2},{4,5},{5,4},{6,7},{7,6},{8,9},{9,8},{10,11... | collective-permute-start | bytes 1572872 | tf_op jit(solution)/shard_map/ppermute | solution.py:27
  28.3 53.2 %collective-permute-start.3 = (bf16[2,256,512]{2,1,0:T(8,128)(2,1)}, bf16[2,256,512]{2,1,0:T(8,128)(2,1)S(1)}, u32[]{:S(2)}, u32[]{:S(2)}) collective-permute-start(bf16[2,256,512]{2,1,0:T(8,128)(2,1)} %get-tuple-element.159), channel_id=1, source_target_pairs={{0,1},{1,0},{2,3},{3,2},{4,5},{5,4},{6,7},{7,6},{8,9},{9,8},{10,11... | collective-permute-start | bytes 1572872 | tf_op jit(solution)/shard_map/ppermute | solution.py:27
  28.8 52.6 %collective-permute-start.4 = (bf16[2,256,512]{2,1,0:T(8,128)(2,1)}, bf16[2,256,512]{2,1,0:T(8,128)(2,1)S(1)}, u32[]{:S(2)}, u32[]{:S(2)}) collective-permute-start(bf16[2,256,512]{2,1,0:T(8,128)(2,1)} %get-tuple-element.160), channel_id=1, source_target_pairs={{0,1},{1,0},{2,3},{3,2},{4,5},{5,4},{6,7},{7,6},{8,9},{9,8},{10,11... | collective-permute-start | bytes 1572872 | tf_op jit(solution)/shard_map/ppermute | solution.py:27
  63.5 22.7 %all-to-all-start = ((bf16[8,128,256]{2,1,0:T(8,128)(2,1)}), bf16[8,128,256]{2,1,0:T(8,128)(2,1)S(1)}, u32[]{:S(2)}, u32[]{:S(2)}) async-start(bf16[8,128,256]{2,1,0:T(8,128)(2,1)} %get-tuple-element.156), calls=%async_computation | async-start | bytes 1048576 | tf_op jit(solution)/shard_map/all_to_all | solution.py:49
  86.2 20.5 %all-to-all-start.2 = ((bf16[8,128,256]{2,1,0:T(8,128)(2,1)}), bf16[8,128,256]{2,1,0:T(8,128)(2,1)S(1)}, u32[]{:S(2)}, u32[]{:S(2)}) async-start(bf16[8,128,256]{2,1,0:T(8,128)(2,1)} %get-tuple-element.161), calls=%async_computation.2 | async-start | bytes 1048576 | tf_op jit(solution)/shard_map/all_to_all | solution.py:49
  92.1 115.2 %all-gather.5.cloned.1.call-start = ((), (), s32[]{:S(2)}) async-start(), calls=%async_computation.20 | async-start | bytes 3342336 | tf_op jit(solution)/shard_map/all_gather | solution.py:1131
  212.2 22.1 %all-to-all-start.6 = ((bf16[8,128,256]{2,1,0:T(8,128)(2,1)}), bf16[8,128,256]{2,1,0:T(8,128)(2,1)S(1)}, u32[]{:S(2)}, u32[]{:S(2)}) async-start(bf16[8,128,256]{2,1,0:T(8,128)(2,1)} %get-tuple-element.180), calls=%async_computation.6 | async-start | bytes 1048576 | tf_op jit(solution)/shard_map/all_to_all | solution.py:49
  234.2 16.8 %all-to-all-start.5 = ((bf16[8,128,256]{2,1,0:T(8,128)(2,1)}), bf16[8,128,256]{2,1,0:T(8,128)(2,1)S(1)}, u32[]{:S(2)}, u32[]{:S(2)}) async-start(bf16[8,128,256]{2,1,0:T(8,128)(2,1)} %get-tuple-element.178), calls=%async_computation.5 | async-start | bytes 1048576 | tf_op jit(solution)/shard_map/all_to_all | solution.py:49
  300.7 15.0 %collective-permute-start.15 = (bf16[256,1024]{1,0:T(8,128)(2,1)}, bf16[256,1024]{1,0:T(8,128)(2,1)S(1)}, u32[]{:S(2)}, u32[]{:S(2)}) collective-permute-start(bf16[256,1024]{1,0:T(8,128)(2,1)} %get-tuple-element.184.own_ref), channel_id=1, source_target_pairs={{0,1},{1,0},{2,3},{3,2},{4,5},{5,4},{6,7},{7,6},{8,9},{9,8},{10,11... | collective-permute-start | bytes 1572872 | tf_op jit(solution)/shard_map/ppermute | solution.py:27
  310.4 23.4 %collective-permute-start.16 = (bf16[256,1024]{1,0:T(8,128)(2,1)}, bf16[256,1024]{1,0:T(8,128)(2,1)S(1)}, u32[]{:S(2)}, u32[]{:S(2)}) collective-permute-start(bf16[256,1024]{1,0:T(8,128)(2,1)} %get-tuple-element.190.own_ref), channel_id=1, source_target_pairs={{0,1},{1,0},{2,3},{3,2},{4,5},{5,4},{6,7},{7,6},{8,9},{9,8},{10,11... | collective-permute-start | bytes 1572872 | tf_op jit(solution)/shard_map/ppermute | solution.py:27
  333.7 20.2 %collective-permute-start.18 = (bf16[256,1024]{1,0:T(8,128)(2,1)}, bf16[256,1024]{1,0:T(8,128)(2,1)S(1)}, u32[]{:S(2)}, u32[]{:S(2)}) collective-permute-start(bf16[256,1024]{1,0:T(8,128)(2,1)} %get-tuple-element.200.own_ref), channel_id=1, source_target_pairs={{0,1},{1,0},{2,3},{3,2},{4,5},{5,4},{6,7},{7,6},{8,9},{9,8},{10,11... | collective-permute-start | bytes 1572872 | tf_op jit(solution)/shard_map/ppermute | solution.py:27
  382.1 209.4 %reduce-scatter.3.cloned.1.call-start = ((), (), s32[]{:S(2)}) async-start(), calls=%async_computation.21 | async-start | bytes 10027008 | tf_op jit(solution)/shard_map/reduce_scatter | solution.py:1046
  459.5 18.4 %all-to-all-start.12 = ((bf16[8,128,256]{2,1,0:T(8,128)(2,1)}), bf16[8,128,256]{2,1,0:T(8,128)(2,1)S(1)}, u32[]{:S(2)}, u32[]{:S(2)}) async-start(bf16[8,128,256]{2,1,0:T(8,128)(2,1)} %get-tuple-element.225), calls=%async_computation.12 | async-start | bytes 1048576 | tf_op jit(solution)/shard_map/all_to_all | solution.py:49
  463.2 19.0 %collective-permute-start.23 = (bf16[256,1024]{1,0:T(8,128)(2,1)S(1)}, bf16[256,1024]{1,0:T(8,128)(2,1)S(1)}, u32[]{:S(2)}, u32[]{:S(2)}) collective-permute-start(bf16[256,1024]{1,0:T(8,128)(2,1)S(1)} %copy-done.45), channel_id=1, source_target_pairs={{0,1},{1,0},{2,3},{3,2},{4,5},{5,4},{6,7},{7,6},{8,9},{9,8},{10,11... | collective-permute-start | bytes 1572872 | tf_op jit(solution)/shard_map/ppermute | solution.py:27
  482.2 16.9 %collective-permute-start.25 = (bf16[256,1024]{1,0:T(8,128)(2,1)}, bf16[256,1024]{1,0:T(8,128)(2,1)S(1)}, u32[]{:S(2)}, u32[]{:S(2)}) collective-permute-start(bf16[256,1024]{1,0:T(8,128)(2,1)} %get-tuple-element.236.own_ref), channel_id=1, source_target_pairs={{0,1},{1,0},{2,3},{3,2},{4,5},{5,4},{6,7},{7,6},{8,9},{9,8},{10,11... | collective-permute-start | bytes 1572872 | tf_op jit(solution)/shard_map/ppermute | solution.py:27
  497.0 16.2 %collective-permute-start.24 = (bf16[256,1024]{1,0:T(8,128)(2,1)}, bf16[256,1024]{1,0:T(8,128)(2,1)S(1)}, u32[]{:S(2)}, u32[]{:S(2)}) collective-permute-start(bf16[256,1024]{1,0:T(8,128)(2,1)} %get-tuple-element.222.own_ref), channel_id=1, source_target_pairs={{0,1},{1,0},{2,3},{3,2},{4,5},{5,4},{6,7},{7,6},{8,9},{9,8},{10,11... | collective-permute-start | bytes 1572872 | tf_op jit(solution)/shard_map/ppermute | solution.py:27
  513.1 22.9 %collective-permute-start.26 = (bf16[256,1024]{1,0:T(8,128)(2,1)}, bf16[256,1024]{1,0:T(8,128)(2,1)S(1)}, u32[]{:S(2)}, u32[]{:S(2)}) collective-permute-start(bf16[256,1024]{1,0:T(8,128)(2,1)} %get-tuple-element.239.own_ref), channel_id=1, source_target_pairs={{0,1},{1,0},{2,3},{3,2},{4,5},{5,4},{6,7},{7,6},{8,9},{9,8},{10,11... | collective-permute-start | bytes 1572872 | tf_op jit(solution)/shard_map/ppermute | solution.py:27
  518.4 18.4 %all-to-all-start.13 = ((bf16[8,128,128]{2,1,0:T(8,128)(2,1)}), bf16[8,128,128]{2,1,0:T(8,128)(2,1)S(1)}, u32[]{:S(2)}, u32[]{:S(2)}) async-start(bf16[8,128,128]{2,1,0:T(8,128)(2,1)} %get-tuple-element.241), calls=%async_computation.13 | async-start | bytes 524288 | tf_op jit(solution)/shard_map/all_to_all | solution.py:49
  521.8 222.8 %reduce-scatter.5.cloned.1.call-start = ((), (), s32[]{:S(2)}) async-start(), calls=%async_computation.22 | async-start | bytes 12255232 | tf_op jit(solution)/shard_map/reduce_scatter | solution.py:1046
  545.2 18.9 %all-to-all-start.14 = ((bf16[8,128,128]{2,1,0:T(8,128)(2,1)}), bf16[8,128,128]{2,1,0:T(8,128)(2,1)S(1)}, u32[]{:S(2)}, u32[]{:S(2)}) async-start(bf16[8,128,128]{2,1,0:T(8,128)(2,1)} %get-tuple-element.254), calls=%async_computation.14 | async-start | bytes 524288 | tf_op jit(solution)/shard_map/all_to_all | solution.py:49
  553.0 14.9 %collective-permute-start.27 = (bf16[8,128,256]{2,1,0:T(8,128)(2,1)}, bf16[8,128,256]{2,1,0:T(8,128)(2,1)S(1)}, u32[]{:S(2)}, u32[]{:S(2)}) collective-permute-start(bf16[8,128,256]{2,1,0:T(8,128)(2,1)} %join_grads.6.refs_0_), channel_id=1, source_target_pairs={{0,2},{2,0},{4,6},{6,4},{8,10},{10,8},{12,14},{14,12},{16,18},{18,... | collective-permute-start | bytes 1572872 | tf_op jit(solution)/shard_map/ppermute | solution.py:27
  618.2 32.8 %all-to-all-start.16 = ((bf16[8,128,256]{2,1,0:T(8,128)(2,1)}), bf16[8,128,256]{2,1,0:T(8,128)(2,1)S(1)}, u32[]{:S(2)}, u32[]{:S(2)}) async-start(bf16[8,128,256]{2,1,0:T(8,128)(2,1)} %get-tuple-element.275), calls=%async_computation.17 | async-start | bytes 1048576 | tf_op jit(solution)/shard_map/all_to_all | solution.py:49
  666.3 24.1 %collective-permute-start.32 = (bf16[4,64,1024]{2,1,0:T(8,128)(2,1)}, bf16[4,64,1024]{2,1,0:T(8,128)(2,1)}, u32[]{:S(2)}, u32[]{:S(2)}) collective-permute-start(bf16[4,64,1024]{2,1,0:T(8,128)(2,1)} %dynamic-slice_bitcast_fusion.1), channel_id=1, source_target_pairs={{0,4},{2,6},{4,0},{6,2},{8,12},{10,14},{12,8},{14,10},{16,20},{18,... | collective-permute-start | bytes 1572872 | tf_op jit(solution)/shard_map/ppermute | solution.py:27
  667.8 26.6 %collective-permute-start.17 = (bf16[512,512]{1,0:T(8,128)(2,1)S(1)}, bf16[512,512]{1,0:T(8,128)(2,1)S(1)}, u32[]{:S(2)}, u32[]{:S(2)}) collective-permute-start(bf16[512,512]{1,0:T(8,128)(2,1)S(1)} %pad_maximum_fusion.2), channel_id=1, source_target_pairs={{0,1},{1,0},{2,3},{3,2},{4,5},{5,4},{6,7},{7,6},{8,9},{9,8},{10,11... | collective-permute-start | bytes 1572872 | tf_op jit(solution)/shard_map/ppermute | solution.py:27
  669.2 39.9 %collective-permute-start.33 = (bf16[256,1024]{1,0:T(8,128)(2,1)}, bf16[256,1024]{1,0:T(8,128)(2,1)}, u32[]{:S(2)}, u32[]{:S(2)}) collective-permute-start(bf16[256,1024]{1,0:T(8,128)(2,1)} %get-tuple-element.278.own_ref), channel_id=1, source_target_pairs={{0,1},{1,0},{2,3},{3,2},{4,5},{5,4},{6,7},{7,6},{8,9},{9,8},{10,11... | collective-permute-start | bytes 1572872 | tf_op jit(solution)/shard_map/ppermute | solution.py:27
  669.9 34.3 %collective-permute-start.30 = (bf16[256,1024]{1,0:T(8,128)(2,1)S(1)}, bf16[256,1024]{1,0:T(8,128)(2,1)}, u32[]{:S(2)}, u32[]{:S(2)}) collective-permute-start(bf16[256,1024]{1,0:T(8,128)(2,1)S(1)} %copy-done.24), channel_id=1, source_target_pairs={{0,1},{1,0},{2,3},{3,2},{4,5},{5,4},{6,7},{7,6},{8,9},{9,8},{10,11... | collective-permute-start | bytes 1572872 | tf_op jit(solution)/shard_map/ppermute | solution.py:27
  691.7 16.6 %collective-permute-start.34 = (bf16[2,64,1024]{2,1,0:T(8,128)(2,1)S(1)}, bf16[2,64,1024]{2,1,0:T(8,128)(2,1)S(1)}, u32[]{:S(2)}, u32[]{:S(2)}) collective-permute-start(bf16[2,64,1024]{2,1,0:T(8,128)(2,1)S(1)} %dynamic-slice_bitcast_fusion.2), channel_id=1, source_target_pairs={{0,8},{2,10},{4,12},{6,14},{8,0},{10,2},{12,4},{14,6},{16,24},{18,... | collective-permute-start | bytes 786440 | tf_op jit(solution)/shard_map/ppermute | solution.py:27
  715.8 17.6 %collective-permute-start.40 = (bf16[1,64,1024]{2,1,0:T(8,128)(2,1)S(1)}, bf16[1,64,1024]{2,1,0:T(8,128)(2,1)S(1)}, u32[]{:S(2)}, u32[]{:S(2)}) collective-permute-start(bf16[1,64,1024]{2,1,0:T(8,128)(2,1)S(1)} %constant_dynamic-slice_fusion.12), channel_id=1, source_target_pairs={{0,16},{2,18},{4,20},{6,22},{8,24},{10,26},{12,28},{14,30},{16,0},... | collective-permute-start | bytes 393224 | tf_op jit(solution)/shard_map/ppermute | solution.py:27
  (104 other events, 749.2 us)
Sparse Core Ops, SparseCore 0:
  11.8 47.8 all-gather.2
  138.4 46.6 all-gather.4
  459.6 118.5 reduce-scatter.2
  582.7 158.0 reduce-scatter.4

commit v4 on v3

--- a/solution.py
+++ b/solution.py
@@ -15,7 +15,7 @@
 F32 = jnp.float32
 BF16 = jnp.bfloat16
 SCALE = HD ** (-0.5)
-VMEM_LIMIT = 56 * 1024 * 1024
+VMEM_LIMIT = 63 * 1024 * 1024
 PAIRS = 8
 SHARE = 0.01
 CHUNKS = 2
@@ -833,15 +833,24 @@
     )(stream, own, other, bias, gain, shift, up, up_bias, down, *after)
 
 
-def ffn_back_kernel(
-    grad_ref, up_ref, down_ref, pre_ref,
-    branch_ref, hidden_ref, low_ref, down_bias_ref, up_bias_ref, part_ref, acc,
-):
+def ffn_back_kernel(norm, *refs):
+    if norm is None:
+        grad_ref, up_ref, down_ref, pre_ref, *refs = refs
+    else:
+        stream_ref, own_ref, other_ref, grad_ref, gain_ref, up_ref, down_ref, pre_ref, *refs = refs
+        new_ref, gain_out, shift_out, *refs = refs
+    branch_ref, hidden_ref, low_ref, down_bias_ref, up_bias_ref, part_ref, acc = refs
     step = pl.program_id(0)
 
     @pl.when(step == 0)
     def _():
-        grad = grad_ref[...]
+        if norm is None:
+            grad = grad_ref[...]
+        else:
+            grad = norm_back(
+                norm, stream_ref, own_ref, other_ref, grad_ref, gain_ref, gain_out, shift_out
+            )
+            new_ref[...] = grad
         branch_ref[...] = grad.astype(BF16)
         down_bias_ref[...] = jnp.sum(grad, axis=0, keepdims=True)
 
@@ -872,30 +881,37 @@
         part_ref[...] = acc[...].astype(BF16)
 
 
-def feed_back(layer, grad, up, down, pre):
+def feed_back(layer, grad, up, down, pre, before=None):
     toks, width = grad.shape
     hidden = down.shape[2]
     step = hidden // FFN_STEPS
     full = pl.BlockSpec((toks, width), lambda i: (0, 0))
+    line = pl.BlockSpec((1, width), lambda i: (0, 0))
     slab = pl.BlockSpec((1, width, step), lambda i: (layer, 0, i))
     tall = pl.BlockSpec((toks, step), lambda i: (0, i))
+    shapes = [
+        bf16_out(toks, width), bf16_out(toks, hidden), bf16_out(toks, hidden),
+        f32_out(1, width), f32_out(1, hidden), bf16_out(toks, width),
+    ]
+    out_specs = [full, tall, tall, line, pl.BlockSpec((1, step), lambda i: (0, i)), full]
+    operands, in_specs = [grad], [full]
+    if before is not None:
+        norm, stream, own, other, gain = before
+        operands = [stream, own, other, grad, gain]
+        in_specs = [full] * 4 + [whole_block(gain)]
+        shapes = [f32_out(toks, width), f32_out(1, width), f32_out(1, width)] + shapes
+        out_specs = [full, line, line] + out_specs
     return pl.pallas_call(
-        ffn_back_kernel,
+        functools.partial(ffn_back_kernel, None if before is None else norm),
         grid=(FFN_STEPS,),
-        out_shape=(
-            bf16_out(toks, width), bf16_out(toks, hidden), bf16_out(toks, hidden),
-            f32_out(1, width), f32_out(1, hidden), bf16_out(toks, width),
-        ),
-        in_specs=[full, slab, slab, tall],
-        out_specs=(
-            full, tall, tall, pl.BlockSpec((1, width), lambda i: (0, 0)),
-            pl.BlockSpec((1, step), lambda i: (0, i)), full,
-        ),
+        out_shape=shapes,
+        in_specs=in_specs + [slab, slab, tall],
+        out_specs=out_specs,
         scratch_shapes=[pltpu.VMEM((toks, width), F32)],
         compiler_params=params(),
         cost_estimate=cost(4 * toks * width * hidden, 15e6),
         name="feed_back",
-    )(grad, up, down, pre)
+    )(*operands, up, down, pre)
 
 
 def products_kernel(counts, *refs):
@@ -1159,16 +1175,22 @@
     second_out = narrow_chunks(pos, second, seqs, LAYERS - 1, [*ffn_parts, got, down_bias])
     summed, waiting = [], []
     done = []
-    small_grads = [None] * LAYERS
+    early_smalls, late_smalls = [None] * LAYERS, [None] * LAYERS
     after = []
     for layer in reversed(range(LAYERS)):
         second_l, normed, sorted_rows, attn, stats, attn_tok, first_l, ffn_in, pre_act = saved[layer]
         branch, hidden, low, parts = [], [], [], []
+        late_gain, late_shift = 0.0, 0.0
         down_bias_grad, up_bias_grad = 0.0, 0.0
         for q in chunks:
-            branch_q, hidden_q, low_q, down_bias_q, up_bias_q, part = feed_back(
-                layer, grad_second[q], up_weight, down_weight, pre_act[q]
+            *results, branch_q, hidden_q, low_q, down_bias_q, up_bias_q, part = feed_back(
+                layer, grad_second[q], up_weight, down_weight, pre_act[q],
+                before[q] if layer + 1 < LAYERS else None,
             )
+            if results:
+                grad_second[q], gain_q, shift_q = results
+                late_gain += gain_q
+                late_shift += shift_q
             branch.append(branch_q)
             hidden.append(hidden_q)
             low.append(low_q)
@@ -1213,7 +1235,7 @@
         )
         own, sib = attention_backward(pos, sources, sorted_rows, tables, [early_small])
         units = add_cores(own, swap(sib, "wide", 1), done)
-        grad_tok, attn_gain_grad, attn_bias_grad = [], 0.0, 0.0
+        grad_tok = []
         backs = [chip_exchange(units[q]) for q in chunks]
         after = []
         if layer > 0:
@@ -1232,16 +1254,26 @@
         if layer == 0:
             stages = reduce_rows(weight_products(waiting, unit_columns))
             summed.append(stages[-1])
-        for q in chunks:
-            grad_second[q], gain_q, shift_q = finish_attention(
-                layer, second_l[q], *merged[q], grad_second[q], attn_norm_gain,
-                stages[q + 1 : q + 2] if layer == 0 else (),
-            )
-            attn_gain_grad += gain_q
-            attn_bias_grad += shift_q
+        before = [
+            (layer, second_l[q], *merged[q], attn_norm_gain) for q in chunks
+        ]
+        if layer + 1 < LAYERS:
+            late_smalls[layer + 1] = (late_gain, late_shift)
         done = summed[-1:]
-        late_small = jnp.concatenate([own_half(attn_gain_grad), own_half(attn_bias_grad)])
-        small_grads[layer] = jnp.concatenate([late_small, early_small])
+        early_smalls[layer] = early_small
+    late_gain, late_shift = 0.0, 0.0
+    for q in chunks:
+        norm, stream, own, other, gain = before[q]
+        grad_second[q], gain_q, shift_q = finish_attention(
+            norm, stream, own, other, grad_second[q], gain, stages[q + 1 : q + 2]
+        )
+        late_gain += gain_q
+        late_shift += shift_q
+    late_smalls[0] = (late_gain, late_shift)
+    small_grads = [
+        jnp.concatenate([own_half(grad) for grad in late_smalls[layer]] + [early_smalls[layer]])
+        for layer in range(LAYERS)
+    ]
     first_grad = narrow_chunks(pos, grad_first, seqs)
     second_grad = narrow_chunks(pos, grad_second, seqs)
 

time: 769 us -> 748 us (0.973)
  waiting for transfers between devices: 210 us -> 194 us
  local copies, waits for them, and re-layouts: 43.8 us -> 34.6 us
    unnamed x164 -> x118, local copies, waits for them, and re-layouts: 28.6 us -> 16.7 us
    all_to_all x12, waiting for transfers between devices: 97.3 us -> 89 us  [chip_exchange(): lax.all_to_all(units, 'wide', 0, 0, tiled=True, axis_index_groups=groups)]
    ppermute x41, waiting for transfers between devices: 109 us -> 101 us  [swap(): lax.ppermute(value, axis, [(source, source ^ mask) for source in range(co...]
    pallas_call x4 -> x2, Pallas kernels: 15.1 us -> 7.29 us  [finish_attention(): pl.pallas_call(functools.partial(finish_kernel, layer), out_shape=(f32_ou...]
  transfers between devices with their start and end apart: 58 -> 58, of which waited for: 33 -> 33; matrix products, arithmetic and copies ran while one was open for 4% -> 6% of each run, Pallas kernels for 28% -> 28%
where the time goes in v4:
time: 748 us; the launch traced here: 738 us
  Pallas kernels  302 us (40%)
  waiting for transfers between devices  194 us (26%)
  starting transfers between devices  91.8 us (12%)
  blocking collectives  68 us (9%)
  local copies, waits for them, and re-layouts  34.6 us (5%)
  other arithmetic  30.1 us (4%)
  between operations  15 us (2%)
    ppermute x41, waiting for transfers between devices, swap(): lax.ppermute(value, axis, [(source, source ^ mask) for source in range(co...  101 us
    all_to_all x12, waiting for transfers between devices, chip_exchange(): lax.all_to_all(units, 'wide', 0, 0, tiled=True, axis_index_groups=groups)  89 us
    all_to_all x4, blocking collectives, chip_exchange(): lax.all_to_all(units, 'wide', 0, 0, tiled=True, axis_index_groups=groups)  68 us
    all_to_all x12, starting transfers between devices, chip_exchange(): lax.all_to_all(units, 'wide', 0, 0, tiled=True, axis_index_groups=groups)  55.1 us
    pallas_call x2, Pallas kernels, attention_backward(): pl.pallas_call(functools.partial(backward_kernel, chunks, len(after)), ou...  42.6 us
    pallas_call x4, Pallas kernels, feed_back(): pl.pallas_call(functools.partial(ffn_back_kernel, None if before is None...  39.5 us
    pallas_call x2, Pallas kernels, attention_forward(): pl.pallas_call(functools.partial(forward_kernel, chunks, len(after)), out...  38.4 us
    pallas_call x4, Pallas kernels, weight_products(): pl.pallas_call(functools.partial(products_kernel, counts), grid=(start,),...  34.6 us
  transfers between devices with their start and end apart: 58, of which 33 were waited for; matrix products, arithmetic and copies ran while one was open for 6% of the time, Pallas kernels for 28%

profile of v4, /device:TPU:0, one launch (start us, length us, event | category | flops | bytes accessed | tf_op | source)
XLA Modules:
  0.0 737.5 jit_solution(10881293123498370407)
XLA Ops:
  16.7 5.9 all-to-all-start.1
  33.6 18.9 %collective-permute-done.1.other_ref = bf16[2,256,512]{2,1,0:T(8,128)(2,1)} collective-permute-done((bf16[2,256,512]{2,1,0:T(8,128)(2,1)}, bf16[2,256,512]{2,1,0:T(8,128)(2,1)}, u32[]{:S(2)}, u32[]{:S(2)}) %collective-permute-start.1) | collective-permute-done | bytes 524320 | tf_op jit(solution)/shard_map/ppermute | solution.py:27
  92.0 14.3 %all-to-all-done.2.refs_2_ = bf16[8,128,256]{2,1,0:T(8,128)(2,1)S(1)} async-done(((bf16[8,128,256]{2,1,0:T(8,128)(2,1)}), bf16[8,128,256]{2,1,0:T(8,128)(2,1)S(1)}, u32[]{:S(2)}, u32[]{:S(2)}) %all-to-all-start.2) | async-done | bytes 524320 | tf_op jit(solution)/shard_map/all_to_all | solution.py:49
  108.4 19.2 %attend_forward.2 = (bf16[2,4096,256]{2,1,0:T(8,128)(2,1)}, bf16[2,8,128,256]{3,2,1,0:T(8,128)(2,1)}, bf16[2,8,128,256]{3,2,1,0:T(8,128)(2,1)}) custom-call(s32[2]{0:T(128)} %pad_add_fusion.pos_ref, bf16[8,128,256]{2,1,0:T(8,128)(2,1)} %all-to-all-done.refs_0_, bf16[8,128,256]{2,1,0:T(8,128)(2,1)} %collective-permute-done.2.refs_1_, ...), custom_call_target="tpu_custom_call" | custom-call | flops 160000000 | bytes 240000 | tf_op jit(solution)/shard_map/attend_forward/pallas_call | solution.py:449
  136.5 16.0 %all_to_all.85.in_ref = bf16[8,128,128]{2,1,0:T(8,128)(2,1)} all-to-all(bf16[8,128,128]{2,1,0:T(8,128)(2,1)} %get-tuple-element.164.refs_2_), channel_id=1, replica_groups={{0,4,8,12,16,20,24,28},{2,6,10,14,18,22,26,30},{1,5,9,13,17,21,25,29},{..., dimensions={0} | all-to-all | bytes 524288 | tf_op jit(solution)/shard_map/all_to_all | solution.py:49
  174.4 8.1 %feed_forward.4 = (f32[256,1024]{1,0:T(8,128)}, bf16[256,1024]{1,0:T(8,128)(2,1)}, f32[256,2048]{1,0:T(8,128)}, bf16[256,1024]{1,0:T(8,128)(2,1)}) custom-call(f32[256,1024]{1,0:T(8,128)} %get-tuple-element.153.refs_4_.stream_ref, bf16[256,1024]{1,0:T(8,128)(2,1)} %get-tuple-element.165.own_ref, bf16[256,1024]{1,0:T(8,128)(2,1)} %copy-done.22, ...), custom_call_target="tpu_custom_call" | custom-call | flops 21474836 | bytes 140000 | tf_op jit(solution)/shard_map/feed_forward/pallas_call | solution.py:817
  183.8 8.0 %feed_forward.5 = (f32[256,1024]{1,0:T(8,128)}, bf16[256,1024]{1,0:T(8,128)(2,1)}, f32[256,2048]{1,0:T(8,128)}, bf16[256,1024]{1,0:T(8,128)(2,1)}) custom-call(f32[256,1024]{1,0:T(8,128)} %get-tuple-element.158.refs_5_.stream_ref, bf16[256,1024]{1,0:T(8,128)(2,1)} %get-tuple-element.175.own_ref, bf16[256,1024]{1,0:T(8,128)(2,1)} %collective-permute-done.10.other_ref, ...), custom_call_target="tpu_custom_call" | custom-call | flops 21474836 | bytes 140000 | tf_op jit(solution)/shard_map/feed_forward/pallas_call | solution.py:817
  193.3 11.5 %collective-permute-done.12.refs_1_ = bf16[256,1024]{1,0:T(8,128)(2,1)S(1)} collective-permute-done((bf16[256,1024]{1,0:T(8,128)(2,1)}, bf16[256,1024]{1,0:T(8,128)(2,1)S(1)}, u32[]{:S(2)}, u32[]{:S(2)}) %collective-permute-start.12) | collective-permute-done | bytes 524320 | tf_op jit(solution)/shard_map/ppermute | solution.py:27
  216.3 11.1 %collective-permute-done.9.refs_1_ = bf16[256,1024]{1,0:T(8,128)(2,1)} collective-permute-done((bf16[256,1024]{1,0:T(8,128)(2,1)}, bf16[256,1024]{1,0:T(8,128)(2,1)}, u32[]{:S(2)}, u32[]{:S(2)}) %collective-permute-start.9) | collective-permute-done | bytes 524320 | tf_op jit(solution)/shard_map/ppermute | solution.py:27
  231.4 6.1 all-to-all-start.5
  237.6 10.8 %all-to-all-done.5.refs_0_ = bf16[8,128,256]{2,1,0:T(8,128)(2,1)S(1)} async-done(((bf16[8,128,256]{2,1,0:T(8,128)(2,1)}), bf16[8,128,256]{2,1,0:T(8,128)(2,1)S(1)}, u32[]{:S(2)}, u32[]{:S(2)}) %all-to-all-start.5) | async-done | bytes 524320 | tf_op jit(solution)/shard_map/all_to_all | solution.py:49
  250.4 19.2 %attend_forward.3 = (bf16[2,4096,256]{2,1,0:T(8,128)(2,1)}, bf16[2,8,128,256]{3,2,1,0:T(8,128)(2,1)}, bf16[2,8,128,256]{3,2,1,0:T(8,128)(2,1)}) custom-call(s32[2]{0:T(128)} %pad_add_fusion.pos_ref, bf16[8,128,256]{2,1,0:T(8,128)(2,1)} %copy-done.8, bf16[8,128,256]{2,1,0:T(8,128)(2,1)} %collective-permute-done.11.refs_1_, bf16[8,128,256]{2,1,0:T(8,128)(2,1)} %copy-done.6, ...), custom_call_target="tpu_custom_call" | custom-call | flops 160000000 | bytes 240000 | tf_op jit(solution)/shard_map/attend_forward/pallas_call | solution.py:449
  276.8 13.5 %all_to_all.86.in_ref = bf16[8,128,128]{2,1,0:T(8,128)(2,1)} all-to-all(bf16[8,128,128]{2,1,0:T(8,128)(2,1)} %get-tuple-element.183), channel_id=1, replica_groups={{0,4,8,12,16,20,24,28},{2,6,10,14,18,22,26,30},{1,5,9,13,17,21,25,29},{..., dimensions={0} | all-to-all | bytes 524288 | tf_op jit(solution)/shard_map/all_to_all | solution.py:49
  296.5 6.5 all-to-all-done.8.in_ref
  312.4 8.0 %feed_forward.6 = (f32[256,1024]{1,0:T(8,128)}, bf16[256,1024]{1,0:T(8,128)(2,1)}, f32[256,2048]{1,0:T(8,128)}, bf16[256,1024]{1,0:T(8,128)(2,1)}) custom-call(f32[256,1024]{1,0:T(8,128)} %get-tuple-element.173.stream_ref, bf16[256,1024]{1,0:T(8,128)(2,1)} %get-tuple-element.184.own_ref, bf16[256,1024]{1,0:T(8,128)(2,1)} %copy-done.24, ...), custom_call_target="tpu_custom_call" | custom-call | flops 21474836 | bytes 140000 | tf_op jit(solution)/shard_map/feed_forward/pallas_call | solution.py:817
  320.4 9.3 %feed_back.4 = (bf16[256,1024]{1,0:T(8,128)(2,1)}, bf16[256,2048]{1,0:T(8,128)(2,1)}, bf16[256,2048]{1,0:T(8,128)(2,1)}, f32[1,1024]{1,0:T(1,128)}, f32[1,2048]{1,0:T(1,128)}, /*index=5*/bf16[256,1024]{1,0:T(8,128)(2,1)}) custom-call(f32[256,1024]{1,0:T(8,128)} %get-tuple-element.167.refs_0_.refs_3_, bf16[2,1024,2048]{2,1,0:T(8,128)(2,1)} %refs_5_.3, ...), custom_call_target="tpu_custom_call" | custom-call | flops 21474836 | bytes 150000 | tf_op jit(solution)/shard_map/feed_back/pallas_call | solution.py:904
  329.7 8.1 %feed_forward.7 = (f32[256,1024]{1,0:T(8,128)}, bf16[256,1024]{1,0:T(8,128)(2,1)}, f32[256,2048]{1,0:T(8,128)}, bf16[256,1024]{1,0:T(8,128)(2,1)}) custom-call(f32[256,1024]{1,0:T(8,128)} %get-tuple-element.189.stream_ref, bf16[256,1024]{1,0:T(8,128)(2,1)} %get-tuple-element.190.own_ref, bf16[256,1024]{1,0:T(8,128)(2,1)} %collective-permute-done.16.other_ref, ...), custom_call_target="tpu_custom_call" | custom-call | flops 21474836 | bytes 140000 | tf_op jit(solution)/shard_map/feed_forward/pallas_call | solution.py:817
  337.8 9.3 %feed_back.5 = (bf16[256,1024]{1,0:T(8,128)(2,1)}, bf16[256,2048]{1,0:T(8,128)(2,1)}, bf16[256,2048]{1,0:T(8,128)(2,1)}, f32[1,1024]{1,0:T(1,128)}, f32[1,2048]{1,0:T(1,128)}, /*index=5*/bf16[256,1024]{1,0:T(8,128)(2,1)}) custom-call(f32[256,1024]{1,0:T(8,128)} %get-tuple-element.168.refs_1_.refs_0_.refs_3_, bf16[2,1024,2048]{2,1,0:T(8,128)(2,1)} %refs_5_.3, ...), custom_call_target="tpu_custom_call" | custom-call | flops 21474836 | bytes 150000 | tf_op jit(solution)/shard_map/feed_back/pallas_call | solution.py:904
  354.4 6.0 all-to-all-start.9
  360.4 8.2 %all-to-all-done.9.in_ref.refs_0_ = bf16[8,128,128]{2,1,0:T(8,128)(2,1)S(1)} async-done(((bf16[8,128,128]{2,1,0:T(8,128)(2,1)}), bf16[8,128,128]{2,1,0:T(8,128)(2,1)S(1)}, u32[]{:S(2)}, u32[]{:S(2)}) %all-to-all-start.9) | async-done | bytes 262176 | tf_op jit(solution)/shard_map/all_to_all | solution.py:49
  390.8 21.2 %attend_backward.2 = (bf16[2,8,128,256]{3,2,1,0:T(8,128)(2,1)}, bf16[2,8,128,256]{3,2,1,0:T(8,128)(2,1)}) custom-call(s32[2]{0:T(128)} %pad_add_fusion.pos_ref, bf16[8,128,256]{2,1,0:T(8,128)(2,1)} %join_grads.4.refs_0_, bf16[8,128,256]{2,1,0:T(8,128)(2,1)} %copy-done.19, bf16[8,128,256]{2,1,0:T(8,128)(2,1)} %join_grads.5.refs_2_, ...), custom_call_target="tpu_custom_call" | custom-call | flops 180000000 | bytes 260000 | tf_op jit(solution)/shard_map/attend_backward/pallas_call | solution.py:479
  417.8 19.2 %all_to_all.87.in_ref = bf16[8,128,256]{2,1,0:T(8,128)(2,1)} all-to-all(bf16[8,128,256]{2,1,0:T(8,128)(2,1)} %get-tuple-element.218), channel_id=1, replica_groups={{0,4,8,12,16,20,24,28},{2,6,10,14,18,22,26,30},{1,5,9,13,17,21,25,29},{..., dimensions={0} | all-to-all | bytes 1048576 | tf_op jit(solution)/shard_map/all_to_all | solution.py:49
  440.2 13.0 %weight_products.4.refs_0_ = bf16[1024,4608]{1,0:T(8,128)(2,1)} custom-call(bf16[256,1024]{1,0:T(8,128)(2,1)} %get-tuple-element.191.refs_1_.refs_0_, bf16[256,1024]{1,0:T(8,128)(2,1)} %get-tuple-element.225.refs_1_, bf16[256,2048]{1,0:T(8,128)(2,1)} %get-tuple-element.226.refs_2_, bf16[256,2048]{1,0:T(8,128)(2,1)} %get-tuple-element.227.refs_3_, ...), custom_call_target="tpu_custom_call" | custom-call | flops 48318384 | bytes 200000 | tf_op jit(solution)/shard_map/weight_products/pallas_call | solution.py:956
  457.0 14.6 %all-to-all-done.12.in_ref = bf16[8,128,256]{2,1,0:T(8,128)(2,1)S(1)} async-done(((bf16[8,128,256]{2,1,0:T(8,128)(2,1)}), bf16[8,128,256]{2,1,0:T(8,128)(2,1)S(1)}, u32[]{:S(2)}, u32[]{:S(2)}) %all-to-all-start.12) | async-done | bytes 524320 | tf_op jit(solution)/shard_map/all_to_all | solution.py:49
  476.0 10.4 %feed_back.6 = (f32[256,1024]{1,0:T(8,128)}, f32[1,1024]{1,0:T(1,128)}, f32[1,1024]{1,0:T(1,128)}, bf16[256,1024]{1,0:T(8,128)(2,1)}, bf16[256,2048]{1,0:T(8,128...) custom-call(f32[256,1024]{1,0:T(8,128)} %get-tuple-element.193.refs_0_, ...), custom_call_target="tpu_custom_call" | custom-call | flops 21474836 | bytes 150000 | tf_op jit(solution)/shard_map/feed_back/pallas_call | solution.py:904
  489.6 10.5 %feed_back.7 = (f32[256,1024]{1,0:T(8,128)}, f32[1,1024]{1,0:T(1,128)}, f32[1,1024]{1,0:T(1,128)}, bf16[256,1024]{1,0:T(8,128)(2,1)}, bf16[256,2048]{1,0:T(8,128...) custom-call(f32[256,1024]{1,0:T(8,128)} %get-tuple-element.194.refs_1_.re, ...), custom_call_target="tpu_custom_call" | custom-call | flops 21474836 | bytes 150000 | tf_op jit(solution)/shard_map/feed_back/pallas_call | solution.py:904
  509.8 14.1 %weight_products.5.refs_1_.refs_4_ = bf16[1024,5632]{1,0:T(8,128)(2,1)} custom-call(bf16[256,1024]{1,0:T(8,128)(2,1)} %get-tuple-element.240.refs_0_, bf16[256,1024]{1,0:T(8,128)(2,1)} %get-tuple-element.241.refs_1_, bf16[256,1024]{1,0:T(8,128)(2,1)} %get-tuple-element.234.refs_12_.refs_1_.refs_2_, bf16[256,1024]{1,0:T(8,128)(2,1)} %get-tuple-element.242.refs_3_, ...), custom_call_target="tpu_custom_call" | custom-call | flops 53687092 | bytes 200000 | tf_op jit(solution)/shard_map/weight_products/pallas_call | solution.py:956
  552.4 21.3 %attend_backward.3 = (bf16[2,8,128,256]{3,2,1,0:T(8,128)(2,1)}, bf16[2,8,128,256]{3,2,1,0:T(8,128)(2,1)}) custom-call(s32[2]{0:T(128)} %pad_add_fusion.pos_ref, bf16[8,128,256]{2,1,0:T(8,128)(2,1)} %join_grads.6.refs_0_, bf16[8,128,256]{2,1,0:T(8,128)(2,1)} %copy-done.20, bf16[8,128,256]{2,1,0:T(8,128)(2,1)} %join_grads.7.refs_2_, ...), custom_call_target="tpu_custom_call" | custom-call | flops 180000000 | bytes 260000 | tf_op jit(solution)/shard_map/attend_backward/pallas_call | solution.py:479
  579.4 19.3 %all_to_all.88.in_ref = bf16[8,128,256]{2,1,0:T(8,128)(2,1)} all-to-all(bf16[8,128,256]{2,1,0:T(8,128)(2,1)} %get-tuple-element.268), channel_id=1, replica_groups={{0,4,8,12,16,20,24,28},{2,6,10,14,18,22,26,30},{1,5,9,13,17,21,25,29},{..., dimensions={0} | all-to-all | bytes 1048576 | tf_op jit(solution)/shard_map/all_to_all | solution.py:49
  605.5 21.0 %all-to-all-done.16.in_ref = bf16[8,128,256]{2,1,0:T(8,128)(2,1)S(1)} async-done(((bf16[8,128,256]{2,1,0:T(8,128)(2,1)}), bf16[8,128,256]{2,1,0:T(8,128)(2,1)S(1)}, u32[]{:S(2)}, u32[]{:S(2)}) %all-to-all-start.16) | async-done | bytes 524320 | tf_op jit(solution)/shard_map/all_to_all | solution.py:49
  647.0 7.8 %collective-permute-done.32 = bf16[4,64,1024]{2,1,0:T(8,128)(2,1)} collective-permute-done((bf16[4,64,1024]{2,1,0:T(8,128)(2,1)S(1)}, bf16[4,64,1024]{2,1,0:T(8,128)(2,1)}, u32[]{:S(2)}, u32[]{:S(2)}) %collective-permute-start.32) | collective-permute-done | bytes 524320 | tf_op jit(solution)/shard_map/ppermute | solution.py:27
  668.0 11.7 %collective-permute-done.30.other_ref = bf16[256,1024]{1,0:T(8,128)(2,1)} collective-permute-done((bf16[256,1024]{1,0:T(8,128)(2,1)}, bf16[256,1024]{1,0:T(8,128)(2,1)}, u32[]{:S(2)}, u32[]{:S(2)}) %collective-permute-start.30) | collective-permute-done | bytes 524320 | tf_op jit(solution)/shard_map/ppermute | solution.py:27
  (351 shorter events, 320.1 us)
Async XLA Ops:
  7.2 52.6 %all-gather.3.cloned.1.call-start = ((), (), s32[]{:S(2)}) async-start(), calls=%async_computation.19 | async-start | bytes 3342336 | tf_op jit(solution)/shard_map/all_gather | solution.py:1102
  12.4 18.4 %collective-permute-start.5 = (f32[2,2,512]{2,1,0:T(2,128)S(1)}, f32[2,2,512]{2,1,0:T(2,128)S(1)}, u32[]{:S(2)}, u32[]{:S(2)}) collective-permute-start(f32[2,2,512]{2,1,0:T(2,128)S(1)} %pad_maximum_fusion.8), channel_id=1, source_target_pairs={{0,1},{1,0},{2,3},{3,2},{4,5},{5,4},{6,7},{7,6},{8,9},{9,8},{10,11... | collective-permute-start | bytes 24584 | tf_op jit(solution)/shard_map/ppermute | solution.py:27
  16.7 14.8 %all-to-all-start.1 = ((s32[16,2,256]{2,1,0:T(2,128)}), s32[16,2,256]{2,1,0:T(2,128)S(1)}, u32[]{:S(2)}, u32[]{:S(2)}) async-start(s32[16,2,256]{2,1,0:T(2,128)} %bitcast.6), calls=%async_computation.1 | async-start | bytes 65536 | tf_op jit(solution)/shard_map/all_to_all | solution.py:1111
  26.2 52.3 %collective-permute-start = (bf16[2,256,512]{2,1,0:T(8,128)(2,1)}, bf16[2,256,512]{2,1,0:T(8,128)(2,1)}, u32[]{:S(2)}, u32[]{:S(2)}) collective-permute-start(bf16[2,256,512]{2,1,0:T(8,128)(2,1)} %get-tuple-element.152), channel_id=1, source_target_pairs={{0,1},{1,0},{2,3},{3,2},{4,5},{5,4},{6,7},{7,6},{8,9},{9,8},{10,11... | collective-permute-start | bytes 1572872 | tf_op jit(solution)/shard_map/ppermute | solution.py:27
  26.8 25.7 %collective-permute-start.1 = (bf16[2,256,512]{2,1,0:T(8,128)(2,1)}, bf16[2,256,512]{2,1,0:T(8,128)(2,1)}, u32[]{:S(2)}, u32[]{:S(2)}) collective-permute-start(bf16[2,256,512]{2,1,0:T(8,128)(2,1)} %get-tuple-element.154), channel_id=1, source_target_pairs={{0,1},{1,0},{2,3},{3,2},{4,5},{5,4},{6,7},{7,6},{8,9},{9,8},{10,11... | collective-permute-start | bytes 1572872 | tf_op jit(solution)/shard_map/ppermute | solution.py:27
  28.3 53.1 %collective-permute-start.3 = (bf16[2,256,512]{2,1,0:T(8,128)(2,1)}, bf16[2,256,512]{2,1,0:T(8,128)(2,1)S(1)}, u32[]{:S(2)}, u32[]{:S(2)}) collective-permute-start(bf16[2,256,512]{2,1,0:T(8,128)(2,1)} %get-tuple-element.159), channel_id=1, source_target_pairs={{0,1},{1,0},{2,3},{3,2},{4,5},{5,4},{6,7},{7,6},{8,9},{9,8},{10,11... | collective-permute-start | bytes 1572872 | tf_op jit(solution)/shard_map/ppermute | solution.py:27
  28.8 52.5 %collective-permute-start.4 = (bf16[2,256,512]{2,1,0:T(8,128)(2,1)}, bf16[2,256,512]{2,1,0:T(8,128)(2,1)}, u32[]{:S(2)}, u32[]{:S(2)}) collective-permute-start(bf16[2,256,512]{2,1,0:T(8,128)(2,1)} %get-tuple-element.160), channel_id=1, source_target_pairs={{0,1},{1,0},{2,3},{3,2},{4,5},{5,4},{6,7},{7,6},{8,9},{9,8},{10,11... | collective-permute-start | bytes 1572872 | tf_op jit(solution)/shard_map/ppermute | solution.py:27
  63.5 22.4 %all-to-all-start = ((bf16[8,128,256]{2,1,0:T(8,128)(2,1)}), bf16[8,128,256]{2,1,0:T(8,128)(2,1)}, u32[]{:S(2)}, u32[]{:S(2)}) async-start(bf16[8,128,256]{2,1,0:T(8,128)(2,1)} %get-tuple-element.156), calls=%async_computation | async-start | bytes 1048576 | tf_op jit(solution)/shard_map/all_to_all | solution.py:49
  85.8 20.5 %all-to-all-start.2 = ((bf16[8,128,256]{2,1,0:T(8,128)(2,1)}), bf16[8,128,256]{2,1,0:T(8,128)(2,1)S(1)}, u32[]{:S(2)}, u32[]{:S(2)}) async-start(bf16[8,128,256]{2,1,0:T(8,128)(2,1)} %get-tuple-element.161), calls=%async_computation.2 | async-start | bytes 1048576 | tf_op jit(solution)/shard_map/all_to_all | solution.py:49
  91.8 113.1 %all-gather.5.cloned.1.call-start = ((), (), s32[]{:S(2)}) async-start(), calls=%async_computation.20 | async-start | bytes 3342336 | tf_op jit(solution)/shard_map/all_gather | solution.py:1147
  92.0 14.4 %collective-permute-start.2 = (bf16[8,128,256]{2,1,0:T(8,128)(2,1)}, bf16[8,128,256]{2,1,0:T(8,128)(2,1)}, u32[]{:S(2)}, u32[]{:S(2)}) collective-permute-start(bf16[8,128,256]{2,1,0:T(8,128)(2,1)} %all-to-all-done.refs_0_), channel_id=1, source_target_pairs={{0,2},{2,0},{4,6},{6,4},{8,10},{10,8},{12,14},{14,12},{16,18},{18,... | collective-permute-start | bytes 1572872 | tf_op jit(solution)/shard_map/ppermute | solution.py:27
  158.8 14.7 %collective-permute-start.8 = (bf16[256,1024]{1,0:T(8,128)(2,1)}, bf16[256,1024]{1,0:T(8,128)(2,1)S(1)}, u32[]{:S(2)}, u32[]{:S(2)}) collective-permute-start(bf16[256,1024]{1,0:T(8,128)(2,1)} %get-tuple-element.165.own_ref), channel_id=1, source_target_pairs={{0,1},{1,0},{2,3},{3,2},{4,5},{5,4},{6,7},{7,6},{8,9},{9,8},{10,11... | collective-permute-start | bytes 1572872 | tf_op jit(solution)/shard_map/ppermute | solution.py:27
  169.5 14.2 %collective-permute-start.10 = (bf16[256,1024]{1,0:T(8,128)(2,1)}, bf16[256,1024]{1,0:T(8,128)(2,1)}, u32[]{:S(2)}, u32[]{:S(2)}) collective-permute-start(bf16[256,1024]{1,0:T(8,128)(2,1)} %get-tuple-element.175.own_ref), channel_id=1, source_target_pairs={{0,1},{1,0},{2,3},{3,2},{4,5},{5,4},{6,7},{7,6},{8,9},{9,8},{10,11... | collective-permute-start | bytes 1572872 | tf_op jit(solution)/shard_map/ppermute | solution.py:27
  209.7 21.7 %all-to-all-start.6 = ((bf16[8,128,256]{2,1,0:T(8,128)(2,1)}), bf16[8,128,256]{2,1,0:T(8,128)(2,1)S(1)}, u32[]{:S(2)}, u32[]{:S(2)}) async-start(bf16[8,128,256]{2,1,0:T(8,128)(2,1)} %get-tuple-element.180), calls=%async_computation.6 | async-start | bytes 1048576 | tf_op jit(solution)/shard_map/all_to_all | solution.py:49
  231.4 16.9 %all-to-all-start.5 = ((bf16[8,128,256]{2,1,0:T(8,128)(2,1)}), bf16[8,128,256]{2,1,0:T(8,128)(2,1)S(1)}, u32[]{:S(2)}, u32[]{:S(2)}) async-start(bf16[8,128,256]{2,1,0:T(8,128)(2,1)} %get-tuple-element.178), calls=%async_computation.5 | async-start | bytes 1048576 | tf_op jit(solution)/shard_map/all_to_all | solution.py:49
  296.5 15.0 %collective-permute-start.15 = (bf16[256,1024]{1,0:T(8,128)(2,1)}, bf16[256,1024]{1,0:T(8,128)(2,1)S(1)}, u32[]{:S(2)}, u32[]{:S(2)}) collective-permute-start(bf16[256,1024]{1,0:T(8,128)(2,1)} %get-tuple-element.184.own_ref), channel_id=1, source_target_pairs={{0,1},{1,0},{2,3},{3,2},{4,5},{5,4},{6,7},{7,6},{8,9},{9,8},{10,11... | collective-permute-start | bytes 1572872 | tf_op jit(solution)/shard_map/ppermute | solution.py:27
  306.3 23.5 %collective-permute-start.16 = (bf16[256,1024]{1,0:T(8,128)(2,1)}, bf16[256,1024]{1,0:T(8,128)(2,1)}, u32[]{:S(2)}, u32[]{:S(2)}) collective-permute-start(bf16[256,1024]{1,0:T(8,128)(2,1)} %get-tuple-element.190.own_ref), channel_id=1, source_target_pairs={{0,1},{1,0},{2,3},{3,2},{4,5},{5,4},{6,7},{7,6},{8,9},{9,8},{10,11... | collective-permute-start | bytes 1572872 | tf_op jit(solution)/shard_map/ppermute | solution.py:27
  329.7 19.5 %collective-permute-start.18 = (bf16[256,1024]{1,0:T(8,128)(2,1)}, bf16[256,1024]{1,0:T(8,128)(2,1)S(1)}, u32[]{:S(2)}, u32[]{:S(2)}) collective-permute-start(bf16[256,1024]{1,0:T(8,128)(2,1)} %get-tuple-element.200.own_ref), channel_id=1, source_target_pairs={{0,1},{1,0},{2,3},{3,2},{4,5},{5,4},{6,7},{7,6},{8,9},{9,8},{10,11... | collective-permute-start | bytes 1572872 | tf_op jit(solution)/shard_map/ppermute | solution.py:27
  354.4 14.2 %all-to-all-start.9 = ((bf16[8,128,128]{2,1,0:T(8,128)(2,1)}), bf16[8,128,128]{2,1,0:T(8,128)(2,1)S(1)}, u32[]{:S(2)}, u32[]{:S(2)}) async-start(bf16[8,128,128]{2,1,0:T(8,128)(2,1)} %get-tuple-element.201), calls=%async_computation.9 | async-start | bytes 524288 | tf_op jit(solution)/shard_map/all_to_all | solution.py:49
  377.4 196.5 %reduce-scatter.3.cloned.1.call-start = ((), (), s32[]{:S(2)}) async-start(), calls=%async_computation.21 | async-start | bytes 10027008 | tf_op jit(solution)/shard_map/reduce_scatter | solution.py:1062
  453.3 18.3 %all-to-all-start.12 = ((bf16[8,128,256]{2,1,0:T(8,128)(2,1)}), bf16[8,128,256]{2,1,0:T(8,128)(2,1)S(1)}, u32[]{:S(2)}, u32[]{:S(2)}) async-start(bf16[8,128,256]{2,1,0:T(8,128)(2,1)} %get-tuple-element.224), calls=%async_computation.12 | async-start | bytes 1048576 | tf_op jit(solution)/shard_map/all_to_all | solution.py:49
  456.9 19.0 %collective-permute-start.23 = (bf16[256,1024]{1,0:T(8,128)(2,1)}, bf16[256,1024]{1,0:T(8,128)(2,1)}, u32[]{:S(2)}, u32[]{:S(2)}) collective-permute-start(bf16[256,1024]{1,0:T(8,128)(2,1)} %get-tuple-element.219.refs_1_), channel_id=1, source_target_pairs={{0,1},{1,0},{2,3},{3,2},{4,5},{5,4},{6,7},{7,6},{8,9},{9,8},{10,11... | collective-permute-start | bytes 1572872 | tf_op jit(solution)/shard_map/ppermute | solution.py:27
  500.2 23.8 %collective-permute-start.26 = (bf16[256,1024]{1,0:T(8,128)(2,1)}, bf16[256,1024]{1,0:T(8,128)(2,1)S(1)}, u32[]{:S(2)}, u32[]{:S(2)}) collective-permute-start(bf16[256,1024]{1,0:T(8,128)(2,1)} %get-tuple-element.237.own_ref), channel_id=1, source_target_pairs={{0,1},{1,0},{2,3},{3,2},{4,5},{5,4},{6,7},{7,6},{8,9},{9,8},{10,11... | collective-permute-start | bytes 1572872 | tf_op jit(solution)/shard_map/ppermute | solution.py:27
  504.7 21.7 %all-to-all-start.13 = ((bf16[8,128,128]{2,1,0:T(8,128)(2,1)}), bf16[8,128,128]{2,1,0:T(8,128)(2,1)S(1)}, u32[]{:S(2)}, u32[]{:S(2)}) async-start(bf16[8,128,128]{2,1,0:T(8,128)(2,1)} %get-tuple-element.239), calls=%async_computation.13 | async-start | bytes 524288 | tf_op jit(solution)/shard_map/all_to_all | solution.py:49
  509.8 213.5 %reduce-scatter.5.cloned.1.call-start = ((), (), s32[]{:S(2)}) async-start(), calls=%async_computation.22 | async-start | bytes 12255232 | tf_op jit(solution)/shard_map/reduce_scatter | solution.py:1062
  598.6 27.9 %all-to-all-start.16 = ((bf16[8,128,256]{2,1,0:T(8,128)(2,1)}), bf16[8,128,256]{2,1,0:T(8,128)(2,1)S(1)}, u32[]{:S(2)}, u32[]{:S(2)}) async-start(bf16[8,128,256]{2,1,0:T(8,128)(2,1)} %get-tuple-element.274), calls=%async_computation.17 | async-start | bytes 1048576 | tf_op jit(solution)/shard_map/all_to_all | solution.py:49
  640.6 14.1 %collective-permute-start.32 = (bf16[4,64,1024]{2,1,0:T(8,128)(2,1)S(1)}, bf16[4,64,1024]{2,1,0:T(8,128)(2,1)}, u32[]{:S(2)}, u32[]{:S(2)}) collective-permute-start(bf16[4,64,1024]{2,1,0:T(8,128)(2,1)S(1)} %dynamic-slice_bitcast_fusion.1), channel_id=1, source_target_pairs={{0,4},{2,6},{4,0},{6,2},{8,12},{10,14},{12,8},{14,10},{16,20},{18,... | collective-permute-start | bytes 1572872 | tf_op jit(solution)/shard_map/ppermute | solution.py:27
  643.2 16.4 %collective-permute-start.17 = (bf16[512,512]{1,0:T(8,128)(2,1)}, bf16[512,512]{1,0:T(8,128)(2,1)}, u32[]{:S(2)}, u32[]{:S(2)}) collective-permute-start(bf16[512,512]{1,0:T(8,128)(2,1)} %pad_maximum_fusion.2), channel_id=1, source_target_pairs={{0,1},{1,0},{2,3},{3,2},{4,5},{5,4},{6,7},{7,6},{8,9},{9,8},{10,11... | collective-permute-start | bytes 1572872 | tf_op jit(solution)/shard_map/ppermute | solution.py:27
  644.9 40.3 %collective-permute-start.33 = (bf16[256,1024]{1,0:T(8,128)(2,1)}, bf16[256,1024]{1,0:T(8,128)(2,1)}, u32[]{:S(2)}, u32[]{:S(2)}) collective-permute-start(bf16[256,1024]{1,0:T(8,128)(2,1)} %get-tuple-element.277.own_ref), channel_id=1, source_target_pairs={{0,1},{1,0},{2,3},{3,2},{4,5},{5,4},{6,7},{7,6},{8,9},{9,8},{10,11... | collective-permute-start | bytes 1572872 | tf_op jit(solution)/shard_map/ppermute | solution.py:27
  645.3 34.4 %collective-permute-start.30 = (bf16[256,1024]{1,0:T(8,128)(2,1)}, bf16[256,1024]{1,0:T(8,128)(2,1)}, u32[]{:S(2)}, u32[]{:S(2)}) collective-permute-start(bf16[256,1024]{1,0:T(8,128)(2,1)} %get-tuple-element.269.own_ref), channel_id=1, source_target_pairs={{0,1},{1,0},{2,3},{3,2},{4,5},{5,4},{6,7},{7,6},{8,9},{9,8},{10,11... | collective-permute-start | bytes 1572872 | tf_op jit(solution)/shard_map/ppermute | solution.py:27
  656.1 27.2 %collective-permute-start.34 = (bf16[2,64,1024]{2,1,0:T(8,128)(2,1)S(1)}, bf16[2,64,1024]{2,1,0:T(8,128)(2,1)}, u32[]{:S(2)}, u32[]{:S(2)}) collective-permute-start(bf16[2,64,1024]{2,1,0:T(8,128)(2,1)S(1)} %dynamic-slice_bitcast_fusion.2), channel_id=1, source_target_pairs={{0,8},{2,10},{4,12},{6,14},{8,0},{10,2},{12,4},{14,6},{16,24},{18,... | collective-permute-start | bytes 786440 | tf_op jit(solution)/shard_map/ppermute | solution.py:27
  693.7 17.2 %collective-permute-start.40 = (bf16[1,64,1024]{2,1,0:T(8,128)(2,1)}, bf16[1,64,1024]{2,1,0:T(8,128)(2,1)}, u32[]{:S(2)}, u32[]{:S(2)}) collective-permute-start(bf16[1,64,1024]{2,1,0:T(8,128)(2,1)} %constant_dynamic-slice_fusion.12), channel_id=1, source_target_pairs={{0,16},{2,18},{4,20},{6,22},{8,24},{10,26},{12,28},{14,30},{16,0},... | collective-permute-start | bytes 393224 | tf_op jit(solution)/shard_map/ppermute | solution.py:27
  (81 other events, 626.4 us)
Sparse Core Ops, SparseCore 0:
  11.8 47.8 all-gather.2
  136.6 46.6 all-gather.4
  453.4 116.3 reduce-scatter.2
  574.3 145.1 reduce-scatter.4

commit v5 on v4

--- a/solution.py
+++ b/solution.py
@@ -1172,7 +1172,6 @@
         lax.dynamic_slice_in_dim(part, (1 - narrow_index) * half, half, 1) for part in ffn_parts
     ]
     got = swap(jnp.concatenate(sent), "narrow", 1)
-    second_out = narrow_chunks(pos, second, seqs, LAYERS - 1, [*ffn_parts, got, down_bias])
     summed, waiting = [], []
     done = []
     early_smalls, late_smalls = [None] * LAYERS, [None] * LAYERS
@@ -1200,10 +1199,7 @@
         pairs = waiting + [(ffn_in, low), (branch, hidden)]
         widths = [right[0].shape[1] for _, right in pairs]
         columns = sum(widths) + head_width
-        if layer == 0:
-            products = [weight_products(pairs, columns)]
-        else:
-            products = []
+        products = [weight_products(pairs, columns)]
         out_low, units = [], []
         ffn_gain_grad, ffn_bias_grad, out_bias_grad = 0.0, 0.0, 0.0
         for q in chunks:
@@ -1224,7 +1220,9 @@
             summed += sum_rows(*products, widths + [head_width])
         sources = []
         for q in chunks:
-            own = join_grads(q, attn, stats, units[q], products if q > 0 else ())
+            own = join_grads(
+                q, attn, stats, units[q], products if q > 0 and layer == 0 else ()
+            )
             sources += [own, swap(own, "wide", 1)]
         early_small = jnp.concatenate(
             [
@@ -1238,15 +1236,16 @@
         grad_tok = []
         backs = [chip_exchange(units[q]) for q in chunks]
         after = []
-        if layer > 0:
-            pairs.append((out_low, attn_tok))
         merged = []
         for q in chunks:
             part, grad_tok_q = merge_units(seqs, backs[q], gathered[layer], 0, after + grad_tok)
             if layer > 0 and q == 0:
-                products = weight_products(pairs, columns, after=[grad_tok_q])
-                summed += sum_rows(products, widths + [head_width])
-                after = [products]
+                after = [
+                    weight_products(
+                        [(out_low, attn_tok)], columns, columns - head_width, *products, [grad_tok_q]
+                    )
+                ]
+                summed += sum_rows(*after, widths + [head_width])
             grad_tok.append(grad_tok_q)
             merged.append((part, swap(part, "narrow", 1)))
         waiting = [(normed, grad_tok)]
@@ -1265,7 +1264,7 @@
     for q in chunks:
         norm, stream, own, other, gain = before[q]
         grad_second[q], gain_q, shift_q = finish_attention(
-            norm, stream, own, other, grad_second[q], gain, stages[q + 1 : q + 2]
+            norm, stream, own, other, grad_second[q], gain, stages[1:2] if q > 0 else ()
         )
         late_gain += gain_q
         late_shift += shift_q
@@ -1276,6 +1275,9 @@
     ]
     first_grad = narrow_chunks(pos, grad_first, seqs)
     second_grad = narrow_chunks(pos, grad_second, seqs)
+    second_out = narrow_chunks(
+        pos, second, seqs, LAYERS - 1, [*ffn_parts, got, down_bias], grad_second[-1:]
+    )
 
     small = sum_wide(jnp.stack(small_grads))
     other = swap(small[:, :4], "narrow", 1)

time: 748 us -> 741 us (level)
    pallas_call x4 -> x5, Pallas kernels: 34.6 us -> 35.9 us  [weight_products(): pl.pallas_call(functools.partial(products_kernel, counts), grid=(start,),...]
    unnamed x118 -> x124, local copies, waits for them, and re-layouts: 16.7 us -> 17.7 us
  transfers between devices with their start and end apart: 58 -> 58, of which waited for: 33 -> 34; matrix products, arithmetic and copies ran while one was open for 6% -> 5% of each run, Pallas kernels for 28% -> 29%
where the time goes in v5:
time: 741 us; the launch traced here: 731 us
  Pallas kernels  304 us (41%)
  waiting for transfers between devices  188 us (25%)
  starting transfers between devices  94.9 us (13%)
  blocking collectives  68 us (9%)
  local copies, waits for them, and re-layouts  32.6 us (4%)
  other arithmetic  27.7 us (4%)
  between operations  15.1 us (2%)
    ppermute x41, waiting for transfers between devices, swap(): lax.ppermute(value, axis, [(source, source ^ mask) for source in range(co...  97.4 us
    all_to_all x12, waiting for transfers between devices, chip_exchange(): lax.all_to_all(units, 'wide', 0, 0, tiled=True, axis_index_groups=groups)  90.3 us
    all_to_all x4, blocking collectives, chip_exchange(): lax.all_to_all(units, 'wide', 0, 0, tiled=True, axis_index_groups=groups)  68 us
    all_to_all x12, starting transfers between devices, chip_exchange(): lax.all_to_all(units, 'wide', 0, 0, tiled=True, axis_index_groups=groups)  56.4 us
    pallas_call x2, Pallas kernels, attention_backward(): pl.pallas_call(functools.partial(backward_kernel, chunks, len(after)), ou...  42.9 us
    pallas_call x4, Pallas kernels, feed_back(): pl.pallas_call(functools.partial(ffn_back_kernel, None if before is None...  39.4 us
    pallas_call x2, Pallas kernels, attention_forward(): pl.pallas_call(functools.partial(forward_kernel, chunks, len(after)), out...  38.5 us
    pallas_call x5, Pallas kernels, weight_products(): pl.pallas_call(functools.partial(products_kernel, counts), grid=(start,),...  35.9 us
  transfers between devices with their start and end apart: 58, of which 34 were waited for; matrix products, arithmetic and copies ran while one was open for 5% of the time, Pallas kernels for 29%

profile of v5, /device:TPU:0, one launch (start us, length us, event | category | flops | bytes accessed | tf_op | source)
XLA Modules:
  0.0 731.4 jit_solution(4480352763372587338)
XLA Ops:
  29.6 13.0 %collective-permute-done.5 = f32[2,2,512]{2,1,0:T(2,128)S(1)} collective-permute-done((f32[2,2,512]{2,1,0:T(2,128)S(1)}, f32[2,2,512]{2,1,0:T(2,128)S(1)}, u32[]{:S(2)}, u32[]{:S(2)}) %collective-permute-start.5) | collective-permute-done | bytes 8224 | tf_op jit(solution)/shard_map/ppermute | solution.py:27
  68.1 6.0 all-to-all-start.2
  77.8 9.9 %all-to-all-done.2.refs_2_ = bf16[8,128,256]{2,1,0:T(8,128)(2,1)S(1)} async-done(((bf16[8,128,256]{2,1,0:T(8,128)(2,1)}), bf16[8,128,256]{2,1,0:T(8,128)(2,1)S(1)}, u32[]{:S(2)}, u32[]{:S(2)}) %all-to-all-start.2) | async-done | bytes 524320 | tf_op jit(solution)/shard_map/all_to_all | solution.py:49
  92.0 13.2 %all-to-all-done.refs_0_ = bf16[8,128,256]{2,1,0:T(8,128)(2,1)S(1)} async-done(((bf16[8,128,256]{2,1,0:T(8,128)(2,1)}), bf16[8,128,256]{2,1,0:T(8,128)(2,1)S(1)}, u32[]{:S(2)}, u32[]{:S(2)}) %all-to-all-start) | async-done | bytes 524320 | tf_op jit(solution)/shard_map/all_to_all | solution.py:49
  107.2 19.2 %attend_forward.2 = (bf16[2,4096,256]{2,1,0:T(8,128)(2,1)}, bf16[2,8,128,256]{3,2,1,0:T(8,128)(2,1)}, bf16[2,8,128,256]{3,2,1,0:T(8,128)(2,1)}) custom-call(s32[2]{0:T(128)} %pad_add_fusion.pos_ref, bf16[8,128,256]{2,1,0:T(8,128)(2,1)} %copy-done.7, bf16[8,128,256]{2,1,0:T(8,128)(2,1)} %collective-permute-done.2.refs_1_, bf16[8,128,256]{2,1,0:T(8,128)(2,1)} %copy-done.6, ...), custom_call_target="tpu_custom_call" | custom-call | flops 160000000 | bytes 240000 | tf_op jit(solution)/shard_map/attend_forward/pallas_call | solution.py:449
  135.2 16.0 %all_to_all.85.in_ref = bf16[8,128,128]{2,1,0:T(8,128)(2,1)} all-to-all(bf16[8,128,128]{2,1,0:T(8,128)(2,1)} %get-tuple-element.164.refs_2_), channel_id=1, replica_groups={{0,4,8,12,16,20,24,28},{2,6,10,14,18,22,26,30},{1,5,9,13,17,21,25,29},{..., dimensions={0} | all-to-all | bytes 524288 | tf_op jit(solution)/shard_map/all_to_all | solution.py:49
  173.0 8.1 %feed_forward.4 = (f32[256,1024]{1,0:T(8,128)}, bf16[256,1024]{1,0:T(8,128)(2,1)}, f32[256,2048]{1,0:T(8,128)}, bf16[256,1024]{1,0:T(8,128)(2,1)}) custom-call(f32[256,1024]{1,0:T(8,128)} %get-tuple-element.153.refs_4_.stream_ref, bf16[256,1024]{1,0:T(8,128)(2,1)} %get-tuple-element.165.own_ref, bf16[256,1024]{1,0:T(8,128)(2,1)} %copy-done.24, ...), custom_call_target="tpu_custom_call" | custom-call | flops 21474836 | bytes 140000 | tf_op jit(solution)/shard_map/feed_forward/pallas_call | solution.py:817
  182.5 8.0 %feed_forward.5 = (f32[256,1024]{1,0:T(8,128)}, bf16[256,1024]{1,0:T(8,128)(2,1)}, f32[256,2048]{1,0:T(8,128)}, bf16[256,1024]{1,0:T(8,128)(2,1)}) custom-call(f32[256,1024]{1,0:T(8,128)} %get-tuple-element.158.refs_5_.stream_ref, bf16[256,1024]{1,0:T(8,128)(2,1)} %get-tuple-element.175.own_ref, bf16[256,1024]{1,0:T(8,128)(2,1)} %collective-permute-done.10.other_ref, ...), custom_call_target="tpu_custom_call" | custom-call | flops 21474836 | bytes 140000 | tf_op jit(solution)/shard_map/feed_forward/pallas_call | solution.py:817
  192.1 11.6 %collective-permute-done.12.refs_1_ = bf16[256,1024]{1,0:T(8,128)(2,1)S(1)} collective-permute-done((bf16[256,1024]{1,0:T(8,128)(2,1)}, bf16[256,1024]{1,0:T(8,128)(2,1)S(1)}, u32[]{:S(2)}, u32[]{:S(2)}) %collective-permute-start.12) | collective-permute-done | bytes 524320 | tf_op jit(solution)/shard_map/ppermute | solution.py:27
  215.1 10.7 %collective-permute-done.9.refs_1_ = bf16[256,1024]{1,0:T(8,128)(2,1)} collective-permute-done((bf16[256,1024]{1,0:T(8,128)(2,1)}, bf16[256,1024]{1,0:T(8,128)(2,1)}, u32[]{:S(2)}, u32[]{:S(2)}) %collective-permute-start.9) | collective-permute-done | bytes 524320 | tf_op jit(solution)/shard_map/ppermute | solution.py:27
  235.9 10.8 %all-to-all-done.5.refs_0_ = bf16[8,128,256]{2,1,0:T(8,128)(2,1)S(1)} async-done(((bf16[8,128,256]{2,1,0:T(8,128)(2,1)}), bf16[8,128,256]{2,1,0:T(8,128)(2,1)S(1)}, u32[]{:S(2)}, u32[]{:S(2)}) %all-to-all-start.5) | async-done | bytes 524320 | tf_op jit(solution)/shard_map/all_to_all | solution.py:49
  248.8 19.3 %attend_forward.3 = (bf16[2,4096,256]{2,1,0:T(8,128)(2,1)}, bf16[2,8,128,256]{3,2,1,0:T(8,128)(2,1)}, bf16[2,8,128,256]{3,2,1,0:T(8,128)(2,1)}) custom-call(s32[2]{0:T(128)} %pad_add_fusion.pos_ref, bf16[8,128,256]{2,1,0:T(8,128)(2,1)} %copy-done.8, bf16[8,128,256]{2,1,0:T(8,128)(2,1)} %collective-permute-done.11.refs_1_, bf16[8,128,256]{2,1,0:T(8,128)(2,1)} %copy-done.5, ...), custom_call_target="tpu_custom_call" | custom-call | flops 160000000 | bytes 240000 | tf_op jit(solution)/shard_map/attend_forward/pallas_call | solution.py:449
  275.5 13.5 %all_to_all.86.in_ref = bf16[8,128,128]{2,1,0:T(8,128)(2,1)} all-to-all(bf16[8,128,128]{2,1,0:T(8,128)(2,1)} %get-tuple-element.183), channel_id=1, replica_groups={{0,4,8,12,16,20,24,28},{2,6,10,14,18,22,26,30},{1,5,9,13,17,21,25,29},{..., dimensions={0} | all-to-all | bytes 524288 | tf_op jit(solution)/shard_map/all_to_all | solution.py:49
  295.3 6.4 all-to-all-done.8.in_ref
  310.3 8.0 %feed_forward.6 = (f32[256,1024]{1,0:T(8,128)}, bf16[256,1024]{1,0:T(8,128)(2,1)}, f32[256,2048]{1,0:T(8,128)}, bf16[256,1024]{1,0:T(8,128)(2,1)}) custom-call(f32[256,1024]{1,0:T(8,128)} %get-tuple-element.173.stream_ref, bf16[256,1024]{1,0:T(8,128)(2,1)} %get-tuple-element.184.own_ref, bf16[256,1024]{1,0:T(8,128)(2,1)} %collective-permute-done.15.other_ref, ...), custom_call_target="tpu_custom_call" | custom-call | flops 21474836 | bytes 140000 | tf_op jit(solution)/shard_map/feed_forward/pallas_call | solution.py:817
  318.3 9.2 %feed_back.4 = (bf16[256,1024]{1,0:T(8,128)(2,1)}, bf16[256,2048]{1,0:T(8,128)(2,1)}, bf16[256,2048]{1,0:T(8,128)(2,1)}, f32[1,1024]{1,0:T(1,128)}, f32[1,2048]{1,0:T(1,128)}, /*index=5*/bf16[256,1024]{1,0:T(8,128)(2,1)}) custom-call(f32[256,1024]{1,0:T(8,128)} %get-tuple-element.167.refs_0_.refs_3_, bf16[2,1024,2048]{2,1,0:T(8,128)(2,1)} %refs_5_.3, ...), custom_call_target="tpu_custom_call" | custom-call | flops 21474836 | bytes 150000 | tf_op jit(solution)/shard_map/feed_back/pallas_call | solution.py:904
  328.5 8.0 %feed_forward.7 = (f32[256,1024]{1,0:T(8,128)}, bf16[256,1024]{1,0:T(8,128)(2,1)}, f32[256,2048]{1,0:T(8,128)}, bf16[256,1024]{1,0:T(8,128)(2,1)}) custom-call(f32[256,1024]{1,0:T(8,128)} %get-tuple-element.189.stream_ref, bf16[256,1024]{1,0:T(8,128)(2,1)} %get-tuple-element.190.own_ref, bf16[256,1024]{1,0:T(8,128)(2,1)} %copy-done.25, ...), custom_call_target="tpu_custom_call" | custom-call | flops 21474836 | bytes 140000 | tf_op jit(solution)/shard_map/feed_forward/pallas_call | solution.py:817
  336.5 9.2 %feed_back.5 = (bf16[256,1024]{1,0:T(8,128)(2,1)}, bf16[256,2048]{1,0:T(8,128)(2,1)}, bf16[256,2048]{1,0:T(8,128)(2,1)}, f32[1,1024]{1,0:T(1,128)}, f32[1,2048]{1,0:T(1,128)}, /*index=5*/bf16[256,1024]{1,0:T(8,128)(2,1)}) custom-call(f32[256,1024]{1,0:T(8,128)} %get-tuple-element.168.refs_1_.refs_0_.refs_3_, bf16[2,1024,2048]{2,1,0:T(8,128)(2,1)} %refs_5_.3, ...), custom_call_target="tpu_custom_call" | custom-call | flops 21474836 | bytes 150000 | tf_op jit(solution)/shard_map/feed_back/pallas_call | solution.py:904
  352.1 6.0 all-to-all-start.9
  358.2 11.3 %weight_products.5.refs_1_.refs_4_ = bf16[1024,4608]{1,0:T(8,128)(2,1)} custom-call(bf16[256,1024]{1,0:T(8,128)(2,1)} %get-tuple-element.191.refs_1_.refs_0_, bf16[256,1024]{1,0:T(8,128)(2,1)} %get-tuple-element.206.refs_1_, bf16[256,2048]{1,0:T(8,128)(2,1)} %get-tuple-element.207.refs_2_, bf16[256,2048]{1,0:T(8,128)(2,1)} %get-tuple-element.208.refs_3_, ...), custom_call_target="tpu_custom_call" | custom-call | flops 42949672 | bytes 200000 | tf_op jit(solution)/shard_map/weight_products/pallas_call | solution.py:956
  374.9 6.1 all-to-all-start.10
  394.5 21.5 %attend_backward.2 = (bf16[2,8,128,256]{3,2,1,0:T(8,128)(2,1)}, bf16[2,8,128,256]{3,2,1,0:T(8,128)(2,1)}) custom-call(s32[2]{0:T(128)} %pad_add_fusion.pos_ref, bf16[8,128,256]{2,1,0:T(8,128)(2,1)} %join_grads.4.refs_0_, bf16[8,128,256]{2,1,0:T(8,128)(2,1)} %copy-done.20, bf16[8,128,256]{2,1,0:T(8,128)(2,1)} %join_grads.5.refs_2_, ...), custom_call_target="tpu_custom_call" | custom-call | flops 180000000 | bytes 260000 | tf_op jit(solution)/shard_map/attend_backward/pallas_call | solution.py:479
  421.7 19.2 %all_to_all.87.in_ref = bf16[8,128,256]{2,1,0:T(8,128)(2,1)} all-to-all(bf16[8,128,256]{2,1,0:T(8,128)(2,1)} %get-tuple-element.227), channel_id=1, replica_groups={{0,4,8,12,16,20,24,28},{2,6,10,14,18,22,26,30},{1,5,9,13,17,21,25,29},{..., dimensions={0} | all-to-all | bytes 1048576 | tf_op jit(solution)/shard_map/all_to_all | solution.py:49
  451.0 14.5 %all-to-all-done.13.in_ref = bf16[8,128,256]{2,1,0:T(8,128)(2,1)S(1)} async-done(((bf16[8,128,256]{2,1,0:T(8,128)(2,1)}), bf16[8,128,256]{2,1,0:T(8,128)(2,1)S(1)}, u32[]{:S(2)}, u32[]{:S(2)}) %all-to-all-start.13) | async-done | bytes 524320 | tf_op jit(solution)/shard_map/all_to_all | solution.py:49
  470.0 10.5 %feed_back.6 = (f32[256,1024]{1,0:T(8,128)}, f32[1,1024]{1,0:T(1,128)}, f32[1,1024]{1,0:T(1,128)}, bf16[256,1024]{1,0:T(8,128)(2,1)}, bf16[256,2048]{1,0:T(8,128...) custom-call(f32[256,1024]{1,0:T(8,128)} %get-tuple-element.193.refs_0_, ...), custom_call_target="tpu_custom_call" | custom-call | flops 21474836 | bytes 150000 | tf_op jit(solution)/shard_map/feed_back/pallas_call | solution.py:904
  483.6 10.5 %feed_back.7 = (f32[256,1024]{1,0:T(8,128)}, f32[1,1024]{1,0:T(1,128)}, f32[1,1024]{1,0:T(1,128)}, bf16[256,1024]{1,0:T(8,128)(2,1)}, bf16[256,2048]{1,0:T(8,128...) custom-call(f32[256,1024]{1,0:T(8,128)} %get-tuple-element.194.refs_0_.re, ...), custom_call_target="tpu_custom_call" | custom-call | flops 21474836 | bytes 150000 | tf_op jit(solution)/shard_map/feed_back/pallas_call | solution.py:904
  503.7 14.1 %weight_products.7.refs_1_.refs_4_ = bf16[1024,5632]{1,0:T(8,128)(2,1)} custom-call(bf16[256,1024]{1,0:T(8,128)(2,1)} %get-tuple-element.241.refs_0_, bf16[256,1024]{1,0:T(8,128)(2,1)} %get-tuple-element.242.refs_1_, bf16[256,1024]{1,0:T(8,128)(2,1)} %get-tuple-element.236.refs_5_.refs_1_.refs_2_, bf16[256,1024]{1,0:T(8,128)(2,1)} %get-tuple-element.243.refs_3_, ...), custom_call_target="tpu_custom_call" | custom-call | flops 53687092 | bytes 200000 | tf_op jit(solution)/shard_map/weight_products/pallas_call | solution.py:956
  546.2 21.4 %attend_backward.3 = (bf16[2,8,128,256]{3,2,1,0:T(8,128)(2,1)}, bf16[2,8,128,256]{3,2,1,0:T(8,128)(2,1)}) custom-call(s32[2]{0:T(128)} %pad_add_fusion.pos_ref, bf16[8,128,256]{2,1,0:T(8,128)(2,1)} %join_grads.6.refs_0_, bf16[8,128,256]{2,1,0:T(8,128)(2,1)} %copy-done.21, bf16[8,128,256]{2,1,0:T(8,128)(2,1)} %join_grads.7.refs_2_, ...), custom_call_target="tpu_custom_call" | custom-call | flops 180000000 | bytes 260000 | tf_op jit(solution)/shard_map/attend_backward/pallas_call | solution.py:479
  573.3 19.3 %all_to_all.88.in_ref = bf16[8,128,256]{2,1,0:T(8,128)(2,1)} all-to-all(bf16[8,128,256]{2,1,0:T(8,128)(2,1)} %get-tuple-element.267), channel_id=1, replica_groups={{0,4,8,12,16,20,24,28},{2,6,10,14,18,22,26,30},{1,5,9,13,17,21,25,29},{..., dimensions={0} | all-to-all | bytes 1048576 | tf_op jit(solution)/shard_map/all_to_all | solution.py:49
  599.4 21.0 %all-to-all-done.15.in_ref = bf16[8,128,256]{2,1,0:T(8,128)(2,1)S(1)} async-done(((bf16[8,128,256]{2,1,0:T(8,128)(2,1)}), bf16[8,128,256]{2,1,0:T(8,128)(2,1)S(1)}, u32[]{:S(2)}, u32[]{:S(2)}) %all-to-all-start.15) | async-done | bytes 524320 | tf_op jit(solution)/shard_map/all_to_all | solution.py:49
  693.9 11.6 %collective-permute-done.39 = bf16[2,64,1024]{2,1,0:T(8,128)(2,1)} collective-permute-done((bf16[2,64,1024]{2,1,0:T(8,128)(2,1)S(1)}, bf16[2,64,1024]{2,1,0:T(8,128)(2,1)}, u32[]{:S(2)}, u32[]{:S(2)}) %collective-permute-start.39) | collective-permute-done | bytes 262176 | tf_op jit(solution)/shard_map/ppermute | solution.py:27
  709.1 7.3 collective-permute-done.40
  (358 shorter events, 321.9 us)
Async XLA Ops:
  7.2 57.1 %all-gather.3.cloned.1.call-start = ((), (), s32[]{:S(2)}) async-start(), calls=%async_computation.19 | async-start | bytes 3342336 | tf_op jit(solution)/shard_map/all_gather | solution.py:1102
  15.3 40.9 %collective-permute-start.1 = (bf16[2,256,512]{2,1,0:T(8,128)(2,1)}, bf16[2,256,512]{2,1,0:T(8,128)(2,1)}, u32[]{:S(2)}, u32[]{:S(2)}) collective-permute-start(bf16[2,256,512]{2,1,0:T(8,128)(2,1)} %get-tuple-element.154), channel_id=1, source_target_pairs={{0,1},{1,0},{2,3},{3,2},{4,5},{5,4},{6,7},{7,6},{8,9},{9,8},{10,11... | collective-permute-start | bytes 1572872 | tf_op jit(solution)/shard_map/ppermute | solution.py:27
  18.2 40.8 %collective-permute-start = (bf16[2,256,512]{2,1,0:T(8,128)(2,1)}, bf16[2,256,512]{2,1,0:T(8,128)(2,1)}, u32[]{:S(2)}, u32[]{:S(2)}) collective-permute-start(bf16[2,256,512]{2,1,0:T(8,128)(2,1)} %get-tuple-element.152), channel_id=1, source_target_pairs={{0,1},{1,0},{2,3},{3,2},{4,5},{5,4},{6,7},{7,6},{8,9},{9,8},{10,11... | collective-permute-start | bytes 1572872 | tf_op jit(solution)/shard_map/ppermute | solution.py:27
  18.3 24.3 %collective-permute-start.5 = (f32[2,2,512]{2,1,0:T(2,128)S(1)}, f32[2,2,512]{2,1,0:T(2,128)S(1)}, u32[]{:S(2)}, u32[]{:S(2)}) collective-permute-start(f32[2,2,512]{2,1,0:T(2,128)S(1)} %pad_maximum_fusion.8), channel_id=1, source_target_pairs={{0,1},{1,0},{2,3},{3,2},{4,5},{5,4},{6,7},{7,6},{8,9},{9,8},{10,11... | collective-permute-start | bytes 24584 | tf_op jit(solution)/shard_map/ppermute | solution.py:27
  21.0 22.3 %all-to-all-start.1 = ((s32[16,2,256]{2,1,0:T(2,128)}), s32[16,2,256]{2,1,0:T(2,128)S(1)}, u32[]{:S(2)}, u32[]{:S(2)}) async-start(s32[16,2,256]{2,1,0:T(2,128)} %bitcast.6), calls=%async_computation.1 | async-start | bytes 65536 | tf_op jit(solution)/shard_map/all_to_all | solution.py:1111
  26.9 35.0 %collective-permute-start.3 = (bf16[2,256,512]{2,1,0:T(8,128)(2,1)}, bf16[2,256,512]{2,1,0:T(8,128)(2,1)S(1)}, u32[]{:S(2)}, u32[]{:S(2)}) collective-permute-start(bf16[2,256,512]{2,1,0:T(8,128)(2,1)} %get-tuple-element.159), channel_id=1, source_target_pairs={{0,1},{1,0},{2,3},{3,2},{4,5},{5,4},{6,7},{7,6},{8,9},{9,8},{10,11... | collective-permute-start | bytes 1572872 | tf_op jit(solution)/shard_map/ppermute | solution.py:27
  27.5 36.9 %collective-permute-start.4 = (bf16[2,256,512]{2,1,0:T(8,128)(2,1)}, bf16[2,256,512]{2,1,0:T(8,128)(2,1)}, u32[]{:S(2)}, u32[]{:S(2)}) collective-permute-start(bf16[2,256,512]{2,1,0:T(8,128)(2,1)} %get-tuple-element.160), channel_id=1, source_target_pairs={{0,1},{1,0},{2,3},{3,2},{4,5},{5,4},{6,7},{7,6},{8,9},{9,8},{10,11... | collective-permute-start | bytes 1572872 | tf_op jit(solution)/shard_map/ppermute | solution.py:27
  68.1 19.7 %all-to-all-start.2 = ((bf16[8,128,256]{2,1,0:T(8,128)(2,1)}), bf16[8,128,256]{2,1,0:T(8,128)(2,1)S(1)}, u32[]{:S(2)}, u32[]{:S(2)}) async-start(bf16[8,128,256]{2,1,0:T(8,128)(2,1)} %get-tuple-element.161), calls=%async_computation.2 | async-start | bytes 1048576 | tf_op jit(solution)/shard_map/all_to_all | solution.py:49
  87.8 17.4 %all-to-all-start = ((bf16[8,128,256]{2,1,0:T(8,128)(2,1)}), bf16[8,128,256]{2,1,0:T(8,128)(2,1)S(1)}, u32[]{:S(2)}, u32[]{:S(2)}) async-start(bf16[8,128,256]{2,1,0:T(8,128)(2,1)} %get-tuple-element.156), calls=%async_computation | async-start | bytes 1048576 | tf_op jit(solution)/shard_map/all_to_all | solution.py:49
  91.4 112.3 %all-gather.5.cloned.1.call-start = ((), (), s32[]{:S(2)}) async-start(), calls=%async_computation.20 | async-start | bytes 3342336 | tf_op jit(solution)/shard_map/all_gather | solution.py:1147
  157.5 14.7 %collective-permute-start.8 = (bf16[256,1024]{1,0:T(8,128)(2,1)}, bf16[256,1024]{1,0:T(8,128)(2,1)S(1)}, u32[]{:S(2)}, u32[]{:S(2)}) collective-permute-start(bf16[256,1024]{1,0:T(8,128)(2,1)} %get-tuple-element.165.own_ref), channel_id=1, source_target_pairs={{0,1},{1,0},{2,3},{3,2},{4,5},{5,4},{6,7},{7,6},{8,9},{9,8},{10,11... | collective-permute-start | bytes 1572872 | tf_op jit(solution)/shard_map/ppermute | solution.py:27
  168.4 14.1 %collective-permute-start.10 = (bf16[256,1024]{1,0:T(8,128)(2,1)}, bf16[256,1024]{1,0:T(8,128)(2,1)}, u32[]{:S(2)}, u32[]{:S(2)}) collective-permute-start(bf16[256,1024]{1,0:T(8,128)(2,1)} %get-tuple-element.175.own_ref), channel_id=1, source_target_pairs={{0,1},{1,0},{2,3},{3,2},{4,5},{5,4},{6,7},{7,6},{8,9},{9,8},{10,11... | collective-permute-start | bytes 1572872 | tf_op jit(solution)/shard_map/ppermute | solution.py:27
  208.5 21.4 %all-to-all-start.6 = ((bf16[8,128,256]{2,1,0:T(8,128)(2,1)}), bf16[8,128,256]{2,1,0:T(8,128)(2,1)S(1)}, u32[]{:S(2)}, u32[]{:S(2)}) async-start(bf16[8,128,256]{2,1,0:T(8,128)(2,1)} %get-tuple-element.180), calls=%async_computation.6 | async-start | bytes 1048576 | tf_op jit(solution)/shard_map/all_to_all | solution.py:49
  229.9 16.8 %all-to-all-start.5 = ((bf16[8,128,256]{2,1,0:T(8,128)(2,1)}), bf16[8,128,256]{2,1,0:T(8,128)(2,1)S(1)}, u32[]{:S(2)}, u32[]{:S(2)}) async-start(bf16[8,128,256]{2,1,0:T(8,128)(2,1)} %get-tuple-element.178), calls=%async_computation.5 | async-start | bytes 1048576 | tf_op jit(solution)/shard_map/all_to_all | solution.py:49
  295.2 15.1 %collective-permute-start.15 = (bf16[256,1024]{1,0:T(8,128)(2,1)}, bf16[256,1024]{1,0:T(8,128)(2,1)}, u32[]{:S(2)}, u32[]{:S(2)}) collective-permute-start(bf16[256,1024]{1,0:T(8,128)(2,1)} %get-tuple-element.184.own_ref), channel_id=1, source_target_pairs={{0,1},{1,0},{2,3},{3,2},{4,5},{5,4},{6,7},{7,6},{8,9},{9,8},{10,11... | collective-permute-start | bytes 1572872 | tf_op jit(solution)/shard_map/ppermute | solution.py:27
  304.9 22.8 %collective-permute-start.16 = (bf16[256,1024]{1,0:T(8,128)(2,1)}, bf16[256,1024]{1,0:T(8,128)(2,1)S(1)}, u32[]{:S(2)}, u32[]{:S(2)}) collective-permute-start(bf16[256,1024]{1,0:T(8,128)(2,1)} %get-tuple-element.190.own_ref), channel_id=1, source_target_pairs={{0,1},{1,0},{2,3},{3,2},{4,5},{5,4},{6,7},{7,6},{8,9},{9,8},{10,11... | collective-permute-start | bytes 1572872 | tf_op jit(solution)/shard_map/ppermute | solution.py:27
  327.6 20.2 %collective-permute-start.18 = (bf16[256,1024]{1,0:T(8,128)(2,1)}, bf16[256,1024]{1,0:T(8,128)(2,1)}, u32[]{:S(2)}, u32[]{:S(2)}) collective-permute-start(bf16[256,1024]{1,0:T(8,128)(2,1)} %get-tuple-element.202.own_ref), channel_id=1, source_target_pairs={{0,1},{1,0},{2,3},{3,2},{4,5},{5,4},{6,7},{7,6},{8,9},{9,8},{10,11... | collective-permute-start | bytes 1572872 | tf_op jit(solution)/shard_map/ppermute | solution.py:27
  345.7 23.7 %collective-permute-start.20 = (bf16[256,1024]{1,0:T(8,128)(2,1)}, bf16[256,1024]{1,0:T(8,128)(2,1)S(1)}, u32[]{:S(2)}, u32[]{:S(2)}) collective-permute-start(bf16[256,1024]{1,0:T(8,128)(2,1)} %get-tuple-element.205.own_ref), channel_id=1, source_target_pairs={{0,1},{1,0},{2,3},{3,2},{4,5},{5,4},{6,7},{7,6},{8,9},{9,8},{10,11... | collective-permute-start | bytes 1572872 | tf_op jit(solution)/shard_map/ppermute | solution.py:27
  352.1 17.3 %all-to-all-start.9 = ((bf16[8,128,128]{2,1,0:T(8,128)(2,1)}), bf16[8,128,128]{2,1,0:T(8,128)(2,1)S(1)}, u32[]{:S(2)}, u32[]{:S(2)}) async-start(bf16[8,128,128]{2,1,0:T(8,128)(2,1)} %get-tuple-element.203), calls=%async_computation.9 | async-start | bytes 524288 | tf_op jit(solution)/shard_map/all_to_all | solution.py:49
  374.9 14.4 %all-to-all-start.10 = ((bf16[8,128,128]{2,1,0:T(8,128)(2,1)}), bf16[8,128,128]{2,1,0:T(8,128)(2,1)S(1)}, u32[]{:S(2)}, u32[]{:S(2)}) async-start(bf16[8,128,128]{2,1,0:T(8,128)(2,1)} %get-tuple-element.213), calls=%async_computation.10 | async-start | bytes 524288 | tf_op jit(solution)/shard_map/all_to_all | solution.py:49
  381.0 186.8 %reduce-scatter.3.cloned.1.call-start = ((), (), s32[]{:S(2)}) async-start(), calls=%async_computation.21 | async-start | bytes 10027008 | tf_op jit(solution)/shard_map/reduce_scatter | solution.py:1062
  447.3 18.3 %all-to-all-start.13 = ((bf16[8,128,256]{2,1,0:T(8,128)(2,1)}), bf16[8,128,256]{2,1,0:T(8,128)(2,1)S(1)}, u32[]{:S(2)}, u32[]{:S(2)}) async-start(bf16[8,128,256]{2,1,0:T(8,128)(2,1)} %get-tuple-element.233), calls=%async_computation.13 | async-start | bytes 1048576 | tf_op jit(solution)/shard_map/all_to_all | solution.py:49
  450.9 19.1 %collective-permute-start.23 = (bf16[256,1024]{1,0:T(8,128)(2,1)}, bf16[256,1024]{1,0:T(8,128)(2,1)}, u32[]{:S(2)}, u32[]{:S(2)}) collective-permute-start(bf16[256,1024]{1,0:T(8,128)(2,1)} %get-tuple-element.228.refs_1_), channel_id=1, source_target_pairs={{0,1},{1,0},{2,3},{3,2},{4,5},{5,4},{6,7},{7,6},{8,9},{9,8},{10,11... | collective-permute-start | bytes 1572872 | tf_op jit(solution)/shard_map/ppermute | solution.py:27
  494.1 23.7 %collective-permute-start.27 = (bf16[256,1024]{1,0:T(8,128)(2,1)}, bf16[256,1024]{1,0:T(8,128)(2,1)S(1)}, u32[]{:S(2)}, u32[]{:S(2)}) collective-permute-start(bf16[256,1024]{1,0:T(8,128)(2,1)} %get-tuple-element.239.own_ref), channel_id=1, source_target_pairs={{0,1},{1,0},{2,3},{3,2},{4,5},{5,4},{6,7},{7,6},{8,9},{9,8},{10,11... | collective-permute-start | bytes 1572872 | tf_op jit(solution)/shard_map/ppermute | solution.py:27
  498.7 21.8 %all-to-all-start.12 = ((bf16[8,128,128]{2,1,0:T(8,128)(2,1)}), bf16[8,128,128]{2,1,0:T(8,128)(2,1)S(1)}, u32[]{:S(2)}, u32[]{:S(2)}) async-start(bf16[8,128,128]{2,1,0:T(8,128)(2,1)} %get-tuple-element.232), calls=%async_computation.12 | async-start | bytes 524288 | tf_op jit(solution)/shard_map/all_to_all | solution.py:49
  503.7 213.3 %reduce-scatter.5.cloned.1.call-start = ((), (), s32[]{:S(2)}) async-start(), calls=%async_computation.22 | async-start | bytes 12255232 | tf_op jit(solution)/shard_map/reduce_scatter | solution.py:1062
  592.5 27.9 %all-to-all-start.15 = ((bf16[8,128,256]{2,1,0:T(8,128)(2,1)}), bf16[8,128,256]{2,1,0:T(8,128)(2,1)S(1)}, u32[]{:S(2)}, u32[]{:S(2)}) async-start(bf16[8,128,256]{2,1,0:T(8,128)(2,1)} %get-tuple-element.266), calls=%async_computation.16 | async-start | bytes 1048576 | tf_op jit(solution)/shard_map/all_to_all | solution.py:49
  630.2 15.1 %collective-permute-start.33 = (bf16[256,1024]{1,0:T(8,128)(2,1)}, bf16[256,1024]{1,0:T(8,128)(2,1)}, u32[]{:S(2)}, u32[]{:S(2)}) collective-permute-start(bf16[256,1024]{1,0:T(8,128)(2,1)} %get-tuple-element.277.own_ref), channel_id=1, source_target_pairs={{0,1},{1,0},{2,3},{3,2},{4,5},{5,4},{6,7},{7,6},{8,9},{9,8},{10,11... | collective-permute-start | bytes 1572872 | tf_op jit(solution)/shard_map/ppermute | solution.py:27
  636.3 14.3 %collective-permute-start.32 = (bf16[4,64,1024]{2,1,0:T(8,128)(2,1)}, bf16[4,64,1024]{2,1,0:T(8,128)(2,1)}, u32[]{:S(2)}, u32[]{:S(2)}) collective-permute-start(bf16[4,64,1024]{2,1,0:T(8,128)(2,1)} %dynamic-slice_bitcast_fusion.1), channel_id=1, source_target_pairs={{0,4},{2,6},{4,0},{6,2},{8,12},{10,14},{12,8},{14,10},{16,20},{18,... | collective-permute-start | bytes 1572872 | tf_op jit(solution)/shard_map/ppermute | solution.py:27
  637.8 18.3 %collective-permute-start.30 = (bf16[256,1024]{1,0:T(8,128)(2,1)}, bf16[256,1024]{1,0:T(8,128)(2,1)}, u32[]{:S(2)}, u32[]{:S(2)}) collective-permute-start(bf16[256,1024]{1,0:T(8,128)(2,1)} %get-tuple-element.269.own_ref), channel_id=1, source_target_pairs={{0,1},{1,0},{2,3},{3,2},{4,5},{5,4},{6,7},{7,6},{8,9},{9,8},{10,11... | collective-permute-start | bytes 1572872 | tf_op jit(solution)/shard_map/ppermute | solution.py:27
  664.9 21.2 %collective-permute-start.17 = (bf16[512,512]{1,0:T(8,128)(2,1)}, bf16[512,512]{1,0:T(8,128)(2,1)}, u32[]{:S(2)}, u32[]{:S(2)}) collective-permute-start(bf16[512,512]{1,0:T(8,128)(2,1)} %pad_maximum_fusion.2), channel_id=1, source_target_pairs={{0,1},{1,0},{2,3},{3,2},{4,5},{5,4},{6,7},{7,6},{8,9},{9,8},{10,11... | collective-permute-start | bytes 1572872 | tf_op jit(solution)/shard_map/ppermute | solution.py:27
  681.4 24.1 %collective-permute-start.39 = (bf16[2,64,1024]{2,1,0:T(8,128)(2,1)S(1)}, bf16[2,64,1024]{2,1,0:T(8,128)(2,1)}, u32[]{:S(2)}, u32[]{:S(2)}) collective-permute-start(bf16[2,64,1024]{2,1,0:T(8,128)(2,1)S(1)} %dynamic-slice_bitcast_fusion.2), channel_id=1, source_target_pairs={{0,8},{2,10},{4,12},{6,14},{8,0},{10,2},{12,4},{14,6},{16,24},{18,... | collective-permute-start | bytes 786440 | tf_op jit(solution)/shard_map/ppermute | solution.py:27
  (84 other events, 674.0 us)
Sparse Core Ops, SparseCore 0:
  11.8 48.3 all-gather.2
  135.4 46.6 all-gather.4
  447.4 116.3 reduce-scatter.2
  568.3 145.2 reduce-scatter.4
